TPU v7x, 32 devices: a whole 2x2x4 slice. The times are simulated.
32 devices in a mesh: gx: 2 (over core), gy: 4 (over y, x), gz: 4 (over z).
Axes of the slice: x: 2, y: 2, z: 4, core: 2. Of those that a mesh axis runs over, the one named last changes fastest.
Arguments:
- tokens: bfloat16 [512, 8192], P('gy', ('gz', 'gx')), may hold values from -6 to 6
- gate_weight: bfloat16 [8192, 8192], P('gz', ('gx', 'gy')), may hold values from -0.0625 to 0.0625
- up_weight: bfloat16 [8192, 8192], P('gz', ('gx', 'gy')), may hold values from -0.0625 to 0.0625
- down_weight: bfloat16 [8192, 8192], P('gz', ('gx', 'gy')), may hold values from -0.0625 to 0.0625
- out_grad: bfloat16 [512, 8192], P('gy', ('gz', 'gx')), may hold values from -6 to 6
Outputs:
- output: bfloat16 [512, 8192], P('gy', ('gz', 'gx'))
- tokens_grad: bfloat16 [512, 8192], P('gy', ('gz', 'gx'))
- gate_grad_w: float32 [8192, 8192], P('gz', ('gx', 'gy'))
- up_grad_w: float32 [8192, 8192], P('gz', ('gx', 'gy'))
- down_grad_w: float32 [8192, 8192], P('gz', ('gx', 'gy'))
All inputs are finite; a program needn't handle non-finite values.
Results may differ from a plain program's by a relative error of at most 0.023.
Values may be sent and summed in bfloat16 or wider, within the bound.
No kernel may reach another device: no remote copies, remote signals or barrier semaphores. Data moves between devices by JAX's collectives and lax.ppermute only.
A program may use at most 192 MiB of HBM per device.

v0:
```python
import jax
import jax.numpy as jnp
from jax import lax
from jax.sharding import PartitionSpec as P


def dot_last(left, right):
    return lax.dot_general(
        left, right, (((1,), (1,)), ((), ())), preferred_element_type=jnp.float32
    )


def dot_first(left, right):
    return lax.dot_general(
        left, right, (((0,), (0,)), ((), ())), preferred_element_type=jnp.float32
    )


def add_block(piece, source):
    return dot_first(piece, source)


def per_device(tokens, gate_weight, up_weight, down_weight, out_grad):
    x_local = lax.all_gather(tokens, "gx", axis=1, tiled=True)
    gate_panel, up_panel, down_panel = (
        lax.all_gather(gate_weight, "gy", axis=1, tiled=True),
        lax.all_gather(up_weight, "gy", axis=1, tiled=True),
        lax.all_gather(down_weight, "gy", axis=1, tiled=True),
    )
    width = gate_panel.shape[1]
    row_block = x_local
    gate_part = jnp.dot(row_block, gate_panel, preferred_element_type=jnp.float32)
    up_part = jnp.dot(row_block, up_panel, preferred_element_type=jnp.float32)
    both_values = lax.psum_scatter(
        jnp.concatenate([gate_part, up_part], axis=1).astype(jnp.bfloat16),
        "gz",
        scatter_dimension=0,
        tiled=True,
    ).astype(jnp.float32)
    gate_value = both_values[:, :width]
    up_value = both_values[:, width:]
    activated = jax.nn.silu(gate_value)
    hidden = (activated * up_value).astype(jnp.bfloat16)
    hidden_block = lax.all_gather(hidden, "gz", axis=0, tiled=True)
    out_part = dot_last(hidden_block, down_panel)
    output = lax.psum_scatter(out_part.astype(jnp.bfloat16), "gx", scatter_dimension=1, tiled=True)
    grad_local = lax.all_gather(out_grad, "gx", axis=1, tiled=True)
    row_block = grad_local
    hidden_grad = lax.psum_scatter(
        jnp.dot(row_block, down_panel, preferred_element_type=jnp.float32).astype(jnp.bfloat16),
        "gz",
        scatter_dimension=0,
        tiled=True,
    ).astype(jnp.float32)
    sigmoid_gate = jax.nn.sigmoid(gate_value)
    gate_grad = (
        hidden_grad * up_value * sigmoid_gate * (1.0 + gate_value * (1.0 - sigmoid_gate))
    ).astype(jnp.bfloat16)
    up_grad = (hidden_grad * activated).astype(jnp.bfloat16)
    gate_block, up_block = (
        lax.all_gather(gate_grad, "gz", axis=0, tiled=True),
        lax.all_gather(up_grad, "gz", axis=0, tiled=True),
    )
    in_part = dot_last(gate_block, gate_panel) + dot_last(up_block, up_panel)
    tokens_grad = lax.psum_scatter(
        in_part.astype(jnp.bfloat16), "gx", scatter_dimension=1, tiled=True
    )
    gate_units, up_units, hidden_units = (
        lax.all_to_all(gate_block, "gy", split_axis=1, concat_axis=0, tiled=True),
        lax.all_to_all(up_block, "gy", split_axis=1, concat_axis=0, tiled=True),
        lax.all_to_all(hidden_block, "gy", split_axis=1, concat_axis=0, tiled=True),
    )
    piece = lax.all_gather(x_local, "gy", axis=0, tiled=True)
    gate_grad_w = add_block(piece, gate_units)
    up_grad_w = add_block(piece, up_units)
    down_grad_w = add_block(lax.all_gather(grad_local, "gy", axis=0, tiled=True), hidden_units)
    return (output, tokens_grad, gate_grad_w, up_grad_w, down_grad_w)


def solution(mesh):
    return jax.shard_map(
        per_device,
        mesh=mesh,
        in_specs=(
            P("gy", ("gz", "gx")),
            P("gz", ("gx", "gy")),
            P("gz", ("gx", "gy")),
            P("gz", ("gx", "gy")),
            P("gy", ("gz", "gx")),
        ),
        out_specs=(
            P("gy", ("gz", "gx")),
            P("gy", ("gz", "gx")),
            P("gz", ("gx", "gy")),
            P("gz", ("gx", "gy")),
            P("gz", ("gx", "gy")),
        ),
        check_vma=False,
    )
```

profile of v0, /device:TPU:0, one launch (start us, length us, event | category | flops | bytes accessed | tf_op | source)
XLA Modules:
  0.0 770.5 jit_solution(10968941129574272111)
XLA Ops:
  7.2 0.0 copy-start.3
  7.2 0.0 all-gather.11.cloned.1.call-start
  7.2 0.7 all-gather.11.cloned.1.call-update
  7.9 0.0 all-gather.9.cloned.1.call-start
  8.0 0.7 all-gather.9.cloned.1.call-update
  8.7 0.0 all-gather.15.cloned.1.call-start
  8.7 0.7 all-gather.15.cloned.1.call-update
  9.4 0.0 reduce-scatter.5.cloned.1.call-start
  9.4 0.0 copy-done.3
  9.4 2.3 all_gather.30
  11.7 158.3 %all-gather.11.cloned.1.call-done = bf16[2048,4096]{1,0:T(8,128)(2,1)} async-done(((bf16[2048,1024]{1,0:T(8,128)(2,1)}), bf16[2048,4096]{1,0:T(8,128)(2,1)}) %all-gather.11.cloned.1.call-update) | async-done | bytes 16777232 | tf_op jit(solution)/shard_map/all_gather | solution.py:27
  170.0 8.1 %convolution_convert_fusion.1 = bf16[128,4096]{1,0:T(8,128)(2,1)S(1)} fusion(bf16[128,2048]{1,0:T(8,128)(2,1)S(1)} %all_gather.30, bf16[2048,4096]{1,0:T(8,128)(2,1)} %all-gather.11.cloned.1.call-done), kind=kOutput, calls=%fused_computation.1 | convolution fusion | flops 2148007936 | bytes 18350080 | tf_op jit(solution)/shard_map/dot_general | solution.py:33
  178.1 0.0 copy-start.4
  178.1 151.2 %all-gather.9.cloned.1.call-done = bf16[2048,4096]{1,0:T(8,128)(2,1)} async-done(((bf16[2048,1024]{1,0:T(8,128)(2,1)}), bf16[2048,4096]{1,0:T(8,128)(2,1)}) %all-gather.9.cloned.1.call-update) | async-done | bytes 16777232 | tf_op jit(solution)/shard_map/all_gather | solution.py:26
  329.3 8.1 %convolution_convert_fusion.2 = bf16[128,4096]{1,0:T(8,128)(2,1)S(1)} fusion(bf16[128,2048]{1,0:T(8,128)(2,1)S(1)} %all_gather.30, bf16[2048,4096]{1,0:T(8,128)(2,1)} %all-gather.9.cloned.1.call-done), kind=kOutput, calls=%fused_computation.2 | convolution fusion | flops 2148007936 | bytes 18350080 | tf_op jit(solution)/shard_map/dot_general | solution.py:32
  337.4 1.5 pad_maximum_fusion
  338.9 0.0 reduce-scatter.5.cloned.1.call-update
  338.9 0.0 reduce-scatter.9.cloned.1.call-start
  339.0 2.2 all_gather.35
  341.2 147.4 %all-gather.15.cloned.1.call-done = bf16[2048,4096]{1,0:T(8,128)(2,1)} async-done(((bf16[2048,1024]{1,0:T(8,128)(2,1)}), bf16[2048,4096]{1,0:T(8,128)(2,1)}) %all-gather.15.cloned.1.call-update) | async-done | bytes 16777232 | tf_op jit(solution)/shard_map/all_gather | solution.py:28
  488.6 9.1 %convolution_convert_fusion = bf16[128,4096]{1,0:T(8,128)(2,1)} fusion(bf16[128,2048]{1,0:T(8,128)(2,1)S(1)} %all_gather.35, bf16[2048,4096]{1,0:T(8,128)(2,1)} %all-gather.15.cloned.1.call-done), kind=kOutput, calls=%fused_computation | convolution fusion | flops 2148007936 | bytes 18350080 | tf_op jit(solution)/shard_map/dot_general | solution.py:50
  497.7 0.0 copy-done.1
  497.7 0.0 reduce-scatter.9.cloned.1.call-update
  497.7 0.0 all-gather.17.cloned.1.call-start
  497.8 37.4 %reduce-scatter.5.cloned.1.call-done = bf16[32,8192]{1,0:T(8,128)(2,1)} async-done(((bf16[128,8192]{1,0:T(8,128)(2,1)}), bf16[32,8192]{1,0:T(8,128)(2,1)}) %reduce-scatter.5.cloned.1.call-update) | async-done | bytes 524304 | tf_op jit(solution)/shard_map/reduce_scatter | solution.py:34
  535.2 1.1 convert_element_type.25
  536.3 28.2 %reduce-scatter.9.cloned.1.call-done = bf16[32,4096]{1,0:T(8,128)(2,1)} async-done(((bf16[128,4096]{1,0:T(8,128)(2,1)}), bf16[32,4096]{1,0:T(8,128)(2,1)}) %reduce-scatter.9.cloned.1.call-update) | async-done | bytes 262160 | tf_op jit(solution)/shard_map/reduce_scatter | solution.py:49
  564.6 2.1 fusion.4
  566.6 0.0 all-gather.17.cloned.1.call-update
  566.7 0.0 all-gather.19.cloned.1.call-start
  566.7 0.7 all-gather.19.cloned.1.call-update
  567.4 0.0 all-gather.13.cloned.1.call-start
  567.5 0.7 all-gather.13.cloned.1.call-update
  568.2 0.0 all-gather.21.cloned.1.call-start
  568.2 0.7 all-gather.21.cloned.1.call-update
  568.9 0.0 all-gather.23.cloned.1.call-start
  568.9 0.5 all-gather.23.cloned.1.call-update
  569.5 23.9 %all-gather.17.cloned.1.call-done = bf16[128,4096]{1,0:T(8,128)(2,1)} async-done(((bf16[32,4096]{1,0:T(8,128)(2,1)}), bf16[128,4096]{1,0:T(8,128)(2,1)}) %all-gather.17.cloned.1.call-update) | async-done | bytes 1048592 | tf_op jit(solution)/shard_map/all_gather | solution.py:61
  593.4 2.3 copy.27
  595.7 3.6 all-to-all-start
  599.3 0.1 reduce-scatter.11.cloned.1.call-start
  599.4 12.0 %fusion.6 = f32[128,2048]{1,0:T(8,128)S(1)} fusion(bf16[128,4096]{1,0:T(8,128)(2,1)} %all-gather.17.cloned.1.call-done, bf16[2048,4096]{1,0:T(8,128)(2,1)} %all-gather.9.cloned.1.call-done), kind=kOutput, calls=%fused_computation.22 | convolution fusion | flops 2147483648 | bytes 18874368 | tf_op jit(solution)/shard_map/dot_general | solution.py:8
  611.5 11.5 %all-gather.19.cloned.1.call-done = bf16[128,4096]{1,0:T(8,128)(2,1)} async-done(((bf16[32,4096]{1,0:T(8,128)(2,1)}), bf16[128,4096]{1,0:T(8,128)(2,1)}) %all-gather.19.cloned.1.call-update) | async-done | bytes 1048592 | tf_op jit(solution)/shard_map/all_gather | solution.py:62
  623.0 12.6 %fusion = bf16[128,2048]{1,0:T(8,128)(2,1)} fusion(f32[128,2048]{1,0:T(8,128)S(1)} %fusion.6, bf16[128,4096]{1,0:T(8,128)(2,1)} %all-gather.19.cloned.1.call-done, bf16[2048,4096]{1,0:T(8,128)(2,1)} %all-gather.11.cloned.1.call-done), kind=kOutput, calls=%fused_computation.7 | convolution fusion | flops 2148007936 | bytes 19398656 | tf_op jit(solution)/shard_map/dot_general | solution.py:8
  635.6 0.0 reduce-scatter.11.cloned.1.call-update
  635.7 1.1 copy.26
  636.7 15.3 %all-gather.13.cloned.1.call-done = bf16[128,4096]{1,0:T(8,128)(2,1)} async-done(((bf16[32,4096]{1,0:T(8,128)(2,1)}), bf16[128,4096]{1,0:T(8,128)(2,1)}) %all-gather.13.cloned.1.call-update) | async-done | bytes 1048592 | tf_op jit(solution)/shard_map/all_gather | solution.py:44
  652.0 2.3 copy.25
  654.3 0.0 all-to-all-done
  654.3 3.6 all-to-all-start.1
  658.0 13.1 %convolution_convert_fusion.3 = bf16[128,2048]{1,0:T(8,128)(2,1)} fusion(bf16[128,4096]{1,0:T(8,128)(2,1)} %all-gather.13.cloned.1.call-done, bf16[2048,4096]{1,0:T(8,128)(2,1)} %all-gather.15.cloned.1.call-done), kind=kOutput, calls=%fused_computation.8 | convolution fusion | flops 2147745792 | bytes 18350080 | tf_op jit(solution)/shard_map/dot_general | solution.py:8
  671.1 0.0 reduce-scatter.7.cloned.1.call-update
  671.1 6.1 all-to-all-done.1
  677.2 3.7 all-to-all-start.2
  680.9 24.1 %all-gather.21.cloned.1.call-done = bf16[512,2048]{1,0:T(8,128)(2,1)} async-done(((bf16[128,2048]{1,0:T(8,128)(2,1)}), bf16[512,2048]{1,0:T(8,128)(2,1)}) %all-gather.21.cloned.1.call-update) | async-done | bytes 2097168 | tf_op jit(solution)/shard_map/all_gather | solution.py:73
  705.1 7.4 convolution_bitcast_fusion.2
  712.4 9.4 %copy.16 = f32[2048,1024]{1,0:T(8,128)} copy(f32[2048,1024]{0,1:T(8,128)} %convolution_bitcast_fusion.2) | data formatting | bytes 16777216
  721.8 7.4 convolution_bitcast_fusion.1
  729.2 9.2 %copy.17 = f32[2048,1024]{1,0:T(8,128)} copy(f32[2048,1024]{0,1:T(8,128)} %convolution_bitcast_fusion.1) | data formatting | bytes 16777216
  738.4 2.6 all-gather.23.cloned.1.call-done
  741.0 0.0 all-to-all-done.2
  741.0 7.3 convolution_bitcast_fusion
  748.3 9.3 %copy.18 = f32[2048,1024]{1,0:T(8,128)} copy(f32[2048,1024]{0,1:T(8,128)} %convolution_bitcast_fusion) | data formatting | bytes 16777216
  757.6 6.1 reduce-scatter.7.cloned.1.call-done
  (8 shorter events, 0.0 us)
Async XLA Ops:
  7.2 2.3 copy-start.3
  7.2 162.8 %all-gather.11.cloned.1.call-start = ((), (), s32[]{:S(2)}) async-start(), calls=%async_computation.8 | async-start | bytes 20971520 | tf_op jit(solution)/shard_map/all_gather | solution.py:27
  7.9 321.4 %all-gather.9.cloned.1.call-start = ((), (), s32[]{:S(2)}) async-start(), calls=%async_computation.7 | async-start | bytes 20971520 | tf_op jit(solution)/shard_map/all_gather | solution.py:26
  8.7 480.0 %all-gather.15.cloned.1.call-start = ((), (), s32[]{:S(2)}) async-start(), calls=%async_computation.11 | async-start | bytes 20971520 | tf_op jit(solution)/shard_map/all_gather | solution.py:28
  9.4 525.8 %reduce-scatter.5.cloned.1.call-start = ((), (), s32[]{:S(2)}) async-start(), calls=%async_computation.9 | async-start | bytes 2621440 | tf_op jit(solution)/shard_map/reduce_scatter | solution.py:34
  11.7 317.6 %copy-start = (bf16[128,2048]{1,0:T(8,128)(2,1)}, bf16[128,2048]{1,0:T(8,128)(2,1)S(1)}, u32[]{:S(2)}) copy-start(bf16[128,2048]{1,0:T(8,128)(2,1)S(1)} %all_gather.30) | copy-start | bytes 1572868
  178.1 160.8 %copy-start.4 = (bf16[128,1024]{1,0:T(8,128)(2,1)S(1)}, bf16[128,1024]{1,0:T(8,128)(2,1)}, u32[]{:S(2)}) copy-start(bf16[128,1024]{1,0:T(8,128)(2,1)} %param.9) | copy-start | bytes 786436
  338.9 225.6 %reduce-scatter.9.cloned.1.call-start = ((), (), s32[]{:S(2)}) async-start(), calls=%async_computation.13 | async-start | bytes 1310720 | tf_op jit(solution)/shard_map/reduce_scatter | solution.py:49
  341.2 156.5 %copy-start.1 = (bf16[128,2048]{1,0:T(8,128)(2,1)}, bf16[128,2048]{1,0:T(8,128)(2,1)S(1)}, u32[]{:S(2)}) copy-start(bf16[128,2048]{1,0:T(8,128)(2,1)S(1)} %all_gather.35) | copy-start | bytes 1572868
  497.7 95.7 %all-gather.17.cloned.1.call-start = ((), (), s32[]{:S(2)}) async-start(), calls=%async_computation.14 | async-start | bytes 1310720 | tf_op jit(solution)/shard_map/all_gather | solution.py:61
  566.7 56.3 %all-gather.19.cloned.1.call-start = ((), (), s32[]{:S(2)}) async-start(), calls=%async_computation.15 | async-start | bytes 1310720 | tf_op jit(solution)/shard_map/all_gather | solution.py:62
  567.4 84.6 %all-gather.13.cloned.1.call-start = ((), (), s32[]{:S(2)}) async-start(), calls=%async_computation.10 | async-start | bytes 1310720 | tf_op jit(solution)/shard_map/all_gather | solution.py:44
  568.2 136.9 %all-gather.21.cloned.1.call-start = ((), (), s32[]{:S(2)}) async-start(), calls=%async_computation.17 | async-start | bytes 2621440 | tf_op jit(solution)/shard_map/all_gather | solution.py:73
  568.9 172.1 %all-gather.23.cloned.1.call-start = ((), (), s32[]{:S(2)}) async-start(), calls=%async_computation.18 | async-start | bytes 2621440 | tf_op jit(solution)/shard_map/all_gather | solution.py:76
  595.7 58.6 %all-to-all-start = ((bf16[128,4,1024]{2,0,1:T(8,128)(2,1)}), bf16[128,4,1024]{2,0,1:T(8,128)(2,1)S(1)}, u32[]{:S(2)}, u32[]{:S(2)}) async-start(bf16[128,4,1024]{2,0,1:T(8,128)(2,1)} %bitcast.44), calls=%async_computation.4 | async-start | bytes 2097152 | tf_op jit(solution)/shard_map/all_to_all | solution.py:69
  599.3 158.2 %reduce-scatter.11.cloned.1.call-start = ((), (), s32[]{:S(2)}) async-start(), calls=%async_computation.16 | async-start | bytes 786432 | tf_op jit(solution)/shard_map/reduce_scatter | solution.py:65
  623.0 12.7 %copy-start.2 = (bf16[128,4096]{1,0:T(8,128)(2,1)S(1)}, bf16[128,4096]{1,0:T(8,128)(2,1)}, u32[]{:S(2)}) copy-start(bf16[128,4096]{1,0:T(8,128)(2,1)} %all-gather.19.cloned.1.call-done) | copy-start | bytes 3145732
  654.3 22.9 %all-to-all-start.1 = ((bf16[128,4,1024]{2,0,1:T(8,128)(2,1)}), bf16[128,4,1024]{2,0,1:T(8,128)(2,1)S(1)}, u32[]{:S(2)}, u32[]{:S(2)}) async-start(bf16[128,4,1024]{2,0,1:T(8,128)(2,1)} %bitcast.43), calls=%async_computation.5 | async-start | bytes 2097152 | tf_op jit(solution)/shard_map/all_to_all | solution.py:70
  658.0 105.7 %reduce-scatter.7.cloned.1.call-start = ((), (), s32[]{:S(2)}) async-start(), calls=%async_computation.12 | async-start | bytes 786432 | tf_op jit(solution)/shard_map/reduce_scatter | solution.py:46
  677.2 63.8 %all-to-all-start.2 = ((bf16[128,4,1024]{2,0,1:T(8,128)(2,1)}), bf16[128,4,1024]{2,0,1:T(8,128)(2,1)S(1)}, u32[]{:S(2)}, u32[]{:S(2)}) async-start(bf16[128,4,1024]{2,0,1:T(8,128)(2,1)} %bitcast.42), calls=%async_computation.6 | async-start | bytes 2097152 | tf_op jit(solution)/shard_map/all_to_all | solution.py:71
Sparse Core Ops, SparseCore 0:
  9.9 160.1 all-gather.10
  171.8 157.4 all-gather.8
  331.2 157.4 all-gather.14
  491.3 43.8 reduce-scatter.4
  538.0 26.4 reduce-scatter.8
  566.8 26.5 all-gather.16
  595.5 27.4 all-gather.18
  624.6 27.4 all-gather.12
  654.5 50.5 all-gather.20
  706.8 34.2 all-gather.22
  743.8 7.9 reduce-scatter.10
  754.6 9.0 reduce-scatter.6
where the time goes:
time: 772 us; the launch traced here: 771 us
  waiting for transfers between devices  617 us (80%)
  matrix products  85.1 us (11%)
  local copies, waits for them, and re-layouts  33.6 us (4%)
  between operations  14.3 us (2%)
  starting transfers between devices  11.5 us (1%)
    all_gather x1, waiting for transfers between devices, per_device(): lax.all_gather(up_weight, 'gy', axis=1, tiled=True)  158 us
    all_gather x1, waiting for transfers between devices, per_device(): lax.all_gather(gate_weight, 'gy', axis=1, tiled=True)  151 us
    all_gather x1, waiting for transfers between devices, per_device(): lax.all_gather(down_weight, 'gy', axis=1, tiled=True)  147 us
    dot_general x3, matrix products, dot_last(): lax.dot_general(left, right, (((1,), (1,)), ((), ())), preferred_element_...  37.8 us
    reduce_scatter x1, waiting for transfers between devices, per_device(): lax.psum_scatter(jnp.concatenate([gate_part, up_part], axis=1).astype(jnp...  37.4 us
    reduce_scatter x1, waiting for transfers between devices, per_device(): lax.psum_scatter(jnp.dot(row_block, down_panel, preferred_element_type=jn...  28.2 us
    unnamed x13, local copies, waits for them, and re-layouts  27.9 us
    all_gather x1, waiting for transfers between devices, per_device(): piece = lax.all_gather(x_local, 'gy', axis=0, tiled=True)  24.1 us
  transfers between devices with their start and end apart: 15, of which 12 were waited for; matrix products, arithmetic and copies ran while one was open for 16% of the time, Pallas kernels for 0%

commit v1 on v0

v1 whole, which is shorter than its diff:
```python
import jax
import jax.numpy as jnp
from jax import lax
from jax.sharding import PartitionSpec as P


def dot(left, right):
    return jnp.dot(left, right, preferred_element_type=jnp.float32)


def dot_last(left, right):
    return lax.dot_general(
        left, right, (((1,), (1,)), ((), ())), preferred_element_type=jnp.float32
    )


def dot_first(left, right):
    return lax.dot_general(
        left, right, (((0,), (0,)), ((), ())), preferred_element_type=jnp.float32
    )


def gather_rows(block):
    rows = lax.all_gather(block, "gy", axis=0, tiled=True)
    return lax.all_gather(rows, "gx", axis=1, tiled=True)


def sum_over_units(part):
    part = lax.psum_scatter(part, "gx", scatter_dimension=1, tiled=True)
    return lax.psum_scatter(part, "gy", scatter_dimension=0, tiled=True)


def per_device(tokens, gate_weight, up_weight, down_weight, out_grad):
    bf16 = jnp.bfloat16
    x_all = gather_rows(tokens)
    g_all = gather_rows(out_grad)
    width = gate_weight.shape[1]
    gate_up = jnp.concatenate(
        [dot(x_all, gate_weight).astype(bf16), dot(x_all, up_weight).astype(bf16)], axis=1
    )
    gate_up = lax.psum_scatter(gate_up, "gz", scatter_dimension=0, tiled=True).astype(jnp.float32)
    hidden_grad = lax.psum_scatter(
        dot(g_all, down_weight).astype(bf16), "gz", scatter_dimension=0, tiled=True
    ).astype(jnp.float32)
    gate_value = gate_up[:, :width]
    up_value = gate_up[:, width:]
    sigmoid_gate = jax.nn.sigmoid(gate_value)
    activated = gate_value * sigmoid_gate
    hidden = (activated * up_value).astype(bf16)
    gate_grad = (
        hidden_grad * up_value * sigmoid_gate * (1.0 + gate_value * (1.0 - sigmoid_gate))
    ).astype(bf16)
    up_grad = (hidden_grad * activated).astype(bf16)
    hidden_all = lax.all_gather(hidden, "gz", axis=0, tiled=True)
    output = sum_over_units(dot_last(hidden_all, down_weight).astype(bf16))
    gate_all = lax.all_gather(gate_grad, "gz", axis=0, tiled=True)
    up_all = lax.all_gather(up_grad, "gz", axis=0, tiled=True)
    tokens_grad = sum_over_units(
        (dot_last(gate_all, gate_weight) + dot_last(up_all, up_weight)).astype(bf16)
    )
    down_grad_w = dot_first(g_all, hidden_all)
    gate_grad_w = dot_first(x_all, gate_all)
    up_grad_w = dot_first(x_all, up_all)
    return (output, tokens_grad, gate_grad_w, up_grad_w, down_grad_w)


def solution(mesh):
    return jax.shard_map(
        per_device,
        mesh=mesh,
        in_specs=(
            P("gy", ("gz", "gx")),
            P("gz", ("gx", "gy")),
            P("gz", ("gx", "gy")),
            P("gz", ("gx", "gy")),
            P("gy", ("gz", "gx")),
        ),
        out_specs=(
            P("gy", ("gz", "gx")),
            P("gy", ("gz", "gx")),
            P("gz", ("gx", "gy")),
            P("gz", ("gx", "gy")),
            P("gz", ("gx", "gy")),
        ),
        check_vma=False,
    )
```

time: 772 us -> 355 us (0.46)
  waiting for transfers between devices: 617 us -> 253 us
  matrix products: 85.1 us -> 53.2 us
  starting transfers between devices: 11.5 us -> 0.69 us
    all_gather x8 -> x7, waiting for transfers between devices: 534 us -> 146 us  [the longest x2 58.9 us: gather_rows(): rows = lax.all_gather(block, 'gy', axis=0, tiled=True)]
    reduce_scatter x4 -> x6, waiting for transfers between devices: 71.8 us -> 105 us  [the longest x1 41.6 us: per_device(): lax.psum_scatter(gate_up, 'gz', scatter_dimension=0, tiled=True)]
    dot_general x3, matrix products: 37.8 us -> 20.6 us  [dot_last(): lax.dot_general(left, right, (((1,), (1,)), ((), ())), preferred_element_...]
    dot_general x3, matrix products: 25.3 us -> 13.8 us  [dot(): return jnp.dot(left, right, preferred_element_type=jnp.float32)]
    all_to_all x3 -> x0, starting transfers between devices: 11 us -> none  [the longest x1 3.74 us: per_device(): lax.all_to_all(hidden_block, 'gy', split_axis=1, concat_axis=0, tiled=True)]
  transfers between devices with their start and end apart: 15 -> 13, of which waited for: 12 -> 12; matrix products, arithmetic and copies ran while one was open for 16% -> 24% of each run, Pallas kernels for 0% -> 0%
where the time goes in v1:
time: 355 us; the launch traced here: 354 us
  waiting for transfers between devices  253 us (71%)
  matrix products  53.2 us (15%)
  local copies, waits for them, and re-layouts  28 us (8%)
  between operations  14 us (4%)
  other arithmetic  4.77 us (1%)
    all_gather x2, waiting for transfers between devices, gather_rows(): rows = lax.all_gather(block, 'gy', axis=0, tiled=True)  58.9 us
    reduce_scatter x1, waiting for transfers between devices, per_device(): lax.psum_scatter(gate_up, 'gz', scatter_dimension=0, tiled=True)  41.6 us
    reduce_scatter x1, waiting for transfers between devices, per_device(): lax.psum_scatter(dot(g_all, down_weight).astype(bf16), 'gz', scatter_dime...  28.2 us
    unnamed x13, local copies, waits for them, and re-layouts  28 us
    all_gather x1, waiting for transfers between devices, per_device(): hidden_all = lax.all_gather(hidden, 'gz', axis=0, tiled=True)  25.2 us
    all_gather x1, waiting for transfers between devices, per_device(): gate_all = lax.all_gather(gate_grad, 'gz', axis=0, tiled=True)  23.1 us
    all_gather x1, waiting for transfers between devices, per_device(): up_all = lax.all_gather(up_grad, 'gz', axis=0, tiled=True)  22.7 us
    dot_general x3, matrix products, dot_last(): lax.dot_general(left, right, (((1,), (1,)), ((), ())), preferred_element_...  20.6 us
  transfers between devices with their start and end apart: 13, of which 12 were waited for; matrix products, arithmetic and copies ran while one was open for 24% of the time, Pallas kernels for 0%

profile of v1, /device:TPU:0, one launch (start us, length us, event | category | flops | bytes accessed | tf_op | source)
XLA Modules:
  0.0 354.0 jit_solution(4037873213729863588)
XLA Ops:
  7.2 0.0 all-gather.8.cloned.1.call-start
  7.2 0.7 all-gather.8.cloned.1.call-update
  7.9 0.0 all-gather.14.cloned.1.call-start
  7.9 0.7 all-gather.14.cloned.1.call-update
  8.6 0.0 all-gather.10.cloned.1.call-start
  8.7 30.5 %all-gather.8.cloned.1.call-done = bf16[512,1024]{1,0:T(8,128)(2,1)} async-done(((bf16[128,1024]{1,0:T(8,128)(2,1)}), bf16[512,1024]{1,0:T(8,128)(2,1)}) %all-gather.8.cloned.1.call-update) | async-done | bytes 1048592 | tf_op jit(solution)/shard_map/all_gather | solution.py:24
  39.2 0.0 all-gather.10.cloned.1.call-update
  39.2 0.0 all-gather.16.cloned.1.call-start
  39.3 28.4 %all-gather.14.cloned.1.call-done = bf16[512,1024]{1,0:T(8,128)(2,1)} async-done(((bf16[128,1024]{1,0:T(8,128)(2,1)}), bf16[512,1024]{1,0:T(8,128)(2,1)}) %all-gather.14.cloned.1.call-update) | async-done | bytes 1048592 | tf_op jit(solution)/shard_map/all_gather | solution.py:24
  67.7 0.0 all-gather.16.cloned.1.call-update
  67.7 0.0 reduce-scatter.7.cloned.1.call-start
  67.8 12.1 %all-gather.10.cloned.1.call-done = bf16[512,2048]{1,0:T(8,128)(2,1)} async-done(((bf16[512,1024]{1,0:T(8,128)(2,1)}), bf16[512,2048]{1,0:T(8,128)(2,1)}) %all-gather.10.cloned.1.call-update) | async-done | bytes 2097168 | tf_op jit(solution)/shard_map/all_gather | solution.py:25
  79.9 0.0 copy-start
  79.9 0.0 copy-start.1
  79.9 5.3 %convolution_convert_fusion.2 = bf16[512,1024]{1,0:T(8,128)(2,1)S(1)} fusion(bf16[512,2048]{1,0:T(8,128)(2,1)} %all-gather.10.cloned.1.call-done, bf16[2048,1024]{1,0:T(8,128)(2,1)} %param.7), kind=kOutput, calls=%fused_computation.7 | convolution fusion | flops 2148007936 | bytes 7340032 | tf_op jit(solution)/shard_map/dot_general | solution.py:8
  85.2 0.0 copy-done
  85.2 0.0 copy-done.1
  85.2 2.4 convolution_convert_fusion.3
  87.6 1.5 pad_maximum_fusion
  89.1 0.0 reduce-scatter.7.cloned.1.call-update
  89.1 0.0 reduce-scatter.13.cloned.1.call-start
  89.2 3.9 %all-gather.16.cloned.1.call-done = bf16[512,2048]{1,0:T(8,128)(2,1)} async-done(((bf16[512,1024]{1,0:T(8,128)(2,1)}), bf16[512,2048]{1,0:T(8,128)(2,1)}) %all-gather.16.cloned.1.call-update) | async-done | bytes 2097168 | tf_op jit(solution)/shard_map/all_gather | solution.py:25
  93.0 6.1 %convolution_convert_fusion.1 = bf16[512,1024]{1,0:T(8,128)(2,1)} fusion(bf16[512,2048]{1,0:T(8,128)(2,1)} %all-gather.16.cloned.1.call-done, bf16[2048,1024]{1,0:T(8,128)(2,1)} %param.8), kind=kOutput, calls=%fused_computation.6 | convolution fusion | flops 2148007936 | bytes 7340032 | tf_op jit(solution)/shard_map/dot_general | solution.py:8
  99.2 0.0 reduce-scatter.13.cloned.1.call-update
  99.2 0.0 all-gather.12.cloned.1.call-start
  99.2 41.6 %reduce-scatter.7.cloned.1.call-done = bf16[128,2048]{1,0:T(8,128)(2,1)} async-done(((bf16[512,2048]{1,0:T(8,128)(2,1)}), bf16[128,2048]{1,0:T(8,128)(2,1)}) %reduce-scatter.7.cloned.1.call-update) | async-done | bytes 524304 | tf_op jit(solution)/shard_map/reduce_scatter | solution.py:41
  140.8 1.1 convert_element_type.32
  142.0 28.2 %reduce-scatter.13.cloned.1.call-done = bf16[128,1024]{1,0:T(8,128)(2,1)} async-done(((bf16[512,1024]{1,0:T(8,128)(2,1)}), bf16[128,1024]{1,0:T(8,128)(2,1)}) %reduce-scatter.13.cloned.1.call-update) | async-done | bytes 262160 | tf_op jit(solution)/shard_map/reduce_scatter | solution.py:42
  170.1 2.1 fusion.3
  172.3 0.0 all-gather.12.cloned.1.call-update
  172.3 0.0 all-gather.18.cloned.1.call-start
  172.3 0.7 all-gather.18.cloned.1.call-update
  173.1 0.0 all-gather.20.cloned.1.call-start
  173.1 0.7 all-gather.20.cloned.1.call-update
  173.8 0.0 reduce-scatter.9.cloned.1.call-start
  173.8 25.2 %all-gather.12.cloned.1.call-done = bf16[512,1024]{1,0:T(8,128)(2,1)} async-done(((bf16[128,1024]{1,0:T(8,128)(2,1)}), bf16[512,1024]{1,0:T(8,128)(2,1)}) %all-gather.12.cloned.1.call-update) | async-done | bytes 1048592 | tf_op jit(solution)/shard_map/all_gather | solution.py:54
  199.0 6.2 %convolution_convert_fusion = bf16[512,2048]{1,0:T(8,128)(2,1)} fusion(bf16[512,1024]{1,0:T(8,128)(2,1)} %all-gather.12.cloned.1.call-done, bf16[2048,1024]{1,0:T(8,128)(2,1)} %param.8), kind=kOutput, calls=%fused_computation.4 | convolution fusion | flops 2148532224 | bytes 7340032 | tf_op jit(solution)/shard_map/dot_general | solution.py:12
  205.2 0.0 reduce-scatter.9.cloned.1.call-update
  205.3 0.2 reduce-scatter.15.cloned.1.call-start
  205.5 23.1 %all-gather.18.cloned.1.call-done = bf16[512,1024]{1,0:T(8,128)(2,1)} async-done(((bf16[128,1024]{1,0:T(8,128)(2,1)}), bf16[512,1024]{1,0:T(8,128)(2,1)}) %all-gather.18.cloned.1.call-update) | async-done | bytes 1048592 | tf_op jit(solution)/shard_map/all_gather | solution.py:56
  228.6 6.9 %fusion.5 = f32[512,2048]{1,0:T(8,128)} fusion(bf16[512,1024]{1,0:T(8,128)(2,1)} %all-gather.18.cloned.1.call-done, bf16[2048,1024]{1,0:T(8,128)(2,1)} %param.6), kind=kOutput, calls=%fused_computation.18 | convolution fusion | flops 2147483648 | bytes 9437184 | tf_op jit(solution)/shard_map/dot_general | solution.py:12
  235.5 22.7 %all-gather.20.cloned.1.call-done = bf16[512,1024]{1,0:T(8,128)(2,1)} async-done(((bf16[128,1024]{1,0:T(8,128)(2,1)}), bf16[512,1024]{1,0:T(8,128)(2,1)}) %all-gather.20.cloned.1.call-update) | async-done | bytes 1048592 | tf_op jit(solution)/shard_map/all_gather | solution.py:57
  258.2 7.5 %add_convert_fusion = bf16[512,2048]{1,0:T(8,128)(2,1)} fusion(f32[512,2048]{1,0:T(8,128)} %fusion.5, bf16[512,1024]{1,0:T(8,128)(2,1)} %all-gather.20.cloned.1.call-done, bf16[2048,1024]{1,0:T(8,128)(2,1)} %param.7), kind=kOutput, calls=%fused_computation.3 | convolution fusion | flops 2149580800 | bytes 11534336 | tf_op jit(solution)/shard_map/dot_general | solution.py:12
  265.7 0.0 copy-start.2
  265.7 0.0 reduce-scatter.15.cloned.1.call-update
  265.7 0.0 reduce-scatter.11.cloned.1.call-start
  265.8 4.3 %reduce-scatter.9.cloned.1.call-done = bf16[512,1024]{1,0:T(8,128)(2,1)} async-done(((bf16[512,2048]{1,0:T(8,128)(2,1)}), bf16[512,1024]{1,0:T(8,128)(2,1)}) %reduce-scatter.9.cloned.1.call-update) | async-done | bytes 1048592 | tf_op jit(solution)/shard_map/reduce_scatter | solution.py:29
  270.1 0.0 reduce-scatter.11.cloned.1.call-update
  270.1 0.0 reduce-scatter.17.cloned.1.call-start
  270.1 13.6 %reduce-scatter.15.cloned.1.call-done = bf16[512,1024]{1,0:T(8,128)(2,1)} async-done(((bf16[512,2048]{1,0:T(8,128)(2,1)}), bf16[512,1024]{1,0:T(8,128)(2,1)}) %reduce-scatter.15.cloned.1.call-update) | async-done | bytes 1048592 | tf_op jit(solution)/shard_map/reduce_scatter | solution.py:29
  283.8 0.0 reduce-scatter.17.cloned.1.call-update
  283.8 0.0 copy-done.2
  283.8 7.4 %convolution_bitcast_fusion = f32[2048,1024]{0,1:T(8,128)} fusion(bf16[512,1024]{1,0:T(8,128)(2,1)S(1)} %copy-done.2, bf16[512,2048]{1,0:T(8,128)(2,1)} %all-gather.16.cloned.1.call-done), kind=kOutput, calls=%fused_computation | convolution fusion | flops 2147483648 | bytes 11534336 | tf_op jit(solution)/shard_map/dot_general | solution.py:18
  291.2 0.0 copy-start.4
  291.2 9.4 %copy.12 = f32[2048,1024]{1,0:T(8,128)} copy(f32[2048,1024]{0,1:T(8,128)} %convolution_bitcast_fusion) | data formatting | bytes 16777216
  300.5 0.0 copy-done.4
  300.5 5.8 %convolution_bitcast_fusion.1 = f32[2048,1024]{0,1:T(8,128)} fusion(bf16[512,1024]{1,0:T(8,128)(2,1)S(1)} %copy-done.4, bf16[512,2048]{1,0:T(8,128)(2,1)S(1)} %copy-done.1), kind=kOutput, calls=%fused_computation.1 | convolution fusion | flops 2147483648 | bytes 11534336 | tf_op jit(solution)/shard_map/dot_general | solution.py:18
  306.3 0.0 copy-start.3
  306.3 9.4 %copy.11 = f32[2048,1024]{1,0:T(8,128)} copy(f32[2048,1024]{0,1:T(8,128)} %convolution_bitcast_fusion.1) | data formatting | bytes 16777216
  315.7 0.0 copy-done.3
  315.7 5.7 %convolution_bitcast_fusion.2 = f32[2048,1024]{0,1:T(8,128)} fusion(bf16[512,1024]{1,0:T(8,128)(2,1)S(1)} %copy-done.3, bf16[512,2048]{1,0:T(8,128)(2,1)S(1)} %copy-done.1), kind=kOutput, calls=%fused_computation.2 | convolution fusion | flops 2147483648 | bytes 11534336 | tf_op jit(solution)/shard_map/dot_general | solution.py:18
  321.3 9.2 %copy.10 = f32[2048,1024]{1,0:T(8,128)} copy(f32[2048,1024]{0,1:T(8,128)} %convolution_bitcast_fusion.2) | data formatting | bytes 16777216
  330.6 0.0 reduce-scatter.11.cloned.1.call-done
  330.6 16.9 %reduce-scatter.17.cloned.1.call-done = bf16[128,1024]{1,0:T(8,128)(2,1)} async-done(((bf16[512,1024]{1,0:T(8,128)(2,1)}), bf16[128,1024]{1,0:T(8,128)(2,1)}) %reduce-scatter.17.cloned.1.call-update) | async-done | bytes 262160 | tf_op jit(solution)/shard_map/reduce_scatter | solution.py:30
Async XLA Ops:
  7.2 32.0 %all-gather.8.cloned.1.call-start = ((), (), s32[]{:S(2)}) async-start(), calls=%async_computation.6 | async-start | bytes 1310720 | tf_op jit(solution)/shard_map/all_gather | solution.py:24
  7.9 59.8 %all-gather.14.cloned.1.call-start = ((), (), s32[]{:S(2)}) async-start(), calls=%async_computation.12 | async-start | bytes 1310720 | tf_op jit(solution)/shard_map/all_gather | solution.py:24
  8.6 71.2 %all-gather.10.cloned.1.call-start = ((), (), s32[]{:S(2)}) async-start(), calls=%async_computation.7 | async-start | bytes 3145728 | tf_op jit(solution)/shard_map/all_gather | solution.py:25
  39.2 53.8 %all-gather.16.cloned.1.call-start = ((), (), s32[]{:S(2)}) async-start(), calls=%async_computation.13 | async-start | bytes 3145728 | tf_op jit(solution)/shard_map/all_gather | solution.py:25
  67.7 73.1 %reduce-scatter.7.cloned.1.call-start = ((), (), s32[]{:S(2)}) async-start(), calls=%async_computation.8 | async-start | bytes 2621440 | tf_op jit(solution)/shard_map/reduce_scatter | solution.py:41
  79.9 5.3 %copy-start = (bf16[2048,1024]{1,0:T(8,128)(2,1)S(1)}, bf16[2048,1024]{1,0:T(8,128)(2,1)}, u32[]{:S(2)}) copy-start(bf16[2048,1024]{1,0:T(8,128)(2,1)} %param.6) | copy-start | bytes 12582916
  79.9 5.3 %copy-start.1 = (bf16[512,2048]{1,0:T(8,128)(2,1)S(1)}, bf16[512,2048]{1,0:T(8,128)(2,1)}, u32[]{:S(2)}) copy-start(bf16[512,2048]{1,0:T(8,128)(2,1)} %all-gather.10.cloned.1.call-done) | copy-start | bytes 6291460
  89.1 81.0 %reduce-scatter.13.cloned.1.call-start = ((), (), s32[]{:S(2)}) async-start(), calls=%async_computation.14 | async-start | bytes 1310720 | tf_op jit(solution)/shard_map/reduce_scatter | solution.py:42
  99.2 99.8 %all-gather.12.cloned.1.call-start = ((), (), s32[]{:S(2)}) async-start(), calls=%async_computation.9 | async-start | bytes 1310720 | tf_op jit(solution)/shard_map/all_gather | solution.py:54
  172.3 56.3 %all-gather.18.cloned.1.call-start = ((), (), s32[]{:S(2)}) async-start(), calls=%async_computation.15 | async-start | bytes 1310720 | tf_op jit(solution)/shard_map/all_gather | solution.py:56
  173.1 85.2 %all-gather.20.cloned.1.call-start = ((), (), s32[]{:S(2)}) async-start(), calls=%async_computation.16 | async-start | bytes 1310720 | tf_op jit(solution)/shard_map/all_gather | solution.py:57
  173.8 96.3 %reduce-scatter.9.cloned.1.call-start = ((), (), s32[]{:S(2)}) async-start(), calls=%async_computation.10 | async-start | bytes 3145728 | tf_op jit(solution)/shard_map/reduce_scatter | solution.py:29
  205.3 78.5 %reduce-scatter.15.cloned.1.call-start = ((), (), s32[]{:S(2)}) async-start(), calls=%async_computation.17 | async-start | bytes 3145728 | tf_op jit(solution)/shard_map/reduce_scatter | solution.py:29
  265.7 18.1 %copy-start.2 = (bf16[512,1024]{1,0:T(8,128)(2,1)S(1)}, bf16[512,1024]{1,0:T(8,128)(2,1)}, u32[]{:S(2)}) copy-start(bf16[512,1024]{1,0:T(8,128)(2,1)} %all-gather.12.cloned.1.call-done) | copy-start | bytes 3145732
  265.7 64.8 %reduce-scatter.11.cloned.1.call-start = ((), (), s32[]{:S(2)}) async-start(), calls=%async_computation.11 | async-start | bytes 1310720 | tf_op jit(solution)/shard_map/reduce_scatter | solution.py:30
  270.1 77.4 %reduce-scatter.17.cloned.1.call-start = ((), (), s32[]{:S(2)}) async-start(), calls=%async_computation.18 | async-start | bytes 1310720 | tf_op jit(solution)/shard_map/reduce_scatter | solution.py:30
  291.2 9.4 %copy-start.4 = (bf16[512,1024]{1,0:T(8,128)(2,1)S(1)}, bf16[512,1024]{1,0:T(8,128)(2,1)}, u32[]{:S(2)}) copy-start(bf16[512,1024]{1,0:T(8,128)(2,1)} %all-gather.20.cloned.1.call-done) | copy-start | bytes 3145732
  306.3 9.4 %copy-start.3 = (bf16[512,1024]{1,0:T(8,128)(2,1)S(1)}, bf16[512,1024]{1,0:T(8,128)(2,1)}, u32[]{:S(2)}) copy-start(bf16[512,1024]{1,0:T(8,128)(2,1)} %all-gather.18.cloned.1.call-done) | copy-start | bytes 3145732
Sparse Core Ops, SparseCore 0:
  9.8 29.3 all-gather.7
  41.0 26.6 all-gather.13
  69.3 10.5 all-gather.9
  81.3 11.7 all-gather.15
  95.8 45.0 reduce-scatter.6
  143.6 26.4 reduce-scatter.12
  172.4 26.5 all-gather.11
  201.2 27.4 all-gather.17
  230.8 27.4 all-gather.19
  260.9 9.1 reduce-scatter.8
  273.0 10.7 reduce-scatter.14
  287.1 28.8 reduce-scatter.10
  319.7 27.7 reduce-scatter.16

commit v2 on v1

v2 whole, which is shorter than its diff:
```python
import functools

import jax
import jax.numpy as jnp
from jax import lax
from jax.experimental import pallas as pl
from jax.experimental.pallas import tpu as pltpu
from jax.sharding import PartitionSpec as P

BF16 = jnp.bfloat16
F32 = jnp.float32
MIB = 1 << 20


def after(value, *earlier):
    return lax.optimization_barrier((value, *earlier))[0]


def swap(value, axis, size, mask):
    return lax.ppermute(value, axis, [(i, i ^ mask) for i in range(size)])


def reversed_bits(index, size):
    bits = size.bit_length() - 1
    out = jnp.zeros((), jnp.int32)
    for bit in range(bits):
        out = out | (((index >> bit) & 1) << (bits - 1 - bit))
    return out


def params(limit=40):
    return pltpu.CompilerParams(vmem_limit_bytes=limit * MIB)


def whole(array):
    zeros = (0,) * array.ndim
    return pl.BlockSpec(array.shape, lambda *_: zeros)


def ordered_rows(tokens, out_grad, flip, pieces):
    rows, width = tokens.shape
    piece = rows // pieces

    def kernel(flip_ref, a_ref, b_ref, o_ref):
        o_ref[0] = a_ref[...]
        o_ref[1] = b_ref[...]

    source = pl.BlockSpec((piece, width), lambda i, flip: (i ^ flip[0], 0))
    return pl.pallas_call(
        kernel,
        grid_spec=pltpu.PrefetchScalarGridSpec(
            num_scalar_prefetch=1,
            grid=(pieces,),
            in_specs=[source, source],
            out_specs=pl.BlockSpec((2, piece, width), lambda i, flip: (0, i, 0)),
        ),
        out_shape=jax.ShapeDtypeStruct((2, rows, width), BF16),
        compiler_params=params(),
        name="ordered_rows",
    )(flip, tokens, out_grad)


def forward_products(core, own, other, gate_weight, up_weight, down_weight):
    _, rows, width = own.shape
    depth, units = gate_weight.shape
    tile = min(256, units)
    half = rows // 2

    def kernel(core_ref, own_ref, other_ref, gate_ref, up_ref, down_ref, keep_ref, send_ref):
        here = pl.ds(pl.multiple_of(core_ref[0] * width, width), width)
        there = pl.ds(pl.multiple_of((1 - core_ref[0]) * width, width), width)
        for index, (which, weight) in enumerate(((0, gate_ref), (0, up_ref), (1, down_ref))):
            part = jnp.dot(own_ref[which], weight[here, :], preferred_element_type=F32)
            part += jnp.dot(other_ref[which], weight[there, :], preferred_element_type=F32)
            part = part.astype(BF16)
            keep_ref[index] = part[:half]
            send_ref[index] = part[half:]

    weight = pl.BlockSpec((depth, tile), lambda j, core: (0, j))
    result = pl.BlockSpec((3, half, tile), lambda j, core: (0, 0, j))
    return pl.pallas_call(
        kernel,
        grid_spec=pltpu.PrefetchScalarGridSpec(
            num_scalar_prefetch=1,
            grid=(units // tile,),
            in_specs=[whole(own), whole(other), weight, weight, weight],
            out_specs=[result, result],
        ),
        out_shape=[jax.ShapeDtypeStruct((3, half, units), BF16)] * 2,
        compiler_params=params(),
        name="forward_products",
    )(core, own, other, gate_weight, up_weight, down_weight)


def add_halves(held, received):
    rows = held.shape[1]
    half = rows // 2

    def kernel(a_ref, b_ref, keep_ref, send_ref):
        for index in range(3):
            total = (a_ref[index].astype(F32) + b_ref[index].astype(F32)).astype(BF16)
            keep_ref[index] = total[:half]
            send_ref[index] = total[half:]

    shape = jax.ShapeDtypeStruct((3, half, held.shape[2]), BF16)
    return pl.pallas_call(
        kernel, out_shape=[shape, shape], compiler_params=params(), name="add_halves"
    )(held, received)


def activations(held, received):
    def kernel(a_ref, b_ref, o_ref):
        gate, up, grad = [a_ref[i].astype(F32) + b_ref[i].astype(F32) for i in range(3)]
        sigmoid = jax.nn.sigmoid(gate)
        active = gate * sigmoid
        o_ref[0] = (active * up).astype(BF16)
        o_ref[1] = (grad * up * sigmoid * (1.0 + gate * (1.0 - sigmoid))).astype(BF16)
        o_ref[2] = (grad * active).astype(BF16)

    return pl.pallas_call(
        kernel,
        out_shape=jax.ShapeDtypeStruct(held.shape, BF16),
        compiler_params=params(),
        name="activations",
    )(held, received)


NT = (((1,), (1,)), ((), ()))
TN = (((0,), (0,)), ((), ()))


def backward_products(core, acts, gate_weight, up_weight, down_weight):
    rows = sum(a.shape[1] for a in acts)
    depth, units = gate_weight.shape
    width = depth // 2
    tile = min(256, width)
    steps = width // tile
    count = len(acts)

    def kernel(core_ref, *refs):
        act_refs = refs[:count]
        gate_ref, up_ref, down_ref, keep_ref, send_ref = refs[count:]
        hidden, gate, up = [
            jnp.concatenate([ref[i] for ref in act_refs], axis=0) for i in range(3)
        ]
        out = lax.dot_general(hidden, down_ref[...], NT, preferred_element_type=F32)
        grad = lax.dot_general(gate, gate_ref[...], NT, preferred_element_type=F32)
        grad += lax.dot_general(up, up_ref[...], NT, preferred_element_type=F32)

        @pl.when(pl.program_id(0) < steps)
        def _():
            send_ref[0] = out.astype(BF16)
            send_ref[1] = grad.astype(BF16)

        @pl.when(pl.program_id(0) >= steps)
        def _():
            keep_ref[0] = out.astype(BF16)
            keep_ref[1] = grad.astype(BF16)

    def place(j, core):
        side = jnp.where(j < steps, 1 - core[0], core[0])
        return (side * steps + j % steps, 0)

    weight = pl.BlockSpec((tile, units), place)
    return pl.pallas_call(
        kernel,
        grid_spec=pltpu.PrefetchScalarGridSpec(
            num_scalar_prefetch=1,
            grid=(2 * steps,),
            in_specs=[whole(a) for a in acts] + [weight, weight, weight],
            out_specs=[
                pl.BlockSpec((2, rows, tile), lambda j, core: (0, 0, jnp.maximum(j - steps, 0))),
                pl.BlockSpec((2, rows, tile), lambda j, core: (0, 0, jnp.minimum(j, steps - 1))),
            ],
        ),
        out_shape=[jax.ShapeDtypeStruct((2, rows, width), BF16)] * 2,
        compiler_params=params(),
        name="backward_products",
    )(core, *acts, gate_weight, up_weight, down_weight)


def weight_grads(core, owns, others, acts):
    count = len(owns)
    _, rows, width = owns[0].shape
    units = acts[0][0].shape[2]
    tile = min(256, width)
    steps = width // tile
    flat = [piece for block in acts for piece in block]
    pieces = len(flat)
    total = rows * count

    def kernel(core_ref, *refs):
        own_refs, other_refs = refs[:count], refs[count : 2 * count]
        act_refs = refs[2 * count : 2 * count + pieces]
        gate_out, up_out, down_out, all_acts, left = refs[2 * count + pieces :]
        step = pl.program_id(0)

        @pl.when(step == 0)
        def _():
            low = 0
            for ref in act_refs:
                all_acts[:, low : low + ref.shape[1]] = ref[...]
                low += ref.shape[1]

        columns = pl.ds(pl.multiple_of((step % steps) * tile, tile), tile)

        @pl.when(step < steps)
        def _():
            for index, ref in enumerate(own_refs):
                left[:, index * rows : (index + 1) * rows] = ref[:, :, columns]

        @pl.when(step >= steps)
        def _():
            for index, ref in enumerate(other_refs):
                left[:, index * rows : (index + 1) * rows] = ref[:, :, columns]

        tokens, grads = left[0], left[1]
        down_out[...] = lax.dot_general(grads, all_acts[0], TN, preferred_element_type=F32)
        gate_out[...] = lax.dot_general(tokens, all_acts[1], TN, preferred_element_type=F32)
        up_out[...] = lax.dot_general(tokens, all_acts[2], TN, preferred_element_type=F32)

    def place(j, core):
        side = jnp.where(j < steps, core[0], 1 - core[0])
        return (side * steps + j % steps, 0)

    return pl.pallas_call(
        kernel,
        grid_spec=pltpu.PrefetchScalarGridSpec(
            num_scalar_prefetch=1,
            grid=(2 * steps,),
            in_specs=[whole(a) for a in (*owns, *others, *flat)],
            out_specs=[pl.BlockSpec((tile, units), place)] * 3,
            scratch_shapes=[
                pltpu.VMEM((3, total, units), BF16),
                pltpu.VMEM((2, total, tile), BF16),
            ],
        ),
        out_shape=[jax.ShapeDtypeStruct((2 * width, units), F32)] * 3,
        compiler_params=params(56),
        name="weight_grads",
    )(core, *owns, *others, *flat)


def add_pair(a, b):
    return (a.astype(F32) + b.astype(F32)).astype(BF16)


def final_sum(parts, flip, pieces):
    _, rows, width = parts[0].shape
    piece = rows // pieces
    count = len(parts)

    def kernel(flip_ref, *refs):
        for index, out_ref in enumerate(refs[count:]):
            total = refs[0][index].astype(F32)
            for ref in refs[1:count]:
                total += ref[index].astype(F32)
            out_ref[...] = total.astype(BF16)

    source = pl.BlockSpec((2, piece, width), lambda i, flip: (0, i, 0))
    target = pl.BlockSpec((piece, width), lambda i, flip: (i ^ flip[0], 0))
    return pl.pallas_call(
        kernel,
        grid_spec=pltpu.PrefetchScalarGridSpec(
            num_scalar_prefetch=1,
            grid=(pieces,),
            in_specs=[source] * count,
            out_specs=[target, target],
        ),
        out_shape=[jax.ShapeDtypeStruct((rows, width), BF16)] * 2,
        compiler_params=params(),
        name="final_sum",
    )(flip, *parts)


def per_device(sizes, tokens, gate_weight, up_weight, down_weight, out_grad):
    n_gy, n_gz = sizes["gy"], sizes["gz"]
    levels = n_gz.bit_length() - 1
    core = lax.axis_index("gx").astype(jnp.int32).reshape(1)
    flip = reversed_bits(lax.axis_index("gz").astype(jnp.int32), n_gz).reshape(1)
    weights = (gate_weight, up_weight, down_weight)
    swap_core = functools.partial(swap, axis="gx", size=2, mask=1)

    mine = ordered_rows(tokens, out_grad, flip, n_gz)
    owns = [mine] + [swap(mine, "gy", n_gy, d) for d in range(1, n_gy)]
    others = [swap_core(own) for own in owns]

    def chunk(d):
        keep, send = forward_products(core, owns[d], others[d], *weights)
        for level in range(levels - 1):
            got = swap(send, "gz", n_gz, 1 << level)
            got = yield got
            keep, send = add_halves(keep, got)
        got = swap(send, "gz", n_gz, 1 << (levels - 1))
        got = yield got
        acts = [activations(keep, got)]
        for level in reversed(range(levels)):
            held = acts[0] if len(acts) == 1 else jnp.concatenate(acts, axis=1)
            got = swap(held, "gz", n_gz, 1 << level)
            got = yield got
            acts.append(got)
        return acts

    acts = [None] * n_gy
    runs = [chunk(d) for d in range(n_gy)]
    waiting = [next(run) for run in runs]
    live = list(range(n_gy))
    while live:
        for d in list(live):
            try:
                waiting[d] = runs[d].send(waiting[d])
            except StopIteration as stop:
                acts[d] = stop.value
                live.remove(d)

    parts = []
    for d in range(n_gy):
        keep, send = backward_products(core, acts[d], *weights)
        part = add_pair(keep, swap_core(send))
        parts.append(swap(part, "gy", n_gy, d) if d else part)
    output, tokens_grad = final_sum(parts, flip, n_gz)
    gate_grad_w, up_grad_w, down_grad_w = weight_grads(core, owns, others, acts)
    return (output, tokens_grad, gate_grad_w, up_grad_w, down_grad_w)


def solution(mesh):
    return jax.shard_map(
        functools.partial(per_device, dict(mesh.shape)),
        mesh=mesh,
        in_specs=(
            P("gy", ("gz", "gx")),
            P("gz", ("gx", "gy")),
            P("gz", ("gx", "gy")),
            P("gz", ("gx", "gy")),
            P("gy", ("gz", "gx")),
        ),
        out_specs=(
            P("gy", ("gz", "gx")),
            P("gy", ("gz", "gx")),
            P("gz", ("gx", "gy")),
            P("gz", ("gx", "gy")),
            P("gz", ("gx", "gy")),
        ),
        check_vma=False,
    )
```

time: 355 us -> 191 us (0.54)
  waiting for transfers between devices: 253 us -> 83.4 us
  Pallas kernels: 0 us -> 56.3 us
  matrix products: 53.2 us -> 0 us
  starting transfers between devices: 0.69 us -> 40.2 us
  local copies, waits for them, and re-layouts: 28 us -> 8.73 us
  between operations: 14 us -> 1.1 us
  other arithmetic: 4.77 us -> 0.88 us
    all_gather x7 -> x0, waiting for transfers between devices: 146 us -> none  [the longest x2 58.9 us: gather_rows(): rows = lax.all_gather(block, 'gy', axis=0, tiled=True)]
    reduce_scatter x6 -> x0, waiting for transfers between devices: 105 us -> none  [the longest x1 41.6 us: per_device(): lax.psum_scatter(gate_up, 'gz', scatter_dimension=0, tiled=True)]
    ppermute x0 -> x30, waiting for transfers between devices: none -> 83.4 us  [swap(): return lax.ppermute(value, axis, [(i, i ^ mask) for i in range(size)])]
    pallas_call x0 -> x19, Pallas kernels: none -> 56.3 us  [the longest x4 22.2 us: backward_products(): pl.pallas_call(kernel, grid_spec=pltpu.PrefetchScalarGridSpec(num_scalar_...]
    dot_general x9 -> x0, matrix products: 53.2 us -> none  [the longest x3 20.6 us: dot_last(): lax.dot_general(left, right, (((1,), (1,)), ((), ())), preferred_element_...]
    ppermute x0 -> x30, starting transfers between devices: none -> 40.2 us  [swap(): return lax.ppermute(value, axis, [(i, i ^ mask) for i in range(size)])]
    unnamed x13 -> x50, local copies, waits for them, and re-layouts: 28 us -> 8.73 us
  transfers between devices with their start and end apart: 13 -> 30, of which waited for: 12 -> 15; matrix products, arithmetic and copies ran while one was open for 24% -> 0% of each run, Pallas kernels for 0% -> 29%
where the time goes in v2:
time: 191 us
  waiting for transfers between devices  83.4 us (44%)
  Pallas kernels  56.3 us (29%)
  starting transfers between devices  40.2 us (21%)
  local copies, waits for them, and re-layouts  8.73 us (5%)
    ppermute x30, waiting for transfers between devices, swap(): return lax.ppermute(value, axis, [(i, i ^ mask) for i in range(size)])  83.4 us
    ppermute x30, starting transfers between devices, swap(): return lax.ppermute(value, axis, [(i, i ^ mask) for i in range(size)])  40.2 us
    pallas_call x4, Pallas kernels, backward_products(): pl.pallas_call(kernel, grid_spec=pltpu.PrefetchScalarGridSpec(num_scalar_...  22.2 us
    pallas_call x4, Pallas kernels, forward_products(): pl.pallas_call(kernel, grid_spec=pltpu.PrefetchScalarGridSpec(num_scalar_...  17.3 us
    pallas_call x1, Pallas kernels, weight_grads(): pl.pallas_call(kernel, grid_spec=pltpu.PrefetchScalarGridSpec(num_scalar_...  14.2 us
    unnamed x50, local copies, waits for them, and re-layouts  8.73 us
  transfers between devices with their start and end apart: 30, of which 15 were waited for; matrix products, arithmetic and copies ran while one was open for 0% of the time, Pallas kernels for 29%

profile of v2, /device:TPU:0, one launch (start us, length us, event | category | flops | bytes accessed | tf_op | source)
XLA Modules:
  0.0 190.6 jit_solution(6717209155745887803)
XLA Ops:
  0.6 0.9 copy-done.23
  1.6 0.9 copy-done.24
  2.5 0.1 ordered_rows.1.own_ref.refs_0_
  2.7 4.0 %collective-permute-start.22 = (bf16[2,128,1024]{2,1,0:T(8,128)(2,1)S(1)}, bf16[2,128,1024]{2,1,0:T(8,128)(2,1)S(1)}, u32[]{:S(2)}, u32[]{:S(2)}) collective-permute-start(bf16[2,128,1024]{2,1,0:T(8,128)(2,1)S(1)} %ordered_rows.1.own_ref.refs_0_), channel_id=1, source_target_pairs={{0,12},{4,8},{8,4},{12,0},{1,13},{5,9},{9,5},{13,1},{2,14},{6,10},... | collective-permute-start | bytes 1572872 | tf_op jit(solution)/shard_map/ppermute | solution.py:20
  6.7 0.5 collective-permute-start.14
  7.2 11.5 %collective-permute-done.22.own_ref.refs_3_ = bf16[2,128,1024]{2,1,0:T(8,128)(2,1)S(1)} collective-permute-done((bf16[2,128,1024]{2,1,0:T(8,128)(2,1)S(1)}, bf16[2,128,1024]{2,1,0:T(8,128)(2,1)S(1)}, u32[]{:S(2)}, u32[]{:S(2)}) %collective-permute-start.22) | collective-permute-done | bytes 524320 | tf_op jit(solution)/shard_map/ppermute | solution.py:20
  18.7 1.7 collective-permute-start.6
  20.4 9.4 %collective-permute-done.14.own_ref.refs_2_ = bf16[2,128,1024]{2,1,0:T(8,128)(2,1)S(1)} collective-permute-done((bf16[2,128,1024]{2,1,0:T(8,128)(2,1)S(1)}, bf16[2,128,1024]{2,1,0:T(8,128)(2,1)S(1)}, u32[]{:S(2)}, u32[]{:S(2)}) %collective-permute-start.14) | collective-permute-done | bytes 524320 | tf_op jit(solution)/shard_map/ppermute | solution.py:20
  29.8 0.5 collective-permute-start
  30.3 2.4 %copy-done = bf16[2048,1024]{1,0:T(8,128)(2,1)S(1)} copy-done((bf16[2048,1024]{1,0:T(8,128)(2,1)S(1)}, bf16[2048,1024]{1,0:T(8,128)(2,1)}, u32[]{:S(2)}) %copy-start) | copy-done | bytes 4194328
  32.7 2.2 %copy-done.2 = bf16[2048,1024]{1,0:T(8,128)(2,1)S(1)} copy-done((bf16[2048,1024]{1,0:T(8,128)(2,1)S(1)}, bf16[2048,1024]{1,0:T(8,128)(2,1)}, u32[]{:S(2)}) %copy-start.2) | copy-done | bytes 4194328
  34.9 2.2 %copy-done.3 = bf16[2048,1024]{1,0:T(8,128)(2,1)S(1)} copy-done((bf16[2048,1024]{1,0:T(8,128)(2,1)S(1)}, bf16[2048,1024]{1,0:T(8,128)(2,1)}, u32[]{:S(2)}) %copy-start.3) | copy-done | bytes 4194328
  37.1 4.1 %forward_products.7 = (bf16[3,64,1024]{2,1,0:T(8,128)(2,1)S(1)}, bf16[3,64,1024]{2,1,0:T(8,128)(2,1)S(1)}) custom-call(s32[1]{0:T(128)} %bitcast.1.core_ref, bf16[2,128,1024]{2,1,0:T(8,128)(2,1)S(1)} %collective-permute-done.22.own_ref.refs_3_, bf16[2,128,1024]{2,1,0:T(8,128)(2,1)S(1)} %collective-permute-done.23.other_ref.refs_7_, ...), custom_call_target="tpu_custom_call" | custom-call | tf_op jit(solution)/shard_map/forward_products/pallas_call | solution.py:81
  41.2 1.8 collective-permute-start.24
  43.1 4.2 %forward_products.6 = (bf16[3,64,1024]{2,1,0:T(8,128)(2,1)S(1)}, bf16[3,64,1024]{2,1,0:T(8,128)(2,1)S(1)}) custom-call(s32[1]{0:T(128)} %bitcast.1.core_ref, bf16[2,128,1024]{2,1,0:T(8,128)(2,1)S(1)} %collective-permute-done.14.own_ref.refs_2_, bf16[2,128,1024]{2,1,0:T(8,128)(2,1)S(1)} %collective-permute-done.15.other_ref.refs_6_, ...), custom_call_target="tpu_custom_call" | custom-call | tf_op jit(solution)/shard_map/forward_products/pallas_call | solution.py:81
  47.2 0.3 collective-permute-start.16
  47.6 4.8 %forward_products.4 = (bf16[3,64,1024]{2,1,0:T(8,128)(2,1)S(1)}, bf16[3,64,1024]{2,1,0:T(8,128)(2,1)S(1)}) custom-call(s32[1]{0:T(128)} %bitcast.1.core_ref, bf16[2,128,1024]{2,1,0:T(8,128)(2,1)S(1)} %ordered_rows.1.own_ref.refs_0_, bf16[2,128,1024]{2,1,0:T(8,128)(2,1)} %collective-permute-done.other_ref.refs_4_, bf16[2048,1024]{1,0:T(8,128)(2,1)S(1)} %copy-done.1, ...), custom_call_target="tpu_custom_call" | custom-call | tf_op jit(solution)/shard_map/forward_products/pallas_call | solution.py:81
  52.4 0.9 collective-permute-done.24.b_ref
  53.2 0.1 add_halves.7
  53.3 2.9 %collective-permute-start.25 = (bf16[3,32,1024]{2,1,0:T(8,128)(2,1)S(1)}, bf16[3,32,1024]{2,1,0:T(8,128)(2,1)S(1)}, u32[]{:S(2)}, u32[]{:S(2)}) collective-permute-start(bf16[3,32,1024]{2,1,0:T(8,128)(2,1)S(1)} %get-tuple-element.55), channel_id=1, source_target_pairs={{0,2},{1,3},{2,0},{3,1},{4,6},{5,7},{6,4},{7,5},{8,10},{9,11},{10,... | collective-permute-start | bytes 589832 | tf_op jit(solution)/shard_map/ppermute | solution.py:20
  56.2 1.6 collective-permute-start.1
  57.8 4.3 %forward_products.5 = (bf16[3,64,1024]{2,1,0:T(8,128)(2,1)S(1)}, bf16[3,64,1024]{2,1,0:T(8,128)(2,1)S(1)}) custom-call(s32[1]{0:T(128)} %bitcast.1.core_ref, bf16[2,128,1024]{2,1,0:T(8,128)(2,1)S(1)} %collective-permute-done.6.own_ref.refs_1_, bf16[2,128,1024]{2,1,0:T(8,128)(2,1)S(1)} %collective-permute-done.7.other_ref.refs_5_, ...), custom_call_target="tpu_custom_call" | custom-call | tf_op jit(solution)/shard_map/forward_products/pallas_call | solution.py:81
  62.0 0.5 collective-permute-start.8
  62.6 2.6 %collective-permute-done.25.b_ref = bf16[3,32,1024]{2,1,0:T(8,128)(2,1)S(1)} collective-permute-done((bf16[3,32,1024]{2,1,0:T(8,128)(2,1)S(1)}, bf16[3,32,1024]{2,1,0:T(8,128)(2,1)S(1)}, u32[]{:S(2)}, u32[]{:S(2)}) %collective-permute-start.25) | collective-permute-done | bytes 196640 | tf_op jit(solution)/shard_map/ppermute | solution.py:20
  65.2 0.1 activations.7.refs_0_.refs_17_
  65.3 3.4 %collective-permute-start.26 = (bf16[3,32,1024]{2,1,0:T(8,128)(2,1)S(1)}, bf16[3,32,1024]{2,1,0:T(8,128)(2,1)S(1)}, u32[]{:S(2)}, u32[]{:S(2)}) collective-permute-start(bf16[3,32,1024]{2,1,0:T(8,128)(2,1)S(1)} %activations.7.refs_0_.refs_17_), channel_id=1, source_target_pairs={{0,2},{1,3},{2,0},{3,1},{4,6},{5,7},{6,4},{7,5},{8,10},{9,11},{10,... | collective-permute-start | bytes 589832 | tf_op jit(solution)/shard_map/ppermute | solution.py:20
  68.7 0.1 add_halves.6
  68.8 0.1 collective-permute-start.17
  68.9 13.8 %collective-permute-done.1.b_ref = bf16[3,64,1024]{2,1,0:T(8,128)(2,1)S(1)} collective-permute-done((bf16[3,64,1024]{2,1,0:T(8,128)(2,1)S(1)}, bf16[3,64,1024]{2,1,0:T(8,128)(2,1)S(1)}, u32[]{:S(2)}, u32[]{:S(2)}) %collective-permute-start.1) | collective-permute-done | bytes 393248 | tf_op jit(solution)/shard_map/ppermute | solution.py:20
  82.7 0.1 add_halves.4
  82.8 3.4 %collective-permute-done.26.refs_1_.refs_18_ = bf16[3,32,1024]{2,1,0:T(8,128)(2,1)S(1)} collective-permute-done((bf16[3,32,1024]{2,1,0:T(8,128)(2,1)S(1)}, bf16[3,32,1024]{2,1,0:T(8,128)(2,1)S(1)}, u32[]{:S(2)}, u32[]{:S(2)}) %collective-permute-start.26) | collective-permute-done | bytes 196640 | tf_op jit(solution)/shard_map/ppermute | solution.py:20
  86.3 3.6 %collective-permute-start.27 = (bf16[3,64,1024]{2,1,0:T(8,128)(2,1)S(1)}, bf16[3,64,1024]{2,1,0:T(8,128)(2,1)S(1)}, u32[]{:S(2)}, u32[]{:S(2)}) collective-permute-start(bf16[3,64,1024]{2,1,0:T(8,128)(2,1)S(1)} %pad_maximum_fusion.3), channel_id=1, source_target_pairs={{0,1},{1,0},{2,3},{3,2},{4,5},{5,4},{6,7},{7,6},{8,9},{9,8},{10,11... | collective-permute-start | bytes 1179656 | tf_op jit(solution)/shard_map/ppermute | solution.py:20
  89.8 1.3 collective-permute-done.8.b_ref
  91.2 0.1 add_halves.5
  91.3 9.5 %collective-permute-start.9 = (bf16[3,32,1024]{2,1,0:T(8,128)(2,1)S(1)}, bf16[3,32,1024]{2,1,0:T(8,128)(2,1)S(1)}, u32[]{:S(2)}, u32[]{:S(2)}) collective-permute-start(bf16[3,32,1024]{2,1,0:T(8,128)(2,1)S(1)} %get-tuple-element.43), channel_id=1, source_target_pairs={{0,2},{1,3},{2,0},{3,1},{4,6},{5,7},{6,4},{7,5},{8,10},{9,11},{10,... | collective-permute-start | bytes 589832 | tf_op jit(solution)/shard_map/ppermute | solution.py:20
  100.7 0.1 activations.6.refs_0_.refs_14_
  100.8 0.1 collective-permute-start.18
  100.9 2.7 %collective-permute-done.2.b_ref = bf16[3,32,1024]{2,1,0:T(8,128)(2,1)S(1)} collective-permute-done((bf16[3,32,1024]{2,1,0:T(8,128)(2,1)S(1)}, bf16[3,32,1024]{2,1,0:T(8,128)(2,1)S(1)}, u32[]{:S(2)}, u32[]{:S(2)}) %collective-permute-start.2) | collective-permute-done | bytes 196640 | tf_op jit(solution)/shard_map/ppermute | solution.py:20
  103.6 0.1 activations.4.refs_0_.refs_8_
  103.7 3.5 %collective-permute-start.3 = (bf16[3,32,1024]{2,1,0:T(8,128)(2,1)S(1)}, bf16[3,32,1024]{2,1,0:T(8,128)(2,1)S(1)}, u32[]{:S(2)}, u32[]{:S(2)}) collective-permute-start(bf16[3,32,1024]{2,1,0:T(8,128)(2,1)S(1)} %activations.4.refs_0_.refs_8_), channel_id=1, source_target_pairs={{0,2},{1,3},{2,0},{3,1},{4,6},{5,7},{6,4},{7,5},{8,10},{9,11},{10,... | collective-permute-start | bytes 589832 | tf_op jit(solution)/shard_map/ppermute | solution.py:20
  107.3 16.8 %collective-permute-done.9.b_ref = bf16[3,32,1024]{2,1,0:T(8,128)(2,1)S(1)} collective-permute-done((bf16[3,32,1024]{2,1,0:T(8,128)(2,1)S(1)}, bf16[3,32,1024]{2,1,0:T(8,128)(2,1)S(1)}, u32[]{:S(2)}, u32[]{:S(2)}) %collective-permute-start.9) | collective-permute-done | bytes 196640 | tf_op jit(solution)/shard_map/ppermute | solution.py:20
  124.0 0.1 activations.5.refs_0_.refs_11_
  124.1 0.1 collective-permute-start.10
  124.2 6.1 %collective-permute-done.18.refs_1_.refs_15_ = bf16[3,32,1024]{2,1,0:T(8,128)(2,1)S(1)} collective-permute-done((bf16[3,32,1024]{2,1,0:T(8,128)(2,1)S(1)}, bf16[3,32,1024]{2,1,0:T(8,128)(2,1)S(1)}, u32[]{:S(2)}, u32[]{:S(2)}) %collective-permute-start.18) | collective-permute-done | bytes 196640 | tf_op jit(solution)/shard_map/ppermute | solution.py:20
  130.5 5.6 %backward_products.7 = (bf16[2,128,1024]{2,1,0:T(8,128)(2,1)S(1)}, bf16[2,128,1024]{2,1,0:T(8,128)(2,1)S(1)}) custom-call(s32[1]{0:T(128)} %bitcast.1.core_ref, bf16[3,32,1024]{2,1,0:T(8,128)(2,1)S(1)} %activations.7.refs_0_.refs_17_, bf16[3,32,1024]{2,1,0:T(8,128)(2,1)S(1)} %collective-permute-done.26.refs_1_.refs_18_, ...), custom_call_target="tpu_custom_call" | custom-call | tf_op jit(solution)/shard_map/backward_products/pallas_call | solution.py:165
  136.2 2.0 %collective-permute-start.4 = (bf16[3,64,1024]{2,1,0:T(8,128)(2,1)S(1)}, bf16[3,64,1024]{2,1,0:T(8,128)(2,1)S(1)}, u32[]{:S(2)}, u32[]{:S(2)}) collective-permute-start(bf16[3,64,1024]{2,1,0:T(8,128)(2,1)S(1)} %pad_maximum_fusion), channel_id=1, source_target_pairs={{0,1},{1,0},{2,3},{3,2},{4,5},{5,4},{6,7},{7,6},{8,9},{9,8},{10,11... | collective-permute-start | bytes 1179656 | tf_op jit(solution)/shard_map/ppermute | solution.py:20
  138.3 0.1 collective-permute-start.11
  138.4 0.4 collective-permute-done.19.refs_2_.refs_16_
  138.8 5.5 %backward_products.6 = (bf16[2,128,1024]{2,1,0:T(8,128)(2,1)S(1)}, bf16[2,128,1024]{2,1,0:T(8,128)(2,1)S(1)}) custom-call(s32[1]{0:T(128)} %bitcast.1.core_ref, bf16[3,32,1024]{2,1,0:T(8,128)(2,1)S(1)} %activations.6.refs_0_.refs_14_, bf16[3,32,1024]{2,1,0:T(8,128)(2,1)S(1)} %collective-permute-done.18.refs_1_.refs_15_, ...), custom_call_target="tpu_custom_call" | custom-call | tf_op jit(solution)/shard_map/backward_products/pallas_call | solution.py:165
  144.5 3.8 %collective-permute-done.4.refs_2_.refs_10_ = bf16[3,64,1024]{2,1,0:T(8,128)(2,1)S(1)} collective-permute-done((bf16[3,64,1024]{2,1,0:T(8,128)(2,1)S(1)}, bf16[3,64,1024]{2,1,0:T(8,128)(2,1)S(1)}, u32[]{:S(2)}, u32[]{:S(2)}) %collective-permute-start.4) | collective-permute-done | bytes 393248 | tf_op jit(solution)/shard_map/ppermute | solution.py:20
  148.3 5.5 %backward_products.4 = (bf16[2,128,1024]{2,1,0:T(8,128)(2,1)S(1)}, bf16[2,128,1024]{2,1,0:T(8,128)(2,1)S(1)}) custom-call(s32[1]{0:T(128)} %bitcast.1.core_ref, bf16[3,32,1024]{2,1,0:T(8,128)(2,1)S(1)} %activations.4.refs_0_.refs_8_, bf16[3,32,1024]{2,1,0:T(8,128)(2,1)S(1)} %collective-permute-done.3.refs_1_.refs_9_, ...), custom_call_target="tpu_custom_call" | custom-call | tf_op jit(solution)/shard_map/backward_products/pallas_call | solution.py:165
  153.9 2.5 %collective-permute-done.11.refs_2_.refs_13_ = bf16[3,64,1024]{2,1,0:T(8,128)(2,1)S(1)} collective-permute-done((bf16[3,64,1024]{2,1,0:T(8,128)(2,1)S(1)}, bf16[3,64,1024]{2,1,0:T(8,128)(2,1)S(1)}, u32[]{:S(2)}, u32[]{:S(2)}) %collective-permute-start.11) | collective-permute-done | bytes 393248 | tf_op jit(solution)/shard_map/ppermute | solution.py:20
  156.4 5.6 %backward_products.5 = (bf16[2,128,1024]{2,1,0:T(8,128)(2,1)S(1)}, bf16[2,128,1024]{2,1,0:T(8,128)(2,1)S(1)}) custom-call(s32[1]{0:T(128)} %bitcast.1.core_ref, bf16[3,32,1024]{2,1,0:T(8,128)(2,1)S(1)} %activations.5.refs_0_.refs_11_, bf16[3,32,1024]{2,1,0:T(8,128)(2,1)S(1)} %collective-permute-done.10.refs_1_.refs_12_, ...), custom_call_target="tpu_custom_call" | custom-call | tf_op jit(solution)/shard_map/backward_products/pallas_call | solution.py:165
  162.1 0.2 add_convert_fusion
  162.3 1.8 collective-permute-start.29
  164.1 0.2 add_convert_fusion.1
  164.3 1.3 collective-permute-start.21
  165.6 0.2 add_convert_fusion.2
  165.8 0.6 collective-permute-start.13
  166.4 14.2 %weight_grads.1 = (f32[2048,1024]{1,0:T(8,128)}, f32[2048,1024]{1,0:T(8,128)}, f32[2048,1024]{1,0:T(8,128)}) custom-call(s32[1]{0:T(128)} %bitcast.1.core_ref, bf16[2,128,1024]{2,1,0:T(8,128)(2,1)} %copy-done.4, bf16[2,128,1024]{2,1,0:T(8,128)(2,1)} %copy-done.12, bf16[2,128,1024]{2,1,0:T(8,128)(2,1)} %copy-done.10, bf16[2,128,1024]{2,1,0:T(8,128)(2,1)} %copy-done.9, ...), custom_call_target="tpu_custom_call" | custom-call | tf_op jit(solution)/shard_map/weight_grads/pallas_call | solution.py:226
  180.6 0.2 add_convert_fusion.3.refs_0_
  180.8 8.0 %collective-permute-done.21.refs_2_ = bf16[2,128,1024]{2,1,0:T(8,128)(2,1)S(1)} collective-permute-done((bf16[2,128,1024]{2,1,0:T(8,128)(2,1)S(1)}, bf16[2,128,1024]{2,1,0:T(8,128)(2,1)S(1)}, u32[]{:S(2)}, u32[]{:S(2)}) %collective-permute-start.21) | collective-permute-done | bytes 524320 | tf_op jit(solution)/shard_map/ppermute | solution.py:20
  188.8 0.1 collective-permute-done.13.refs_1_
  188.9 1.7 final_sum.1
  (73 shorter events, 0.6 us)
Async XLA Ops:
  0.6 1.0 copy-start.23
  1.6 0.9 copy-start.24
  2.7 44.9 %copy-start.4 = (bf16[2,128,1024]{2,1,0:T(8,128)(2,1)}, bf16[2,128,1024]{2,1,0:T(8,128)(2,1)S(1)}, u32[]{:S(2)}) copy-start(bf16[2,128,1024]{2,1,0:T(8,128)(2,1)S(1)} %ordered_rows.1.own_ref.refs_0_) | copy-start | bytes 1572868
  2.7 16.0 %collective-permute-start.22 = (bf16[2,128,1024]{2,1,0:T(8,128)(2,1)S(1)}, bf16[2,128,1024]{2,1,0:T(8,128)(2,1)S(1)}, u32[]{:S(2)}, u32[]{:S(2)}) collective-permute-start(bf16[2,128,1024]{2,1,0:T(8,128)(2,1)S(1)} %ordered_rows.1.own_ref.refs_0_), channel_id=1, source_target_pairs={{0,12},{4,8},{8,4},{12,0},{1,13},{5,9},{9,5},{13,1},{2,14},{6,10},... | collective-permute-start | bytes 1572872 | tf_op jit(solution)/shard_map/ppermute | solution.py:20
  6.7 23.2 %collective-permute-start.14 = (bf16[2,128,1024]{2,1,0:T(8,128)(2,1)S(1)}, bf16[2,128,1024]{2,1,0:T(8,128)(2,1)S(1)}, u32[]{:S(2)}, u32[]{:S(2)}) collective-permute-start(bf16[2,128,1024]{2,1,0:T(8,128)(2,1)S(1)} %ordered_rows.1.own_ref.refs_0_), channel_id=1, source_target_pairs={{0,8},{4,12},{8,0},{12,4},{1,9},{5,13},{9,1},{13,5},{2,10},{6,14},... | collective-permute-start | bytes 1572872 | tf_op jit(solution)/shard_map/ppermute | solution.py:20
  18.7 28.5 %copy-start.9 = (bf16[2,128,1024]{2,1,0:T(8,128)(2,1)}, bf16[2,128,1024]{2,1,0:T(8,128)(2,1)S(1)}, u32[]{:S(2)}) copy-start(bf16[2,128,1024]{2,1,0:T(8,128)(2,1)S(1)} %collective-permute-done.22.own_ref.refs_3_) | copy-start | bytes 1572868
  18.7 11.6 %collective-permute-start.23 = (bf16[2,128,1024]{2,1,0:T(8,128)(2,1)S(1)}, bf16[2,128,1024]{2,1,0:T(8,128)(2,1)S(1)}, u32[]{:S(2)}, u32[]{:S(2)}) collective-permute-start(bf16[2,128,1024]{2,1,0:T(8,128)(2,1)S(1)} %collective-permute-done.22.own_ref.refs_3_), channel_id=1, source_target_pairs={{0,16},{16,0},{1,17},{17,1},{2,18},{18,2},{3,19},{19,3},{4,20},{20... | collective-permute-start | bytes 1572872 | tf_op jit(solution)/shard_map/ppermute | solution.py:20
  18.7 24.3 %collective-permute-start.6 = (bf16[2,128,1024]{2,1,0:T(8,128)(2,1)S(1)}, bf16[2,128,1024]{2,1,0:T(8,128)(2,1)S(1)}, u32[]{:S(2)}, u32[]{:S(2)}) collective-permute-start(bf16[2,128,1024]{2,1,0:T(8,128)(2,1)S(1)} %ordered_rows.1.own_ref.refs_0_), channel_id=1, source_target_pairs={{0,4},{4,0},{8,12},{12,8},{1,5},{5,1},{9,13},{13,9},{2,6},{6,2},{1... | collective-permute-start | bytes 1572872 | tf_op jit(solution)/shard_map/ppermute | solution.py:20
  29.8 17.4 %copy-start.10 = (bf16[2,128,1024]{2,1,0:T(8,128)(2,1)}, bf16[2,128,1024]{2,1,0:T(8,128)(2,1)S(1)}, u32[]{:S(2)}) copy-start(bf16[2,128,1024]{2,1,0:T(8,128)(2,1)S(1)} %collective-permute-done.14.own_ref.refs_2_) | copy-start | bytes 1572868
  29.8 13.2 %collective-permute-start.15 = (bf16[2,128,1024]{2,1,0:T(8,128)(2,1)S(1)}, bf16[2,128,1024]{2,1,0:T(8,128)(2,1)S(1)}, u32[]{:S(2)}, u32[]{:S(2)}) collective-permute-start(bf16[2,128,1024]{2,1,0:T(8,128)(2,1)S(1)} %collective-permute-done.14.own_ref.refs_2_), channel_id=1, source_target_pairs={{0,16},{16,0},{1,17},{17,1},{2,18},{18,2},{3,19},{19,3},{4,20},{20... | collective-permute-start | bytes 1572872 | tf_op jit(solution)/shard_map/ppermute | solution.py:20
  29.8 17.8 %collective-permute-start = (bf16[2,128,1024]{2,1,0:T(8,128)(2,1)S(1)}, bf16[2,128,1024]{2,1,0:T(8,128)(2,1)}, u32[]{:S(2)}, u32[]{:S(2)}) collective-permute-start(bf16[2,128,1024]{2,1,0:T(8,128)(2,1)S(1)} %ordered_rows.1.own_ref.refs_0_), channel_id=1, source_target_pairs={{0,16},{16,0},{1,17},{17,1},{2,18},{18,2},{3,19},{19,3},{4,20},{20... | collective-permute-start | bytes 1572872 | tf_op jit(solution)/shard_map/ppermute | solution.py:20
  30.3 16.9 %copy-start.11 = (bf16[2,128,1024]{2,1,0:T(8,128)(2,1)}, bf16[2,128,1024]{2,1,0:T(8,128)(2,1)S(1)}, u32[]{:S(2)}) copy-start(bf16[2,128,1024]{2,1,0:T(8,128)(2,1)S(1)} %collective-permute-done.23.other_ref.refs_7_) | copy-start | bytes 1572868
  30.3 2.4 %copy-start = (bf16[2048,1024]{1,0:T(8,128)(2,1)S(1)}, bf16[2048,1024]{1,0:T(8,128)(2,1)}, u32[]{:S(2)}) copy-start(bf16[2048,1024]{1,0:T(8,128)(2,1)} %refs_3_.7) | copy-start | bytes 12582916
  32.7 2.2 %copy-start.2 = (bf16[2048,1024]{1,0:T(8,128)(2,1)S(1)}, bf16[2048,1024]{1,0:T(8,128)(2,1)}, u32[]{:S(2)}) copy-start(bf16[2048,1024]{1,0:T(8,128)(2,1)} %refs_4_.7) | copy-start | bytes 12582916
  34.9 2.2 %copy-start.3 = (bf16[2048,1024]{1,0:T(8,128)(2,1)S(1)}, bf16[2048,1024]{1,0:T(8,128)(2,1)}, u32[]{:S(2)}) copy-start(bf16[2048,1024]{1,0:T(8,128)(2,1)} %refs_5_.7) | copy-start | bytes 12582916
  41.2 6.4 %copy-start.1 = (bf16[2048,1024]{1,0:T(8,128)(2,1)S(1)}, bf16[2048,1024]{1,0:T(8,128)(2,1)}, u32[]{:S(2)}) copy-start(bf16[2048,1024]{1,0:T(8,128)(2,1)} %refs_3_.7) | copy-start | bytes 12582916
  41.2 12.0 %collective-permute-start.24 = (bf16[3,64,1024]{2,1,0:T(8,128)(2,1)S(1)}, bf16[3,64,1024]{2,1,0:T(8,128)(2,1)S(1)}, u32[]{:S(2)}, u32[]{:S(2)}) collective-permute-start(bf16[3,64,1024]{2,1,0:T(8,128)(2,1)S(1)} %get-tuple-element.53), channel_id=1, source_target_pairs={{0,1},{1,0},{2,3},{3,2},{4,5},{5,4},{6,7},{7,6},{8,9},{9,8},{10,11... | collective-permute-start | bytes 1179656 | tf_op jit(solution)/shard_map/ppermute | solution.py:20
  43.0 14.7 %copy-start.12 = (bf16[2,128,1024]{2,1,0:T(8,128)(2,1)}, bf16[2,128,1024]{2,1,0:T(8,128)(2,1)S(1)}, u32[]{:S(2)}) copy-start(bf16[2,128,1024]{2,1,0:T(8,128)(2,1)S(1)} %collective-permute-done.6.own_ref.refs_1_) | copy-start | bytes 1572868
  43.0 14.7 %collective-permute-start.7 = (bf16[2,128,1024]{2,1,0:T(8,128)(2,1)S(1)}, bf16[2,128,1024]{2,1,0:T(8,128)(2,1)S(1)}, u32[]{:S(2)}, u32[]{:S(2)}) collective-permute-start(bf16[2,128,1024]{2,1,0:T(8,128)(2,1)S(1)} %collective-permute-done.6.own_ref.refs_1_), channel_id=1, source_target_pairs={{0,16},{16,0},{1,17},{17,1},{2,18},{18,2},{3,19},{19,3},{4,20},{20... | collective-permute-start | bytes 1572872 | tf_op jit(solution)/shard_map/ppermute | solution.py:20
  43.1 9.3 %copy-start.13 = (bf16[2,128,1024]{2,1,0:T(8,128)(2,1)}, bf16[2,128,1024]{2,1,0:T(8,128)(2,1)S(1)}, u32[]{:S(2)}) copy-start(bf16[2,128,1024]{2,1,0:T(8,128)(2,1)S(1)} %collective-permute-done.15.other_ref.refs_6_) | copy-start | bytes 1572868
  47.2 21.5 %collective-permute-start.16 = (bf16[3,64,1024]{2,1,0:T(8,128)(2,1)S(1)}, bf16[3,64,1024]{2,1,0:T(8,128)(2,1)S(1)}, u32[]{:S(2)}, u32[]{:S(2)}) collective-permute-start(bf16[3,64,1024]{2,1,0:T(8,128)(2,1)S(1)} %get-tuple-element.47), channel_id=1, source_target_pairs={{0,1},{1,0},{2,3},{3,2},{4,5},{5,4},{6,7},{7,6},{8,9},{9,8},{10,11... | collective-permute-start | bytes 1179656 | tf_op jit(solution)/shard_map/ppermute | solution.py:20
  53.3 11.8 %collective-permute-start.25 = (bf16[3,32,1024]{2,1,0:T(8,128)(2,1)S(1)}, bf16[3,32,1024]{2,1,0:T(8,128)(2,1)S(1)}, u32[]{:S(2)}, u32[]{:S(2)}) collective-permute-start(bf16[3,32,1024]{2,1,0:T(8,128)(2,1)S(1)} %get-tuple-element.55), channel_id=1, source_target_pairs={{0,2},{1,3},{2,0},{3,1},{4,6},{5,7},{6,4},{7,5},{8,10},{9,11},{10,... | collective-permute-start | bytes 589832 | tf_op jit(solution)/shard_map/ppermute | solution.py:20
  56.2 26.5 %collective-permute-start.1 = (bf16[3,64,1024]{2,1,0:T(8,128)(2,1)S(1)}, bf16[3,64,1024]{2,1,0:T(8,128)(2,1)S(1)}, u32[]{:S(2)}, u32[]{:S(2)}) collective-permute-start(bf16[3,64,1024]{2,1,0:T(8,128)(2,1)S(1)} %get-tuple-element.35), channel_id=1, source_target_pairs={{0,1},{1,0},{2,3},{3,2},{4,5},{5,4},{6,7},{7,6},{8,9},{9,8},{10,11... | collective-permute-start | bytes 1179656 | tf_op jit(solution)/shard_map/ppermute | solution.py:20
  57.8 33.5 %copy-start.14 = (bf16[2,128,1024]{2,1,0:T(8,128)(2,1)}, bf16[2,128,1024]{2,1,0:T(8,128)(2,1)S(1)}, u32[]{:S(2)}) copy-start(bf16[2,128,1024]{2,1,0:T(8,128)(2,1)S(1)} %collective-permute-done.7.other_ref.refs_5_) | copy-start | bytes 1572868
  62.0 29.1 %collective-permute-start.8 = (bf16[3,64,1024]{2,1,0:T(8,128)(2,1)S(1)}, bf16[3,64,1024]{2,1,0:T(8,128)(2,1)S(1)}, u32[]{:S(2)}, u32[]{:S(2)}) collective-permute-start(bf16[3,64,1024]{2,1,0:T(8,128)(2,1)S(1)} %get-tuple-element.41), channel_id=1, source_target_pairs={{0,1},{1,0},{2,3},{3,2},{4,5},{5,4},{6,7},{7,6},{8,9},{9,8},{10,11... | collective-permute-start | bytes 1179656 | tf_op jit(solution)/shard_map/ppermute | solution.py:20
  65.3 70.8 %copy-start.5 = (bf16[3,32,1024]{2,1,0:T(8,128)(2,1)}, bf16[3,32,1024]{2,1,0:T(8,128)(2,1)S(1)}, u32[]{:S(2)}) copy-start(bf16[3,32,1024]{2,1,0:T(8,128)(2,1)S(1)} %activations.7.refs_0_.refs_17_) | copy-start | bytes 589828
  65.3 20.9 %collective-permute-start.26 = (bf16[3,32,1024]{2,1,0:T(8,128)(2,1)S(1)}, bf16[3,32,1024]{2,1,0:T(8,128)(2,1)S(1)}, u32[]{:S(2)}, u32[]{:S(2)}) collective-permute-start(bf16[3,32,1024]{2,1,0:T(8,128)(2,1)S(1)} %activations.7.refs_0_.refs_17_), channel_id=1, source_target_pairs={{0,2},{1,3},{2,0},{3,1},{4,6},{5,7},{6,4},{7,5},{8,10},{9,11},{10,... | collective-permute-start | bytes 589832 | tf_op jit(solution)/shard_map/ppermute | solution.py:20
  68.8 31.9 %collective-permute-start.17 = (bf16[3,32,1024]{2,1,0:T(8,128)(2,1)S(1)}, bf16[3,32,1024]{2,1,0:T(8,128)(2,1)S(1)}, u32[]{:S(2)}, u32[]{:S(2)}) collective-permute-start(bf16[3,32,1024]{2,1,0:T(8,128)(2,1)S(1)} %get-tuple-element.49), channel_id=1, source_target_pairs={{0,2},{1,3},{2,0},{3,1},{4,6},{5,7},{6,4},{7,5},{8,10},{9,11},{10,... | collective-permute-start | bytes 589832 | tf_op jit(solution)/shard_map/ppermute | solution.py:20
  86.2 49.8 %copy-start.15 = (bf16[3,32,1024]{2,1,0:T(8,128)(2,1)}, bf16[3,32,1024]{2,1,0:T(8,128)(2,1)S(1)}, u32[]{:S(2)}) copy-start(bf16[3,32,1024]{2,1,0:T(8,128)(2,1)S(1)} %collective-permute-done.26.refs_1_.refs_18_) | copy-start | bytes 589828
  86.3 44.2 %collective-permute-start.27 = (bf16[3,64,1024]{2,1,0:T(8,128)(2,1)S(1)}, bf16[3,64,1024]{2,1,0:T(8,128)(2,1)S(1)}, u32[]{:S(2)}, u32[]{:S(2)}) collective-permute-start(bf16[3,64,1024]{2,1,0:T(8,128)(2,1)S(1)} %pad_maximum_fusion.3), channel_id=1, source_target_pairs={{0,1},{1,0},{2,3},{3,2},{4,5},{5,4},{6,7},{7,6},{8,9},{9,8},{10,11... | collective-permute-start | bytes 1179656 | tf_op jit(solution)/shard_map/ppermute | solution.py:20
  89.8 13.8 %collective-permute-start.2 = (bf16[3,32,1024]{2,1,0:T(8,128)(2,1)S(1)}, bf16[3,32,1024]{2,1,0:T(8,128)(2,1)S(1)}, u32[]{:S(2)}, u32[]{:S(2)}) collective-permute-start(bf16[3,32,1024]{2,1,0:T(8,128)(2,1)S(1)} %get-tuple-element.37), channel_id=1, source_target_pairs={{0,2},{1,3},{2,0},{3,1},{4,6},{5,7},{6,4},{7,5},{8,10},{9,11},{10,... | collective-permute-start | bytes 589832 | tf_op jit(solution)/shard_map/ppermute | solution.py:20
  91.3 32.8 %collective-permute-start.9 = (bf16[3,32,1024]{2,1,0:T(8,128)(2,1)S(1)}, bf16[3,32,1024]{2,1,0:T(8,128)(2,1)S(1)}, u32[]{:S(2)}, u32[]{:S(2)}) collective-permute-start(bf16[3,32,1024]{2,1,0:T(8,128)(2,1)S(1)} %get-tuple-element.43), channel_id=1, source_target_pairs={{0,2},{1,3},{2,0},{3,1},{4,6},{5,7},{6,4},{7,5},{8,10},{9,11},{10,... | collective-permute-start | bytes 589832 | tf_op jit(solution)/shard_map/ppermute | solution.py:20
  100.8 38.0 %copy-start.6 = (bf16[3,32,1024]{2,1,0:T(8,128)(2,1)}, bf16[3,32,1024]{2,1,0:T(8,128)(2,1)S(1)}, u32[]{:S(2)}) copy-start(bf16[3,32,1024]{2,1,0:T(8,128)(2,1)S(1)} %activations.6.refs_0_.refs_14_) | copy-start | bytes 589828
  100.8 29.5 %collective-permute-start.18 = (bf16[3,32,1024]{2,1,0:T(8,128)(2,1)S(1)}, bf16[3,32,1024]{2,1,0:T(8,128)(2,1)S(1)}, u32[]{:S(2)}, u32[]{:S(2)}) collective-permute-start(bf16[3,32,1024]{2,1,0:T(8,128)(2,1)S(1)} %activations.6.refs_0_.refs_14_), channel_id=1, source_target_pairs={{0,2},{1,3},{2,0},{3,1},{4,6},{5,7},{6,4},{7,5},{8,10},{9,11},{10,... | collective-permute-start | bytes 589832 | tf_op jit(solution)/shard_map/ppermute | solution.py:20
  103.7 44.6 %copy-start.7 = (bf16[3,32,1024]{2,1,0:T(8,128)(2,1)}, bf16[3,32,1024]{2,1,0:T(8,128)(2,1)S(1)}, u32[]{:S(2)}) copy-start(bf16[3,32,1024]{2,1,0:T(8,128)(2,1)S(1)} %activations.4.refs_0_.refs_8_) | copy-start | bytes 589828
  103.7 32.4 %collective-permute-start.3 = (bf16[3,32,1024]{2,1,0:T(8,128)(2,1)S(1)}, bf16[3,32,1024]{2,1,0:T(8,128)(2,1)S(1)}, u32[]{:S(2)}, u32[]{:S(2)}) collective-permute-start(bf16[3,32,1024]{2,1,0:T(8,128)(2,1)S(1)} %activations.4.refs_0_.refs_8_), channel_id=1, source_target_pairs={{0,2},{1,3},{2,0},{3,1},{4,6},{5,7},{6,4},{7,5},{8,10},{9,11},{10,... | collective-permute-start | bytes 589832 | tf_op jit(solution)/shard_map/ppermute | solution.py:20
  124.1 32.3 %copy-start.8 = (bf16[3,32,1024]{2,1,0:T(8,128)(2,1)}, bf16[3,32,1024]{2,1,0:T(8,128)(2,1)S(1)}, u32[]{:S(2)}) copy-start(bf16[3,32,1024]{2,1,0:T(8,128)(2,1)S(1)} %activations.5.refs_0_.refs_11_) | copy-start | bytes 589828
  124.1 14.1 %collective-permute-start.10 = (bf16[3,32,1024]{2,1,0:T(8,128)(2,1)S(1)}, bf16[3,32,1024]{2,1,0:T(8,128)(2,1)S(1)}, u32[]{:S(2)}, u32[]{:S(2)}) collective-permute-start(bf16[3,32,1024]{2,1,0:T(8,128)(2,1)S(1)} %activations.5.refs_0_.refs_11_), channel_id=1, source_target_pairs={{0,2},{1,3},{2,0},{3,1},{4,6},{5,7},{6,4},{7,5},{8,10},{9,11},{10,... | collective-permute-start | bytes 589832 | tf_op jit(solution)/shard_map/ppermute | solution.py:20
  130.3 14.0 %copy-start.16 = (bf16[3,32,1024]{2,1,0:T(8,128)(2,1)}, bf16[3,32,1024]{2,1,0:T(8,128)(2,1)S(1)}, u32[]{:S(2)}) copy-start(bf16[3,32,1024]{2,1,0:T(8,128)(2,1)S(1)} %collective-permute-done.18.refs_1_.refs_15_) | copy-start | bytes 589828
  130.4 8.4 %collective-permute-start.19 = (bf16[3,64,1024]{2,1,0:T(8,128)(2,1)S(1)}, bf16[3,64,1024]{2,1,0:T(8,128)(2,1)S(1)}, u32[]{:S(2)}, u32[]{:S(2)}) collective-permute-start(bf16[3,64,1024]{2,1,0:T(8,128)(2,1)S(1)} %pad_maximum_fusion.2), channel_id=1, source_target_pairs={{0,1},{1,0},{2,3},{3,2},{4,5},{5,4},{6,7},{7,6},{8,9},{9,8},{10,11... | collective-permute-start | bytes 1179656 | tf_op jit(solution)/shard_map/ppermute | solution.py:20
  130.5 13.9 %copy-start.19 = (bf16[3,64,1024]{2,1,0:T(8,128)(2,1)}, bf16[3,64,1024]{2,1,0:T(8,128)(2,1)S(1)}, u32[]{:S(2)}) copy-start(bf16[3,64,1024]{2,1,0:T(8,128)(2,1)S(1)} %collective-permute-done.27.refs_2_.refs_19_) | copy-start | bytes 1179652
  136.1 26.0 %collective-permute-start.28 = (bf16[2,128,1024]{2,1,0:T(8,128)(2,1)S(1)}, bf16[2,128,1024]{2,1,0:T(8,128)(2,1)S(1)}, u32[]{:S(2)}, u32[]{:S(2)}) collective-permute-start(bf16[2,128,1024]{2,1,0:T(8,128)(2,1)S(1)} %get-tuple-element.57), channel_id=1, source_target_pairs={{0,16},{16,0},{1,17},{17,1},{2,18},{18,2},{3,19},{19,3},{4,20},{20... | collective-permute-start | bytes 1572872 | tf_op jit(solution)/shard_map/ppermute | solution.py:20
  136.2 17.7 %copy-start.17 = (bf16[3,32,1024]{2,1,0:T(8,128)(2,1)}, bf16[3,32,1024]{2,1,0:T(8,128)(2,1)S(1)}, u32[]{:S(2)}) copy-start(bf16[3,32,1024]{2,1,0:T(8,128)(2,1)S(1)} %collective-permute-done.3.refs_1_.refs_9_) | copy-start | bytes 589828
  136.2 12.1 %collective-permute-start.4 = (bf16[3,64,1024]{2,1,0:T(8,128)(2,1)S(1)}, bf16[3,64,1024]{2,1,0:T(8,128)(2,1)S(1)}, u32[]{:S(2)}, u32[]{:S(2)}) collective-permute-start(bf16[3,64,1024]{2,1,0:T(8,128)(2,1)S(1)} %pad_maximum_fusion), channel_id=1, source_target_pairs={{0,1},{1,0},{2,3},{3,2},{4,5},{5,4},{6,7},{7,6},{8,9},{9,8},{10,11... | collective-permute-start | bytes 1179656 | tf_op jit(solution)/shard_map/ppermute | solution.py:20
  138.2 18.2 %copy-start.18 = (bf16[3,32,1024]{2,1,0:T(8,128)(2,1)}, bf16[3,32,1024]{2,1,0:T(8,128)(2,1)S(1)}, u32[]{:S(2)}) copy-start(bf16[3,32,1024]{2,1,0:T(8,128)(2,1)S(1)} %collective-permute-done.10.refs_1_.refs_12_) | copy-start | bytes 589828
  138.3 18.1 %collective-permute-start.11 = (bf16[3,64,1024]{2,1,0:T(8,128)(2,1)S(1)}, bf16[3,64,1024]{2,1,0:T(8,128)(2,1)S(1)}, u32[]{:S(2)}, u32[]{:S(2)}) collective-permute-start(bf16[3,64,1024]{2,1,0:T(8,128)(2,1)S(1)} %pad_maximum_fusion.1), channel_id=1, source_target_pairs={{0,1},{1,0},{2,3},{3,2},{4,5},{5,4},{6,7},{7,6},{8,9},{9,8},{10,11... | collective-permute-start | bytes 1179656 | tf_op jit(solution)/shard_map/ppermute | solution.py:20
  138.8 15.0 %copy-start.20 = (bf16[3,64,1024]{2,1,0:T(8,128)(2,1)}, bf16[3,64,1024]{2,1,0:T(8,128)(2,1)S(1)}, u32[]{:S(2)}) copy-start(bf16[3,64,1024]{2,1,0:T(8,128)(2,1)S(1)} %collective-permute-done.19.refs_2_.refs_16_) | copy-start | bytes 1179652
  144.4 19.7 %collective-permute-start.20 = (bf16[2,128,1024]{2,1,0:T(8,128)(2,1)S(1)}, bf16[2,128,1024]{2,1,0:T(8,128)(2,1)S(1)}, u32[]{:S(2)}, u32[]{:S(2)}) collective-permute-start(bf16[2,128,1024]{2,1,0:T(8,128)(2,1)S(1)} %get-tuple-element.51), channel_id=1, source_target_pairs={{0,16},{16,0},{1,17},{17,1},{2,18},{18,2},{3,19},{19,3},{4,20},{20... | collective-permute-start | bytes 1572872 | tf_op jit(solution)/shard_map/ppermute | solution.py:20
  148.3 13.7 %copy-start.21 = (bf16[3,64,1024]{2,1,0:T(8,128)(2,1)}, bf16[3,64,1024]{2,1,0:T(8,128)(2,1)S(1)}, u32[]{:S(2)}) copy-start(bf16[3,64,1024]{2,1,0:T(8,128)(2,1)S(1)} %collective-permute-done.4.refs_2_.refs_10_) | copy-start | bytes 1179652
  153.8 26.8 %collective-permute-start.5 = (bf16[2,128,1024]{2,1,0:T(8,128)(2,1)S(1)}, bf16[2,128,1024]{2,1,0:T(8,128)(2,1)S(1)}, u32[]{:S(2)}, u32[]{:S(2)}) collective-permute-start(bf16[2,128,1024]{2,1,0:T(8,128)(2,1)S(1)} %get-tuple-element.39), channel_id=1, source_target_pairs={{0,16},{16,0},{1,17},{17,1},{2,18},{18,2},{3,19},{19,3},{4,20},{20... | collective-permute-start | bytes 1572872 | tf_op jit(solution)/shard_map/ppermute | solution.py:20
  156.4 9.3 %copy-start.22 = (bf16[3,64,1024]{2,1,0:T(8,128)(2,1)}, bf16[3,64,1024]{2,1,0:T(8,128)(2,1)S(1)}, u32[]{:S(2)}) copy-start(bf16[3,64,1024]{2,1,0:T(8,128)(2,1)S(1)} %collective-permute-done.11.refs_2_.refs_13_) | copy-start | bytes 1179652
  162.0 3.6 %collective-permute-start.12 = (bf16[2,128,1024]{2,1,0:T(8,128)(2,1)S(1)}, bf16[2,128,1024]{2,1,0:T(8,128)(2,1)S(1)}, u32[]{:S(2)}, u32[]{:S(2)}) collective-permute-start(bf16[2,128,1024]{2,1,0:T(8,128)(2,1)S(1)} %get-tuple-element.45), channel_id=1, source_target_pairs={{0,16},{16,0},{1,17},{17,1},{2,18},{18,2},{3,19},{19,3},{4,20},{20... | collective-permute-start | bytes 1572872 | tf_op jit(solution)/shard_map/ppermute | solution.py:20
  162.3 18.5 %collective-permute-start.29 = (bf16[2,128,1024]{2,1,0:T(8,128)(2,1)S(1)}, bf16[2,128,1024]{2,1,0:T(8,128)(2,1)S(1)}, u32[]{:S(2)}, u32[]{:S(2)}) collective-permute-start(bf16[2,128,1024]{2,1,0:T(8,128)(2,1)S(1)} %add_convert_fusion), channel_id=1, source_target_pairs={{0,12},{4,8},{8,4},{12,0},{1,13},{5,9},{9,5},{13,1},{2,14},{6,10},... | collective-permute-start | bytes 1572872 | tf_op jit(solution)/shard_map/ppermute | solution.py:20
  164.3 24.5 %collective-permute-start.21 = (bf16[2,128,1024]{2,1,0:T(8,128)(2,1)S(1)}, bf16[2,128,1024]{2,1,0:T(8,128)(2,1)S(1)}, u32[]{:S(2)}, u32[]{:S(2)}) collective-permute-start(bf16[2,128,1024]{2,1,0:T(8,128)(2,1)S(1)} %add_convert_fusion.1), channel_id=1, source_target_pairs={{0,8},{4,12},{8,0},{12,4},{1,9},{5,13},{9,1},{13,5},{2,10},{6,14},... | collective-permute-start | bytes 1572872 | tf_op jit(solution)/shard_map/ppermute | solution.py:20
  165.8 23.1 %collective-permute-start.13 = (bf16[2,128,1024]{2,1,0:T(8,128)(2,1)S(1)}, bf16[2,128,1024]{2,1,0:T(8,128)(2,1)S(1)}, u32[]{:S(2)}, u32[]{:S(2)}) collective-permute-start(bf16[2,128,1024]{2,1,0:T(8,128)(2,1)S(1)} %add_convert_fusion.2), channel_id=1, source_target_pairs={{0,4},{4,0},{8,12},{12,8},{1,5},{5,1},{9,13},{13,9},{2,6},{6,2},{1... | collective-permute-start | bytes 1572872 | tf_op jit(solution)/shard_map/ppermute | solution.py:20

commit v3 on v1

v3 whole, which is shorter than its diff:
```python
import functools

import jax
import jax.numpy as jnp
from jax import lax
from jax.experimental import pallas as pl
from jax.experimental.pallas import tpu as pltpu
from jax.sharding import PartitionSpec as P

BF16 = jnp.bfloat16
F32 = jnp.float32
MIB = 1 << 20
NT = (((1,), (1,)), ((), ()))
TN = (((0,), (0,)), ((), ()))
LOCAL = pl.BlockSpec(memory_space=pltpu.VMEM)
SCALAR = pl.BlockSpec(memory_space=pltpu.SMEM)
ANY = pl.BlockSpec(memory_space=pl.ANY)


def shaped(*dims, dtype=BF16):
    return jax.ShapeDtypeStruct(dims, dtype)


class Line:
    def __init__(self):
        self.last = None

    def call(self, name, kernel, operands, in_specs, out_specs, out_shape, limit=16, **rest):
        if self.last is not None:
            count, inner = len(operands), kernel
            operands, in_specs = [*operands, self.last], [*in_specs, ANY]

            def kernel(*refs):
                inner(*refs[:count], *refs[count + 1 :])

        result = pl.pallas_call(
            kernel,
            in_specs=in_specs,
            out_specs=out_specs,
            out_shape=out_shape,
            compiler_params=pltpu.CompilerParams(vmem_limit_bytes=limit * MIB),
            cost_estimate=pl.CostEstimate(flops=1000, bytes_accessed=1000, transcendentals=0),
            name=name,
            **rest,
        )(*operands)
        self.last = result[0] if isinstance(result, (list, tuple)) else result
        return result


def swap(value, axis, size, mask):
    return lax.ppermute(value, axis, [(i, i ^ mask) for i in range(size)])


def ordered_rows(line, tokens, out_grad, flip, pieces):
    rows, width = tokens.shape
    piece = rows // pieces

    def kernel(flip_ref, a_ref, b_ref, o_ref, sems):
        copies = []
        for index, ref in enumerate((a_ref, b_ref)):
            for at in range(pieces):
                source = pl.ds(pl.multiple_of((at ^ flip_ref[0]) * piece, piece), piece)
                target = o_ref.at[index, at * piece : (at + 1) * piece]
                copies.append(
                    pltpu.make_async_copy(ref.at[source], target, sems.at[index * pieces + at])
                )
        for copy in copies:
            copy.start()
        for copy in copies:
            copy.wait()

    return line.call(
        "ordered_rows",
        kernel,
        [flip, tokens, out_grad],
        [SCALAR, ANY, ANY],
        LOCAL,
        shaped(2, rows, width),
        limit=52,
        scratch_shapes=[pltpu.SemaphoreType.DMA((2 * pieces,))],
    )


def pass_on(line, value):
    def kernel(a_ref, o_ref):
        pass

    return line.call(
        "pass_on",
        kernel,
        [value],
        [ANY],
        ANY,
        shaped(*value.shape),
        limit=1,
        input_output_aliases={0: 0},
    )


def forward_products(line, core, own, other, low, rows, piece, weights):
    width = own.shape[2]
    units = weights[0].shape[1]
    tile = min(256, units)

    def kernel(core_ref, own_ref, other_ref, gate_ref, up_ref, down_ref, last_ref, first_ref):
        here = pl.ds(pl.multiple_of(core_ref[0] * width, width), width)
        there = pl.ds(pl.multiple_of((1 - core_ref[0]) * width, width), width)

        @pl.loop(0, units // tile)
        def _(step):
            columns = pl.ds(pl.multiple_of(step * tile, tile), tile)
            for index, (which, weight) in enumerate(((0, gate_ref), (0, up_ref), (1, down_ref))):
                left = own_ref[which, low : low + rows]
                part = jnp.dot(left, weight[here, columns], preferred_element_type=F32)
                left = other_ref[which, low : low + rows]
                part += jnp.dot(left, weight[there, columns], preferred_element_type=F32)
                part = part.astype(BF16)
                for at in range(0, rows // piece, 2):
                    to = slice(at // 2 * piece, (at // 2 + 1) * piece)
                    last_ref[index, to, columns] = part[at * piece : (at + 1) * piece]
                    first_ref[index, to, columns] = part[(at + 1) * piece : (at + 2) * piece]

    return line.call(
        "forward_products",
        kernel,
        [core, own, other, *weights],
        [SCALAR] + [LOCAL] * 5,
        [LOCAL] * 2,
        [shaped(3, rows // 2, units)] * 2,
    )


def add_on(line, held, received):
    def kernel(a_ref, b_ref, o_ref):
        o_ref[...] = (a_ref[...].astype(F32) + b_ref[...].astype(F32)).astype(BF16)

    return line.call(
        "add_on", kernel, [held, received], [LOCAL] * 2, LOCAL, shaped(*held.shape), limit=4
    )


def activations(line, held, received):
    def kernel(a_ref, b_ref, o_ref):
        gate, up, grad = [a_ref[i].astype(F32) + b_ref[i].astype(F32) for i in range(3)]
        sigmoid = jax.nn.sigmoid(gate)
        active = gate * sigmoid
        o_ref[0] = (active * up).astype(BF16)
        o_ref[1] = (grad * up * sigmoid * (1.0 + gate * (1.0 - sigmoid))).astype(BF16)
        o_ref[2] = (grad * active).astype(BF16)

    return line.call(
        "activations", kernel, [held, received], [LOCAL] * 2, LOCAL, shaped(*held.shape), limit=4
    )


def backward_products(line, core, place, passed, piece, weights):
    count = len(passed)
    _, half, units = passed[0].shape
    rows = 2 * half
    width = weights[0].shape[0] // 2

    def kernel(core_ref, place_ref, *refs):
        passed_refs = refs[:count]
        gate_ref, up_ref, down_ref, keep_ref, send_ref, acts_ref = refs[count:]
        near = jnp.minimum(place_ref[0], count - 1 - place_ref[0])
        for index, ref in enumerate(passed_refs):
            far = index >= count // 2

            @pl.when(near == (count - 1 - index if far else index))
            def _(ref=ref, far=far):
                for at in range(half // piece):
                    to = (2 * at + far) * piece
                    acts_ref[:, to : to + piece] = ref[:, at * piece : (at + 1) * piece]

        def fill(target, side):
            lines = pl.ds(pl.multiple_of(side * width, width), width)
            out = lax.dot_general(down_ref[lines], acts_ref[0], NT, preferred_element_type=F32)
            grad = lax.dot_general(gate_ref[lines], acts_ref[1], NT, preferred_element_type=F32)
            grad += lax.dot_general(up_ref[lines], acts_ref[2], NT, preferred_element_type=F32)
            target[0] = out.astype(BF16).T
            target[1] = grad.astype(BF16).T

        fill(send_ref, 1 - core_ref[0])
        fill(keep_ref, core_ref[0])

    return line.call(
        "backward_products",
        kernel,
        [core, place, *passed, *weights],
        [SCALAR] * 2 + [LOCAL] * (count + 3),
        [LOCAL] * 3,
        [shaped(2, rows, width)] * 2 + [shaped(3, rows, units)],
    )


def weight_grads(line, core, owns, others, acts, spans):
    count, chunks = len(owns), len(acts)
    _, rows, width = owns[0].shape
    units = acts[0].shape[2]
    tile = min(256, width)
    steps = width // tile
    total = rows * count

    def kernel(core_ref, *refs):
        own_refs, other_refs = refs[:count], refs[count : 2 * count]
        act_refs = refs[2 * count : 2 * count + chunks]
        _, gate_out, up_out, down_out, all_acts, left, held, sems = refs[2 * count + chunks :]
        for ref, (low, high) in zip(act_refs, spans):
            all_acts[:, low:high] = ref[...]

        def copies(step, slot):
            side = jnp.where(step < steps, core_ref[0], 1 - core_ref[0])
            line_at = pl.multiple_of((side * steps + lax.rem(step, steps)) * tile, tile)
            return [
                pltpu.make_async_copy(
                    held.at[slot, index], out.at[pl.ds(line_at, tile)], sems.at[slot, index]
                )
                for index, out in enumerate((gate_out, up_out, down_out))
            ]

        @pl.loop(0, 2 * steps)
        def _(step):
            slot = lax.rem(step, 2)
            columns = pl.ds(pl.multiple_of(lax.rem(step, steps) * tile, tile), tile)

            @pl.when(step < steps)
            def _():
                for index, ref in enumerate(own_refs):
                    left[:, index * rows : (index + 1) * rows] = ref[:, :, columns]

            @pl.when(step >= steps)
            def _():
                for index, ref in enumerate(other_refs):
                    left[:, index * rows : (index + 1) * rows] = ref[:, :, columns]

            @pl.when(step >= 2)
            def _():
                for copy in copies(step - 2, slot):
                    copy.wait()

            for index, (which, act) in enumerate(((0, 1), (0, 2), (1, 0))):
                held[slot, index] = lax.dot_general(
                    left[which], all_acts[act], TN, preferred_element_type=F32
                )
            for copy in copies(step, slot):
                copy.start()

        for step in (2 * steps - 2, 2 * steps - 1):
            for copy in copies(step, step % 2):
                copy.wait()

    return line.call(
        "weight_grads",
        kernel,
        [core, *owns, *others, *acts],
        [SCALAR] + [LOCAL] * (2 * count + chunks),
        [ANY] * 4,
        [shaped(16, 128)] + [shaped(2 * width, units, dtype=F32)] * 3,
        limit=24,
        scratch_shapes=[
            pltpu.VMEM((3, total, units), BF16),
            pltpu.VMEM((2, total, tile), BF16),
            pltpu.VMEM((2, 3, tile, units), F32),
            pltpu.SemaphoreType.DMA((2, 3)),
        ],
    )


def final_sum(line, parts, flip, piece):
    rows = sum(part.shape[1] for part in parts[0])
    width = parts[0][0].shape[2]
    flat = [part for block in parts for part in block]

    def kernel(flip_ref, *refs):
        outs = refs[len(flat) :]
        at = 0
        sources = []
        for block in parts:
            spans = []
            for part in block:
                for low in range(0, part.shape[1], piece):
                    spans.append((refs[at], low))
                at += 1
            sources.append(spans)
        for place in range(rows // piece):
            to = pl.ds(pl.multiple_of((place ^ flip_ref[0]) * piece, piece), piece)
            for index, out_ref in enumerate(outs):
                total = 0.0
                for spans in sources:
                    ref, low = spans[place]
                    total += ref[index, low : low + piece].astype(F32)
                out_ref[to] = total.astype(BF16)

    return line.call(
        "final_sum",
        kernel,
        [flip, *flat],
        [SCALAR] + [LOCAL] * len(flat),
        [LOCAL] * 2,
        [shaped(rows, width)] * 2,
    )


WEIGHTS = -1
FOUR = (2, 1, 2, 0, 1, 3, 2, 3, 1, 2, 3, 1, 2, 0, 3, 1, 2, 0, 3, 1, 2, 0, 3, 1, 2, 0, 3, 1, 2, 0, 3, 1, 2, 0, 3, WEIGHTS, 1, 0, 3)


def plan_of(n_gy, n_gz, pieces):
    chunks = [(d, 0, pieces) for d in range(n_gy)]
    if (n_gy, n_gz) == (4, 4):
        return chunks, FOUR
    events = []
    for at, (d, _, _) in enumerate(chunks):
        for k in range(-1 if d else 0, 2 * n_gz + (1 if d else 0)):
            events.append((at + 2 * k, at))
    return chunks, [at for _, at in sorted(events)] + [WEIGHTS]


def per_device(sizes, tokens, gate_weight, up_weight, down_weight, out_grad):
    n_gy, n_gz = sizes["gy"], sizes["gz"]
    pieces = 4
    piece = tokens.shape[0] // pieces
    core = lax.axis_index("gx").astype(jnp.int32).reshape(1)
    level = lax.axis_index("gz").astype(jnp.int32)
    place = level.reshape(1)
    flip = (level >= n_gz // 2).astype(jnp.int32).reshape(1)
    swap_core = functools.partial(swap, axis="gx", size=2, mask=1)
    line = Line()

    def hop(value, step):
        pairs = [(step, step + 1), (n_gz - 1 - step, n_gz - 2 - step)]
        return lax.ppermute(value, "gz", pairs)

    mine = ordered_rows(line, tokens, out_grad, flip, pieces)
    others = [swap_core(mine)] + [None] * (n_gy - 1)
    owns = {0: mine}

    def send_blocks(d):
        step = 1 << d.bit_length()
        while step < n_gy:
            owns[d | step] = swap(owns[d], "gy", n_gy, step)
            step <<= 1

    send_blocks(0)
    weights = (gate_weight, up_weight, down_weight)
    acts = {}

    def chunk(at, d, first_piece, count):
        if others[d] is None:
            yield
            owns[d] = pass_on(line, owns[d])
            others[d] = swap_core(owns[d])
            send_blocks(d)
        yield
        last, first = forward_products(
            line, core, owns[d], others[d], first_piece * piece, count * piece, piece, weights
        )
        value = first
        for step in range(n_gz - 1):
            got = hop(value, step)
            yield
            if step < n_gz - 2:
                value = add_on(line, first if step + 1 < n_gz // 2 else last, got)
        value = activations(line, last, got)
        passed = [value]
        for step in range(n_gz - 1):
            value = hop(value, step)
            yield
            if step < n_gz - 2:
                value = pass_on(line, value)
            passed.append(value)
        keep, send, acts[at] = backward_products(line, core, place, passed, piece, weights)
        got = swap_core(send)
        yield
        part = add_on(line, keep, got)
        if d:
            part = swap(part, "gy", n_gy, d)
            yield
            part = pass_on(line, part)
        parts[d].append(part)
        yield

    plan, order = plan_of(n_gy, n_gz, pieces)
    spans = []
    for d, first_piece, count in plan:
        low = (d * pieces + first_piece) * piece
        spans.append((low, low + count * piece))
    parts = [[] for _ in range(n_gy)]
    runs = [chunk(at, *entry) for at, entry in enumerate(plan)]
    for run in runs:
        next(run)
    for at in order:
        if at == WEIGHTS:
            every = [acts[i] for i in range(len(plan))]
            grads = weight_grads(
                line, core, [owns[d] for d in range(n_gy)], others, every, spans
            )
        else:
            next(runs[at])
    output, tokens_grad = final_sum(line, parts, flip, piece)
    _, gate_grad_w, up_grad_w, down_grad_w = grads
    return (output, tokens_grad, gate_grad_w, up_grad_w, down_grad_w)


def solution(mesh):
    return jax.shard_map(
        functools.partial(per_device, dict(mesh.shape)),
        mesh=mesh,
        in_specs=(
            P("gy", ("gz", "gx")),
            P("gz", ("gx", "gy")),
            P("gz", ("gx", "gy")),
            P("gz", ("gx", "gy")),
            P("gy", ("gz", "gx")),
        ),
        out_specs=(
            P("gy", ("gz", "gx")),
            P("gy", ("gz", "gx")),
            P("gz", ("gx", "gy")),
            P("gz", ("gx", "gy")),
            P("gz", ("gx", "gy")),
        ),
        check_vma=False,
    )
```

time: 355 us -> 164 us (0.46)
  waiting for transfers between devices: 253 us -> 52.6 us
  starting transfers between devices: 0.69 us -> 57.9 us
  matrix products: 53.2 us -> 0 us
  Pallas kernels: 0 us -> 42.9 us
  local copies, waits for them, and re-layouts: 28 us -> 8.47 us
  between operations: 14 us -> 1.3 us
  other arithmetic: 4.77 us -> 0 us
    all_gather x7 -> x0, waiting for transfers between devices: 146 us -> none  [the longest x2 58.9 us: gather_rows(): rows = lax.all_gather(block, 'gy', axis=0, tiled=True)]
    reduce_scatter x6 -> x0, waiting for transfers between devices: 105 us -> none  [the longest x1 41.6 us: per_device(): lax.psum_scatter(gate_up, 'gz', scatter_dimension=0, tiled=True)]
    ppermute x0 -> x38, starting transfers between devices: none -> 57.9 us  [the longest x24 46.2 us: hop(): return lax.ppermute(value, 'gz', pairs)]
    dot_general x9 -> x0, matrix products: 53.2 us -> none  [the longest x3 20.6 us: dot_last(): lax.dot_general(left, right, (((1,), (1,)), ((), ())), preferred_element_...]
    ppermute x0 -> x38, waiting for transfers between devices: none -> 52.6 us  [the longest x24 37.5 us: hop(): return lax.ppermute(value, 'gz', pairs)]
    pallas_call x0 -> x41, Pallas kernels: none -> 42.9 us  [call(): pl.pallas_call(kernel, in_specs=in_specs, out_specs=out_specs, out_shape=...]
    unnamed x13 -> x16, local copies, waits for them, and re-layouts: 28 us -> 8.47 us
  transfers between devices with their start and end apart: 13 -> 38, of which waited for: 12 -> 15; matrix products, arithmetic and copies ran while one was open for 24% -> 0% of each run, Pallas kernels for 0% -> 25%
where the time goes in v3:
time: 164 us; the launch traced here: 163 us
  starting transfers between devices  57.9 us (35%)
  waiting for transfers between devices  52.6 us (32%)
  Pallas kernels  42.9 us (26%)
  local copies, waits for them, and re-layouts  8.47 us (5%)
    ppermute x24, starting transfers between devices, hop(): return lax.ppermute(value, 'gz', pairs)  46.2 us
    pallas_call x41, Pallas kernels, call(): pl.pallas_call(kernel, in_specs=in_specs, out_specs=out_specs, out_shape=...  42.9 us
    ppermute x24, waiting for transfers between devices, hop(): return lax.ppermute(value, 'gz', pairs)  37.5 us
    ppermute x14, waiting for transfers between devices, swap(): return lax.ppermute(value, axis, [(i, i ^ mask) for i in range(size)])  15.1 us
    ppermute x14, starting transfers between devices, swap(): return lax.ppermute(value, axis, [(i, i ^ mask) for i in range(size)])  11.7 us
    unnamed x16, local copies, waits for them, and re-layouts  8.47 us
  transfers between devices with their start and end apart: 38, of which 15 were waited for; matrix products, arithmetic and copies ran while one was open for 0% of the time, Pallas kernels for 25%

profile of v3, /device:TPU:0, one launch (start us, length us, event | category | flops | bytes accessed | tf_op | source)
XLA Modules:
  0.0 163.2 jit_solution(18270210612802286826)
XLA Ops:
  0.6 0.9 copy-done.6
  1.6 0.9 copy-done.7
  2.5 0.7 ordered_rows.1.refs_1_
  3.3 3.0 %collective-permute-start.1 = (bf16[2,128,1024]{2,1,0:T(8,128)(2,1)S(1)}, bf16[2,128,1024]{2,1,0:T(8,128)(2,1)S(1)}, u32[]{:S(2)}, u32[]{:S(2)}) collective-permute-start(bf16[2,128,1024]{2,1,0:T(8,128)(2,1)S(1)} %ordered_rows.1.refs_1_), channel_id=1, source_target_pairs={{0,8},{4,12},{8,0},{12,4},{1,9},{5,13},{9,1},{13,5},{2,10},{6,14},... | collective-permute-start | bytes 1572872 | tf_op jit(solution)/shard_map/ppermute | solution.py:51
  6.3 1.5 collective-permute-start.3
  7.8 10.4 %collective-permute-done.1.refs_0_ = bf16[2,128,1024]{2,1,0:T(8,128)(2,1)S(1)} collective-permute-done((bf16[2,128,1024]{2,1,0:T(8,128)(2,1)S(1)}, bf16[2,128,1024]{2,1,0:T(8,128)(2,1)S(1)}, u32[]{:S(2)}, u32[]{:S(2)}) %collective-permute-start.1) | collective-permute-done | bytes 524320 | tf_op jit(solution)/shard_map/ppermute | solution.py:51
  18.2 0.5 collective-permute-start
  18.7 0.9 collective-permute-done.3.refs_0_
  19.7 0.8 collective-permute-start.6
  20.5 2.2 %copy-done = bf16[2048,1024]{1,0:T(8,128)(2,1)S(1)} copy-done((bf16[2048,1024]{1,0:T(8,128)(2,1)S(1)}, bf16[2048,1024]{1,0:T(8,128)(2,1)}, u32[]{:S(2)}) %copy-start) | copy-done | bytes 4194328
  22.7 2.2 %copy-done.2 = bf16[2048,1024]{1,0:T(8,128)(2,1)S(1)} copy-done((bf16[2048,1024]{1,0:T(8,128)(2,1)S(1)}, bf16[2048,1024]{1,0:T(8,128)(2,1)}, u32[]{:S(2)}) %copy-start.2) | copy-done | bytes 4194328
  24.9 2.2 %copy-done.4 = bf16[2048,1024]{1,0:T(8,128)(2,1)S(1)} copy-done((bf16[2048,1024]{1,0:T(8,128)(2,1)S(1)}, bf16[2048,1024]{1,0:T(8,128)(2,1)}, u32[]{:S(2)}) %copy-start.4) | copy-done | bytes 4194328
  27.1 2.7 %forward_products.4 = (bf16[3,64,1024]{2,1,0:T(8,128)(2,1)S(1)}, bf16[3,64,1024]{2,1,0:T(8,128)(2,1)S(1)}) custom-call(s32[1]{0:T(128)} %bitcast.1.refs_0_, bf16[2,128,1024]{2,1,0:T(8,128)(2,1)S(1)} %pass_on.14.refs_1_.refs_3_, bf16[2,128,1024]{2,1,0:T(8,128)(2,1)S(1)} %collective-permute-done.2.refs_2_.refs_7_, bf16[2048,1024]{1,0:T(8,128)(2,1)S(1)} %copy-done, ...), custom_call_target="tpu_custom_call" | custom-call | flops 1000 | bytes 1000 | tf_op jit(solution)/shard_map/forward_products/pallas_call | solution.py:36
  29.8 3.8 %collective-permute-start.5 = (bf16[3,64,1024]{2,1,0:T(8,128)(2,1)S(1)}, bf16[3,64,1024]{2,1,0:T(8,128)(2,1)S(1)}, u32[]{:S(2)}, u32[]{:S(2)}) collective-permute-start(bf16[3,64,1024]{2,1,0:T(8,128)(2,1)S(1)} %get-tuple-element.34.refs_0_), channel_id=1, source_target_pairs={{0,1},{3,2},{4,5},{7,6},{8,9},{11,10},{12,13},{15,14},{16,17},{19,... | collective-permute-start | bytes 1179656 | tf_op jit(solution)/shard_map/ppermute | solution.py:332
  33.6 2.7 %forward_products.5 = (bf16[3,64,1024]{2,1,0:T(8,128)(2,1)S(1)}, bf16[3,64,1024]{2,1,0:T(8,128)(2,1)S(1)}) custom-call(s32[1]{0:T(128)} %bitcast.1.refs_0_, bf16[2,128,1024]{2,1,0:T(8,128)(2,1)S(1)} %ordered_rows.1.refs_1_, bf16[2,128,1024]{2,1,0:T(8,128)(2,1)S(1)} %collective-permute-done.refs_2_.refs_5_, bf16[2048,1024]{1,0:T(8,128)(2,1)S(1)} %copy-done.1, ...), custom_call_target="tpu_custom_call" | custom-call | flops 1000 | bytes 1000 | tf_op jit(solution)/shard_map/forward_products/pallas_call | solution.py:36
  36.3 3.7 %forward_products.6 = (bf16[3,64,1024]{2,1,0:T(8,128)(2,1)S(1)}, bf16[3,64,1024]{2,1,0:T(8,128)(2,1)S(1)}) custom-call(s32[1]{0:T(128)} %bitcast.1.refs_0_, bf16[2,128,1024]{2,1,0:T(8,128)(2,1)S(1)} %pass_on.15.refs_6_.refs_1_.refs_2_, bf16[2,128,1024]{2,1,0:T(8,128)(2,1)} %collective-permute-done.7.refs_2_.refs_6_, bf16[2048,1024]{1,0:T(8,128)(2,1)S(1)} %copy-done.1, ...), custom_call_target="tpu_custom_call" | custom-call | flops 1000 | bytes 1000 | tf_op jit(solution)/shard_map/forward_products/pallas_call | solution.py:36
  40.1 1.8 %collective-permute-start.9 = (bf16[3,64,1024]{2,1,0:T(8,128)(2,1)S(1)}, bf16[3,64,1024]{2,1,0:T(8,128)(2,1)S(1)}, u32[]{:S(2)}, u32[]{:S(2)}) collective-permute-start(bf16[3,64,1024]{2,1,0:T(8,128)(2,1)S(1)} %get-tuple-element.36.refs_0_), channel_id=1, source_target_pairs={{0,1},{3,2},{4,5},{7,6},{8,9},{11,10},{12,13},{15,14},{16,17},{19,... | collective-permute-start | bytes 1179656 | tf_op jit(solution)/shard_map/ppermute | solution.py:332
  41.9 0.4 collective-permute-done.5.refs_1_
  42.4 0.7 collective-permute-start.8
  43.1 2.7 %forward_products.7 = (bf16[3,64,1024]{2,1,0:T(8,128)(2,1)S(1)}, bf16[3,64,1024]{2,1,0:T(8,128)(2,1)S(1)}) custom-call(s32[1]{0:T(128)} %bitcast.1.refs_0_, bf16[2,128,1024]{2,1,0:T(8,128)(2,1)S(1)} %pass_on.16.refs_2_.refs_1_.refs_4_, bf16[2,128,1024]{2,1,0:T(8,128)(2,1)S(1)} %collective-permute-done.10.refs_2_.refs_8_, bf16[2048,1024]{1,0:T(8,128)(2,1)S(1)} %copy-done.1, ...), custom_call_target="tpu_custom_call" | custom-call | flops 1000 | bytes 1000 | tf_op jit(solution)/shard_map/forward_products/pallas_call | solution.py:36
  45.8 7.2 %collective-permute-start.13 = (bf16[3,64,1024]{2,1,0:T(8,128)(2,1)S(1)}, bf16[3,64,1024]{2,1,0:T(8,128)(2,1)S(1)}, u32[]{:S(2)}, u32[]{:S(2)}) collective-permute-start(bf16[3,64,1024]{2,1,0:T(8,128)(2,1)S(1)} %get-tuple-element.38.refs_0_), channel_id=1, source_target_pairs={{0,1},{3,2},{4,5},{7,6},{8,9},{11,10},{12,13},{15,14},{16,17},{19,... | collective-permute-start | bytes 1179656 | tf_op jit(solution)/shard_map/ppermute | solution.py:332
  53.1 0.7 collective-permute-start.12
  53.9 1.3 collective-permute-start.11
  55.2 5.3 %collective-permute-start.4 = (bf16[3,64,1024]{2,1,0:T(8,128)(2,1)S(1)}, bf16[3,64,1024]{2,1,0:T(8,128)(2,1)S(1)}, u32[]{:S(2)}, u32[]{:S(2)}) collective-permute-start(bf16[3,64,1024]{2,1,0:T(8,128)(2,1)S(1)} %get-tuple-element.33.refs_0_), channel_id=1, source_target_pairs={{0,1},{3,2},{4,5},{7,6},{8,9},{11,10},{12,13},{15,14},{16,17},{19,... | collective-permute-start | bytes 1179656 | tf_op jit(solution)/shard_map/ppermute | solution.py:332
  60.6 1.2 collective-permute-done.13.refs_1_
  61.9 0.7 collective-permute-start.17
  62.7 1.3 collective-permute-start.16
  64.0 2.8 %collective-permute-done.11.refs_1_ = bf16[3,64,1024]{2,1,0:T(8,128)(2,1)S(1)} collective-permute-done((bf16[3,64,1024]{2,1,0:T(8,128)(2,1)S(1)}, bf16[3,64,1024]{2,1,0:T(8,128)(2,1)S(1)}, u32[]{:S(2)}, u32[]{:S(2)}) %collective-permute-start.11) | collective-permute-done | bytes 393248 | tf_op jit(solution)/shard_map/ppermute | solution.py:332
  66.8 0.2 activations.4.refs_2_
  67.0 2.9 %collective-permute-start.15 = (bf16[3,64,1024]{2,1,0:T(8,128)(2,1)S(1)}, bf16[3,64,1024]{2,1,0:T(8,128)(2,1)S(1)}, u32[]{:S(2)}, u32[]{:S(2)}) collective-permute-start(bf16[3,64,1024]{2,1,0:T(8,128)(2,1)S(1)} %activations.4.refs_2_), channel_id=1, source_target_pairs={{0,1},{3,2},{4,5},{7,6},{8,9},{11,10},{12,13},{15,14},{16,17},{19,... | collective-permute-start | bytes 1179656 | tf_op jit(solution)/shard_map/ppermute | solution.py:332
  69.9 0.3 collective-permute-done.4.refs_1_
  70.3 0.7 collective-permute-start.14
  71.1 1.3 collective-permute-start.21
  72.4 2.9 %collective-permute-done.16.refs_1_ = bf16[3,64,1024]{2,1,0:T(8,128)(2,1)S(1)} collective-permute-done((bf16[3,64,1024]{2,1,0:T(8,128)(2,1)S(1)}, bf16[3,64,1024]{2,1,0:T(8,128)(2,1)S(1)}, u32[]{:S(2)}, u32[]{:S(2)}) %collective-permute-start.16) | collective-permute-done | bytes 393248 | tf_op jit(solution)/shard_map/ppermute | solution.py:332
  75.3 0.2 activations.5.refs_1_.refs_2_
  75.5 2.8 %collective-permute-start.20 = (bf16[3,64,1024]{2,1,0:T(8,128)(2,1)S(1)}, bf16[3,64,1024]{2,1,0:T(8,128)(2,1)S(1)}, u32[]{:S(2)}, u32[]{:S(2)}) collective-permute-start(bf16[3,64,1024]{2,1,0:T(8,128)(2,1)S(1)} %activations.5.refs_1_.refs_2_), channel_id=1, source_target_pairs={{0,1},{3,2},{4,5},{7,6},{8,9},{11,10},{12,13},{15,14},{16,17},{19,... | collective-permute-start | bytes 1179656 | tf_op jit(solution)/shard_map/ppermute | solution.py:332
  78.3 0.4 collective-permute-done.15.refs_0_
  78.7 0.7 collective-permute-start.19
  79.5 1.3 collective-permute-start.18
  80.8 3.5 %collective-permute-done.21.refs_1_ = bf16[3,64,1024]{2,1,0:T(8,128)(2,1)S(1)} collective-permute-done((bf16[3,64,1024]{2,1,0:T(8,128)(2,1)S(1)}, bf16[3,64,1024]{2,1,0:T(8,128)(2,1)S(1)}, u32[]{:S(2)}, u32[]{:S(2)}) %collective-permute-start.21) | collective-permute-done | bytes 393248 | tf_op jit(solution)/shard_map/ppermute | solution.py:332
  84.5 3.4 %collective-permute-start.25 = (bf16[3,64,1024]{2,1,0:T(8,128)(2,1)S(1)}, bf16[3,64,1024]{2,1,0:T(8,128)(2,1)S(1)}, u32[]{:S(2)}, u32[]{:S(2)}) collective-permute-start(bf16[3,64,1024]{2,1,0:T(8,128)(2,1)S(1)} %activations.6.refs_1_.refs_2_), channel_id=1, source_target_pairs={{0,1},{3,2},{4,5},{7,6},{8,9},{11,10},{12,13},{15,14},{16,17},{19,... | collective-permute-start | bytes 1179656 | tf_op jit(solution)/shard_map/ppermute | solution.py:332
  88.0 0.7 collective-permute-start.24
  88.7 1.3 collective-permute-start.23
  90.0 2.8 %collective-permute-done.18.refs_1_ = bf16[3,64,1024]{2,1,0:T(8,128)(2,1)S(1)} collective-permute-done((bf16[3,64,1024]{2,1,0:T(8,128)(2,1)S(1)}, bf16[3,64,1024]{2,1,0:T(8,128)(2,1)S(1)}, u32[]{:S(2)}, u32[]{:S(2)}) %collective-permute-start.18) | collective-permute-done | bytes 393248 | tf_op jit(solution)/shard_map/ppermute | solution.py:332
  93.0 3.2 %collective-permute-start.22 = (bf16[3,64,1024]{2,1,0:T(8,128)(2,1)S(1)}, bf16[3,64,1024]{2,1,0:T(8,128)(2,1)S(1)}, u32[]{:S(2)}, u32[]{:S(2)}) collective-permute-start(bf16[3,64,1024]{2,1,0:T(8,128)(2,1)S(1)} %activations.7.refs_1_.refs_2_), channel_id=1, source_target_pairs={{0,1},{3,2},{4,5},{7,6},{8,9},{11,10},{12,13},{15,14},{16,17},{19,... | collective-permute-start | bytes 1179656 | tf_op jit(solution)/shard_map/ppermute | solution.py:332
  96.3 0.7 collective-permute-start.29
  97.0 3.4 %collective-permute-done.23.refs_5_ = bf16[3,64,1024]{2,1,0:T(8,128)(2,1)S(1)} collective-permute-done((bf16[3,64,1024]{2,1,0:T(8,128)(2,1)S(1)}, bf16[3,64,1024]{2,1,0:T(8,128)(2,1)S(1)}, u32[]{:S(2)}, u32[]{:S(2)}) %collective-permute-start.23) | collective-permute-done | bytes 393248 | tf_op jit(solution)/shard_map/ppermute | solution.py:332
  100.4 3.5 %backward_products.4 = (bf16[2,128,1024]{2,1,0:T(8,128)(2,1)S(1)}, bf16[2,128,1024]{2,1,0:T(8,128)(2,1)S(1)}, bf16[3,128,1024]{2,1,0:T(8,128)(2,1)S(1)}) custom-call(s32[1]{0:T(128)} %bitcast.1.refs_0_, s32[1]{0:T(128)} %bitcast.2.refs_1_, bf16[3,64,1024]{2,1,0:T(8,128)(2,1)S(1)} %activations.4.refs_2_, bf16[3,64,1024]{2,1,0:T(8,128)(2,1)S(1)} %pass_on.17.refs_2_.refs_3_, ...), custom_call_target="tpu_custom_call" | custom-call | flops 1000 | bytes 1000 | tf_op jit(solution)/shard_map/backward_products/pallas_call | solution.py:36
  104.0 1.3 collective-permute-start.28
  105.3 0.7 collective-permute-start.26
  106.0 1.3 collective-permute-start.33
  107.3 10.5 %collective-permute-done.28.refs_5_ = bf16[3,64,1024]{2,1,0:T(8,128)(2,1)S(1)} collective-permute-done((bf16[3,64,1024]{2,1,0:T(8,128)(2,1)S(1)}, bf16[3,64,1024]{2,1,0:T(8,128)(2,1)S(1)}, u32[]{:S(2)}, u32[]{:S(2)}) %collective-permute-start.28) | collective-permute-done | bytes 393248 | tf_op jit(solution)/shard_map/ppermute | solution.py:332
  117.8 3.7 %backward_products.5 = (bf16[2,128,1024]{2,1,0:T(8,128)(2,1)S(1)}, bf16[2,128,1024]{2,1,0:T(8,128)(2,1)S(1)}, bf16[3,128,1024]{2,1,0:T(8,128)(2,1)S(1)}) custom-call(s32[1]{0:T(128)} %bitcast.1.refs_0_, s32[1]{0:T(128)} %bitcast.2.refs_1_, bf16[3,64,1024]{2,1,0:T(8,128)(2,1)S(1)} %activations.5.refs_1_.refs_2_, ...), custom_call_target="tpu_custom_call" | custom-call | flops 1000 | bytes 1000 | tf_op jit(solution)/shard_map/backward_products/pallas_call | solution.py:36
  121.7 1.5 collective-permute-start.31
  123.3 2.5 %collective-permute-done.33.refs_5_ = bf16[3,64,1024]{2,1,0:T(8,128)(2,1)S(1)} collective-permute-done((bf16[3,64,1024]{2,1,0:T(8,128)(2,1)S(1)}, bf16[3,64,1024]{2,1,0:T(8,128)(2,1)S(1)}, u32[]{:S(2)}, u32[]{:S(2)}) %collective-permute-start.33) | collective-permute-done | bytes 393248 | tf_op jit(solution)/shard_map/ppermute | solution.py:332
  125.8 3.5 %backward_products.6 = (bf16[2,128,1024]{2,1,0:T(8,128)(2,1)S(1)}, bf16[2,128,1024]{2,1,0:T(8,128)(2,1)S(1)}, bf16[3,128,1024]{2,1,0:T(8,128)(2,1)S(1)}) custom-call(s32[1]{0:T(128)} %bitcast.1.refs_0_, s32[1]{0:T(128)} %bitcast.2.refs_1_, bf16[3,64,1024]{2,1,0:T(8,128)(2,1)S(1)} %activations.6.refs_1_.refs_2_, ...), custom_call_target="tpu_custom_call" | custom-call | flops 1000 | bytes 1000 | tf_op jit(solution)/shard_map/backward_products/pallas_call | solution.py:36
  129.4 1.3 collective-permute-start.30
  130.9 1.6 collective-permute-start.35
  132.4 3.7 %collective-permute-done.31.refs_0_ = bf16[2,128,1024]{2,1,0:T(8,128)(2,1)S(1)} collective-permute-done((bf16[2,128,1024]{2,1,0:T(8,128)(2,1)S(1)}, bf16[2,128,1024]{2,1,0:T(8,128)(2,1)S(1)}, u32[]{:S(2)}, u32[]{:S(2)}) %collective-permute-start.31) | collective-permute-done | bytes 524320 | tf_op jit(solution)/shard_map/ppermute | solution.py:51
  136.1 6.7 %collective-permute-done.30.refs_5_ = bf16[3,64,1024]{2,1,0:T(8,128)(2,1)S(1)} collective-permute-done((bf16[3,64,1024]{2,1,0:T(8,128)(2,1)S(1)}, bf16[3,64,1024]{2,1,0:T(8,128)(2,1)S(1)}, u32[]{:S(2)}, u32[]{:S(2)}) %collective-permute-start.30) | collective-permute-done | bytes 393248 | tf_op jit(solution)/shard_map/ppermute | solution.py:332
  142.8 3.5 %backward_products.7 = (bf16[2,128,1024]{2,1,0:T(8,128)(2,1)S(1)}, bf16[2,128,1024]{2,1,0:T(8,128)(2,1)S(1)}, bf16[3,128,1024]{2,1,0:T(8,128)(2,1)S(1)}) custom-call(s32[1]{0:T(128)} %bitcast.1.refs_0_, s32[1]{0:T(128)} %bitcast.2.refs_1_, bf16[3,64,1024]{2,1,0:T(8,128)(2,1)S(1)} %activations.7.refs_1_.refs_2_, ...), custom_call_target="tpu_custom_call" | custom-call | flops 1000 | bytes 1000 | tf_op jit(solution)/shard_map/backward_products/pallas_call | solution.py:36
  146.6 2.4 %collective-permute-start.37 = (bf16[2,128,1024]{2,1,0:T(8,128)(2,1)S(1)}, bf16[2,128,1024]{2,1,0:T(8,128)(2,1)S(1)}, u32[]{:S(2)}, u32[]{:S(2)}) collective-permute-start(bf16[2,128,1024]{2,1,0:T(8,128)(2,1)S(1)} %add_on.22.refs_13_), channel_id=1, source_target_pairs={{0,12},{4,8},{8,4},{12,0},{1,13},{5,9},{9,5},{13,1},{2,14},{6,10},... | collective-permute-start | bytes 1572872 | tf_op jit(solution)/shard_map/ppermute | solution.py:51
  149.0 12.9 %weight_grads.1 = (bf16[16,128]{1,0:T(8,128)(2,1)S(1)}, f32[2048,1024]{1,0:T(8,128)}, f32[2048,1024]{1,0:T(8,128)}, f32[2048,1024]{1,0:T(8,128)}) custom-call(s32[1]{0:T(128)} %bitcast.1.refs_0_, bf16[2,128,1024]{2,1,0:T(8,128)(2,1)S(1)} %ordered_rows.1.refs_1_, bf16[2,128,1024]{2,1,0:T(8,128)(2,1)S(1)} %pass_on.15.refs_6_.refs_1_.refs_2_, ...), custom_call_target="tpu_custom_call" | custom-call | flops 1000 | bytes 1000 | tf_op jit(solution)/shard_map/weight_grads/pallas_call | solution.py:36
  162.2 1.0 final_sum.1
  (69 shorter events, 2.1 us)
Async XLA Ops:
  0.6 1.0 copy-start.6
  1.6 0.9 copy-start.7
  3.3 15.0 %collective-permute-start.1 = (bf16[2,128,1024]{2,1,0:T(8,128)(2,1)S(1)}, bf16[2,128,1024]{2,1,0:T(8,128)(2,1)S(1)}, u32[]{:S(2)}, u32[]{:S(2)}) collective-permute-start(bf16[2,128,1024]{2,1,0:T(8,128)(2,1)S(1)} %ordered_rows.1.refs_1_), channel_id=1, source_target_pairs={{0,8},{4,12},{8,0},{12,4},{1,9},{5,13},{9,1},{13,5},{2,10},{6,14},... | collective-permute-start | bytes 1572872 | tf_op jit(solution)/shard_map/ppermute | solution.py:51
  6.3 13.4 %collective-permute-start.3 = (bf16[2,128,1024]{2,1,0:T(8,128)(2,1)S(1)}, bf16[2,128,1024]{2,1,0:T(8,128)(2,1)S(1)}, u32[]{:S(2)}, u32[]{:S(2)}) collective-permute-start(bf16[2,128,1024]{2,1,0:T(8,128)(2,1)S(1)} %ordered_rows.1.refs_1_), channel_id=1, source_target_pairs={{0,4},{4,0},{8,12},{12,8},{1,5},{5,1},{9,13},{13,9},{2,6},{6,2},{1... | collective-permute-start | bytes 1572872 | tf_op jit(solution)/shard_map/ppermute | solution.py:51
  18.2 2.3 %collective-permute-start.2 = (bf16[2,128,1024]{2,1,0:T(8,128)(2,1)S(1)}, bf16[2,128,1024]{2,1,0:T(8,128)(2,1)S(1)}, u32[]{:S(2)}, u32[]{:S(2)}) collective-permute-start(bf16[2,128,1024]{2,1,0:T(8,128)(2,1)S(1)} %pass_on.14.refs_1_.refs_3_), channel_id=1, source_target_pairs={{0,16},{16,0},{1,17},{17,1},{2,18},{18,2},{3,19},{19,3},{4,20},{20... | collective-permute-start | bytes 1572872 | tf_op jit(solution)/shard_map/ppermute | solution.py:51
  18.2 15.3 %collective-permute-start = (bf16[2,128,1024]{2,1,0:T(8,128)(2,1)S(1)}, bf16[2,128,1024]{2,1,0:T(8,128)(2,1)S(1)}, u32[]{:S(2)}, u32[]{:S(2)}) collective-permute-start(bf16[2,128,1024]{2,1,0:T(8,128)(2,1)S(1)} %ordered_rows.1.refs_1_), channel_id=1, source_target_pairs={{0,16},{16,0},{1,17},{17,1},{2,18},{18,2},{3,19},{19,3},{4,20},{20... | collective-permute-start | bytes 1572872 | tf_op jit(solution)/shard_map/ppermute | solution.py:51
  19.7 16.6 %collective-permute-start.7 = (bf16[2,128,1024]{2,1,0:T(8,128)(2,1)S(1)}, bf16[2,128,1024]{2,1,0:T(8,128)(2,1)}, u32[]{:S(2)}, u32[]{:S(2)}) collective-permute-start(bf16[2,128,1024]{2,1,0:T(8,128)(2,1)S(1)} %pass_on.15.refs_6_.refs_1_.refs_2_), channel_id=1, source_target_pairs={{0,16},{16,0},{1,17},{17,1},{2,18},{18,2},{3,19},{19,3},{4,20},{20... | collective-permute-start | bytes 1572872 | tf_op jit(solution)/shard_map/ppermute | solution.py:51
  19.7 20.3 %collective-permute-start.6 = (bf16[2,128,1024]{2,1,0:T(8,128)(2,1)S(1)}, bf16[2,128,1024]{2,1,0:T(8,128)(2,1)S(1)}, u32[]{:S(2)}, u32[]{:S(2)}) collective-permute-start(bf16[2,128,1024]{2,1,0:T(8,128)(2,1)S(1)} %pass_on.15.refs_6_.refs_1_.refs_2_), channel_id=1, source_target_pairs={{0,8},{4,12},{8,0},{12,4},{1,9},{5,13},{9,1},{13,5},{2,10},{6,14},... | collective-permute-start | bytes 1572872 | tf_op jit(solution)/shard_map/ppermute | solution.py:51
  20.5 2.2 %copy-start = (bf16[2048,1024]{1,0:T(8,128)(2,1)S(1)}, bf16[2048,1024]{1,0:T(8,128)(2,1)}, u32[]{:S(2)}) copy-start(bf16[2048,1024]{1,0:T(8,128)(2,1)} %refs_6_.7) | copy-start | bytes 12582916
  22.7 2.2 %copy-start.2 = (bf16[2048,1024]{1,0:T(8,128)(2,1)S(1)}, bf16[2048,1024]{1,0:T(8,128)(2,1)}, u32[]{:S(2)}) copy-start(bf16[2048,1024]{1,0:T(8,128)(2,1)} %refs_7_.7) | copy-start | bytes 12582916
  24.9 2.2 %copy-start.4 = (bf16[2048,1024]{1,0:T(8,128)(2,1)S(1)}, bf16[2048,1024]{1,0:T(8,128)(2,1)}, u32[]{:S(2)}) copy-start(bf16[2048,1024]{1,0:T(8,128)(2,1)} %refs_8_.7) | copy-start | bytes 12582916
  27.1 6.5 %copy-start.1 = (bf16[2048,1024]{1,0:T(8,128)(2,1)S(1)}, bf16[2048,1024]{1,0:T(8,128)(2,1)}, u32[]{:S(2)}) copy-start(bf16[2048,1024]{1,0:T(8,128)(2,1)} %refs_6_.7) | copy-start | bytes 12582916
  27.1 6.5 %copy-start.3 = (bf16[2048,1024]{1,0:T(8,128)(2,1)S(1)}, bf16[2048,1024]{1,0:T(8,128)(2,1)}, u32[]{:S(2)}) copy-start(bf16[2048,1024]{1,0:T(8,128)(2,1)} %refs_7_.7) | copy-start | bytes 12582916
  27.1 6.5 %copy-start.5 = (bf16[2048,1024]{1,0:T(8,128)(2,1)S(1)}, bf16[2048,1024]{1,0:T(8,128)(2,1)}, u32[]{:S(2)}) copy-start(bf16[2048,1024]{1,0:T(8,128)(2,1)} %refs_8_.7) | copy-start | bytes 12582916
  29.8 12.5 %collective-permute-start.5 = (bf16[3,64,1024]{2,1,0:T(8,128)(2,1)S(1)}, bf16[3,64,1024]{2,1,0:T(8,128)(2,1)S(1)}, u32[]{:S(2)}, u32[]{:S(2)}) collective-permute-start(bf16[3,64,1024]{2,1,0:T(8,128)(2,1)S(1)} %get-tuple-element.34.refs_0_), channel_id=1, source_target_pairs={{0,1},{3,2},{4,5},{7,6},{8,9},{11,10},{12,13},{15,14},{16,17},{19,... | collective-permute-start | bytes 1179656 | tf_op jit(solution)/shard_map/ppermute | solution.py:332
  40.1 3.0 %collective-permute-start.10 = (bf16[2,128,1024]{2,1,0:T(8,128)(2,1)S(1)}, bf16[2,128,1024]{2,1,0:T(8,128)(2,1)S(1)}, u32[]{:S(2)}, u32[]{:S(2)}) collective-permute-start(bf16[2,128,1024]{2,1,0:T(8,128)(2,1)S(1)} %pass_on.16.refs_2_.refs_1_.refs_4_), channel_id=1, source_target_pairs={{0,16},{16,0},{1,17},{17,1},{2,18},{18,2},{3,19},{19,3},{4,20},{20... | collective-permute-start | bytes 1572872 | tf_op jit(solution)/shard_map/ppermute | solution.py:51
  40.1 12.9 %collective-permute-start.9 = (bf16[3,64,1024]{2,1,0:T(8,128)(2,1)S(1)}, bf16[3,64,1024]{2,1,0:T(8,128)(2,1)S(1)}, u32[]{:S(2)}, u32[]{:S(2)}) collective-permute-start(bf16[3,64,1024]{2,1,0:T(8,128)(2,1)S(1)} %get-tuple-element.36.refs_0_), channel_id=1, source_target_pairs={{0,1},{3,2},{4,5},{7,6},{8,9},{11,10},{12,13},{15,14},{16,17},{19,... | collective-permute-start | bytes 1179656 | tf_op jit(solution)/shard_map/ppermute | solution.py:332
  42.4 11.4 %collective-permute-start.8 = (bf16[3,64,1024]{2,1,0:T(8,128)(2,1)S(1)}, bf16[3,64,1024]{2,1,0:T(8,128)(2,1)S(1)}, u32[]{:S(2)}, u32[]{:S(2)}) collective-permute-start(bf16[3,64,1024]{2,1,0:T(8,128)(2,1)S(1)} %add_on.12.refs_6_), channel_id=1, source_target_pairs={{1,2},{2,1},{5,6},{6,5},{9,10},{10,9},{13,14},{14,13},{17,18},{18,... | collective-permute-start | bytes 1179656 | tf_op jit(solution)/shard_map/ppermute | solution.py:332
  45.8 16.0 %collective-permute-start.13 = (bf16[3,64,1024]{2,1,0:T(8,128)(2,1)S(1)}, bf16[3,64,1024]{2,1,0:T(8,128)(2,1)S(1)}, u32[]{:S(2)}, u32[]{:S(2)}) collective-permute-start(bf16[3,64,1024]{2,1,0:T(8,128)(2,1)S(1)} %get-tuple-element.38.refs_0_), channel_id=1, source_target_pairs={{0,1},{3,2},{4,5},{7,6},{8,9},{11,10},{12,13},{15,14},{16,17},{19,... | collective-permute-start | bytes 1179656 | tf_op jit(solution)/shard_map/ppermute | solution.py:332
  53.1 9.5 %collective-permute-start.12 = (bf16[3,64,1024]{2,1,0:T(8,128)(2,1)S(1)}, bf16[3,64,1024]{2,1,0:T(8,128)(2,1)S(1)}, u32[]{:S(2)}, u32[]{:S(2)}) collective-permute-start(bf16[3,64,1024]{2,1,0:T(8,128)(2,1)S(1)} %add_on.13.refs_2_), channel_id=1, source_target_pairs={{1,2},{2,1},{5,6},{6,5},{9,10},{10,9},{13,14},{14,13},{17,18},{18,... | collective-permute-start | bytes 1179656 | tf_op jit(solution)/shard_map/ppermute | solution.py:332
  53.9 12.8 %collective-permute-start.11 = (bf16[3,64,1024]{2,1,0:T(8,128)(2,1)S(1)}, bf16[3,64,1024]{2,1,0:T(8,128)(2,1)S(1)}, u32[]{:S(2)}, u32[]{:S(2)}) collective-permute-start(bf16[3,64,1024]{2,1,0:T(8,128)(2,1)S(1)} %add_on.14.refs_2_), channel_id=1, source_target_pairs={{2,3},{1,0},{6,7},{5,4},{10,11},{9,8},{14,15},{13,12},{18,19},{17,... | collective-permute-start | bytes 1179656 | tf_op jit(solution)/shard_map/ppermute | solution.py:332
  55.2 15.0 %collective-permute-start.4 = (bf16[3,64,1024]{2,1,0:T(8,128)(2,1)S(1)}, bf16[3,64,1024]{2,1,0:T(8,128)(2,1)S(1)}, u32[]{:S(2)}, u32[]{:S(2)}) collective-permute-start(bf16[3,64,1024]{2,1,0:T(8,128)(2,1)S(1)} %get-tuple-element.33.refs_0_), channel_id=1, source_target_pairs={{0,1},{3,2},{4,5},{7,6},{8,9},{11,10},{12,13},{15,14},{16,17},{19,... | collective-permute-start | bytes 1179656 | tf_op jit(solution)/shard_map/ppermute | solution.py:332
  61.9 9.1 %collective-permute-start.17 = (bf16[3,64,1024]{2,1,0:T(8,128)(2,1)S(1)}, bf16[3,64,1024]{2,1,0:T(8,128)(2,1)S(1)}, u32[]{:S(2)}, u32[]{:S(2)}) collective-permute-start(bf16[3,64,1024]{2,1,0:T(8,128)(2,1)S(1)} %add_on.15.refs_2_), channel_id=1, source_target_pairs={{1,2},{2,1},{5,6},{6,5},{9,10},{10,9},{13,14},{14,13},{17,18},{18,... | collective-permute-start | bytes 1179656 | tf_op jit(solution)/shard_map/ppermute | solution.py:332
  62.7 12.6 %collective-permute-start.16 = (bf16[3,64,1024]{2,1,0:T(8,128)(2,1)S(1)}, bf16[3,64,1024]{2,1,0:T(8,128)(2,1)S(1)}, u32[]{:S(2)}, u32[]{:S(2)}) collective-permute-start(bf16[3,64,1024]{2,1,0:T(8,128)(2,1)S(1)} %add_on.16.refs_2_), channel_id=1, source_target_pairs={{2,3},{1,0},{6,7},{5,4},{10,11},{9,8},{14,15},{13,12},{18,19},{17,... | collective-permute-start | bytes 1179656 | tf_op jit(solution)/shard_map/ppermute | solution.py:332
  67.0 11.7 %collective-permute-start.15 = (bf16[3,64,1024]{2,1,0:T(8,128)(2,1)S(1)}, bf16[3,64,1024]{2,1,0:T(8,128)(2,1)S(1)}, u32[]{:S(2)}, u32[]{:S(2)}) collective-permute-start(bf16[3,64,1024]{2,1,0:T(8,128)(2,1)S(1)} %activations.4.refs_2_), channel_id=1, source_target_pairs={{0,1},{3,2},{4,5},{7,6},{8,9},{11,10},{12,13},{15,14},{16,17},{19,... | collective-permute-start | bytes 1179656 | tf_op jit(solution)/shard_map/ppermute | solution.py:332
  70.3 9.1 %collective-permute-start.14 = (bf16[3,64,1024]{2,1,0:T(8,128)(2,1)S(1)}, bf16[3,64,1024]{2,1,0:T(8,128)(2,1)S(1)}, u32[]{:S(2)}, u32[]{:S(2)}) collective-permute-start(bf16[3,64,1024]{2,1,0:T(8,128)(2,1)S(1)} %add_on.17.refs_2_), channel_id=1, source_target_pairs={{1,2},{2,1},{5,6},{6,5},{9,10},{10,9},{13,14},{14,13},{17,18},{18,... | collective-permute-start | bytes 1179656 | tf_op jit(solution)/shard_map/ppermute | solution.py:332
  71.1 13.2 %collective-permute-start.21 = (bf16[3,64,1024]{2,1,0:T(8,128)(2,1)S(1)}, bf16[3,64,1024]{2,1,0:T(8,128)(2,1)S(1)}, u32[]{:S(2)}, u32[]{:S(2)}) collective-permute-start(bf16[3,64,1024]{2,1,0:T(8,128)(2,1)S(1)} %add_on.18.refs_2_), channel_id=1, source_target_pairs={{2,3},{1,0},{6,7},{5,4},{10,11},{9,8},{14,15},{13,12},{18,19},{17,... | collective-permute-start | bytes 1179656 | tf_op jit(solution)/shard_map/ppermute | solution.py:332
  75.5 12.4 %collective-permute-start.20 = (bf16[3,64,1024]{2,1,0:T(8,128)(2,1)S(1)}, bf16[3,64,1024]{2,1,0:T(8,128)(2,1)S(1)}, u32[]{:S(2)}, u32[]{:S(2)}) collective-permute-start(bf16[3,64,1024]{2,1,0:T(8,128)(2,1)S(1)} %activations.5.refs_1_.refs_2_), channel_id=1, source_target_pairs={{0,1},{3,2},{4,5},{7,6},{8,9},{11,10},{12,13},{15,14},{16,17},{19,... | collective-permute-start | bytes 1179656 | tf_op jit(solution)/shard_map/ppermute | solution.py:332
  78.7 9.9 %collective-permute-start.19 = (bf16[3,64,1024]{2,1,0:T(8,128)(2,1)S(1)}, bf16[3,64,1024]{2,1,0:T(8,128)(2,1)S(1)}, u32[]{:S(2)}, u32[]{:S(2)}) collective-permute-start(bf16[3,64,1024]{2,1,0:T(8,128)(2,1)S(1)} %pass_on.17.refs_2_.refs_3_), channel_id=1, source_target_pairs={{1,2},{2,1},{5,6},{6,5},{9,10},{10,9},{13,14},{14,13},{17,18},{18,... | collective-permute-start | bytes 1179656 | tf_op jit(solution)/shard_map/ppermute | solution.py:332
  79.5 13.3 %collective-permute-start.18 = (bf16[3,64,1024]{2,1,0:T(8,128)(2,1)S(1)}, bf16[3,64,1024]{2,1,0:T(8,128)(2,1)S(1)}, u32[]{:S(2)}, u32[]{:S(2)}) collective-permute-start(bf16[3,64,1024]{2,1,0:T(8,128)(2,1)S(1)} %add_on.19.refs_2_), channel_id=1, source_target_pairs={{2,3},{1,0},{6,7},{5,4},{10,11},{9,8},{14,15},{13,12},{18,19},{17,... | collective-permute-start | bytes 1179656 | tf_op jit(solution)/shard_map/ppermute | solution.py:332
  84.5 11.7 %collective-permute-start.25 = (bf16[3,64,1024]{2,1,0:T(8,128)(2,1)S(1)}, bf16[3,64,1024]{2,1,0:T(8,128)(2,1)S(1)}, u32[]{:S(2)}, u32[]{:S(2)}) collective-permute-start(bf16[3,64,1024]{2,1,0:T(8,128)(2,1)S(1)} %activations.6.refs_1_.refs_2_), channel_id=1, source_target_pairs={{0,1},{3,2},{4,5},{7,6},{8,9},{11,10},{12,13},{15,14},{16,17},{19,... | collective-permute-start | bytes 1179656 | tf_op jit(solution)/shard_map/ppermute | solution.py:332
  88.0 9.0 %collective-permute-start.24 = (bf16[3,64,1024]{2,1,0:T(8,128)(2,1)S(1)}, bf16[3,64,1024]{2,1,0:T(8,128)(2,1)S(1)}, u32[]{:S(2)}, u32[]{:S(2)}) collective-permute-start(bf16[3,64,1024]{2,1,0:T(8,128)(2,1)S(1)} %pass_on.18.refs_1_.refs_3_), channel_id=1, source_target_pairs={{1,2},{2,1},{5,6},{6,5},{9,10},{10,9},{13,14},{14,13},{17,18},{18,... | collective-permute-start | bytes 1179656 | tf_op jit(solution)/shard_map/ppermute | solution.py:332
  88.7 11.7 %collective-permute-start.23 = (bf16[3,64,1024]{2,1,0:T(8,128)(2,1)S(1)}, bf16[3,64,1024]{2,1,0:T(8,128)(2,1)S(1)}, u32[]{:S(2)}, u32[]{:S(2)}) collective-permute-start(bf16[3,64,1024]{2,1,0:T(8,128)(2,1)S(1)} %pass_on.19.refs_2_.refs_4_), channel_id=1, source_target_pairs={{2,3},{1,0},{6,7},{5,4},{10,11},{9,8},{14,15},{13,12},{18,19},{17,... | collective-permute-start | bytes 1179656 | tf_op jit(solution)/shard_map/ppermute | solution.py:332
  93.0 12.3 %collective-permute-start.22 = (bf16[3,64,1024]{2,1,0:T(8,128)(2,1)S(1)}, bf16[3,64,1024]{2,1,0:T(8,128)(2,1)S(1)}, u32[]{:S(2)}, u32[]{:S(2)}) collective-permute-start(bf16[3,64,1024]{2,1,0:T(8,128)(2,1)S(1)} %activations.7.refs_1_.refs_2_), channel_id=1, source_target_pairs={{0,1},{3,2},{4,5},{7,6},{8,9},{11,10},{12,13},{15,14},{16,17},{19,... | collective-permute-start | bytes 1179656 | tf_op jit(solution)/shard_map/ppermute | solution.py:332
  96.3 9.7 %collective-permute-start.29 = (bf16[3,64,1024]{2,1,0:T(8,128)(2,1)S(1)}, bf16[3,64,1024]{2,1,0:T(8,128)(2,1)S(1)}, u32[]{:S(2)}, u32[]{:S(2)}) collective-permute-start(bf16[3,64,1024]{2,1,0:T(8,128)(2,1)S(1)} %pass_on.20.refs_1_.refs_3_), channel_id=1, source_target_pairs={{1,2},{2,1},{5,6},{6,5},{9,10},{10,9},{13,14},{14,13},{17,18},{18,... | collective-permute-start | bytes 1179656 | tf_op jit(solution)/shard_map/ppermute | solution.py:332
  103.9 17.7 %collective-permute-start.27 = (bf16[2,128,1024]{2,1,0:T(8,128)(2,1)S(1)}, bf16[2,128,1024]{2,1,0:T(8,128)(2,1)S(1)}, u32[]{:S(2)}, u32[]{:S(2)}) collective-permute-start(bf16[2,128,1024]{2,1,0:T(8,128)(2,1)S(1)} %get-tuple-element.40), channel_id=1, source_target_pairs={{0,16},{16,0},{1,17},{17,1},{2,18},{18,2},{3,19},{19,3},{4,20},{20... | collective-permute-start | bytes 1572872 | tf_op jit(solution)/shard_map/ppermute | solution.py:51
  104.0 13.8 %collective-permute-start.28 = (bf16[3,64,1024]{2,1,0:T(8,128)(2,1)S(1)}, bf16[3,64,1024]{2,1,0:T(8,128)(2,1)S(1)}, u32[]{:S(2)}, u32[]{:S(2)}) collective-permute-start(bf16[3,64,1024]{2,1,0:T(8,128)(2,1)S(1)} %pass_on.21.refs_9_.refs_4_), channel_id=1, source_target_pairs={{2,3},{1,0},{6,7},{5,4},{10,11},{9,8},{14,15},{13,12},{18,19},{17,... | collective-permute-start | bytes 1179656 | tf_op jit(solution)/shard_map/ppermute | solution.py:332
  105.3 18.0 %collective-permute-start.26 = (bf16[3,64,1024]{2,1,0:T(8,128)(2,1)S(1)}, bf16[3,64,1024]{2,1,0:T(8,128)(2,1)S(1)}, u32[]{:S(2)}, u32[]{:S(2)}) collective-permute-start(bf16[3,64,1024]{2,1,0:T(8,128)(2,1)S(1)} %pass_on.22.refs_1_.refs_3_), channel_id=1, source_target_pairs={{1,2},{2,1},{5,6},{6,5},{9,10},{10,9},{13,14},{14,13},{17,18},{18,... | collective-permute-start | bytes 1179656 | tf_op jit(solution)/shard_map/ppermute | solution.py:332
  106.0 19.8 %collective-permute-start.33 = (bf16[3,64,1024]{2,1,0:T(8,128)(2,1)S(1)}, bf16[3,64,1024]{2,1,0:T(8,128)(2,1)S(1)}, u32[]{:S(2)}, u32[]{:S(2)}) collective-permute-start(bf16[3,64,1024]{2,1,0:T(8,128)(2,1)S(1)} %pass_on.23.refs_9_.refs_4_), channel_id=1, source_target_pairs={{2,3},{1,0},{6,7},{5,4},{10,11},{9,8},{14,15},{13,12},{18,19},{17,... | collective-permute-start | bytes 1179656 | tf_op jit(solution)/shard_map/ppermute | solution.py:332
  121.5 9.2 %collective-permute-start.32 = (bf16[2,128,1024]{2,1,0:T(8,128)(2,1)S(1)}, bf16[2,128,1024]{2,1,0:T(8,128)(2,1)S(1)}, u32[]{:S(2)}, u32[]{:S(2)}) collective-permute-start(bf16[2,128,1024]{2,1,0:T(8,128)(2,1)S(1)} %get-tuple-element.42), channel_id=1, source_target_pairs={{0,16},{16,0},{1,17},{17,1},{2,18},{18,2},{3,19},{19,3},{4,20},{20... | collective-permute-start | bytes 1572872 | tf_op jit(solution)/shard_map/ppermute | solution.py:51
  121.7 14.4 %collective-permute-start.31 = (bf16[2,128,1024]{2,1,0:T(8,128)(2,1)S(1)}, bf16[2,128,1024]{2,1,0:T(8,128)(2,1)S(1)}, u32[]{:S(2)}, u32[]{:S(2)}) collective-permute-start(bf16[2,128,1024]{2,1,0:T(8,128)(2,1)S(1)} %add_on.20.refs_1_), channel_id=1, source_target_pairs={{0,8},{4,12},{8,0},{12,4},{1,9},{5,13},{9,1},{13,5},{2,10},{6,14},... | collective-permute-start | bytes 1572872 | tf_op jit(solution)/shard_map/ppermute | solution.py:51
  129.4 17.1 %collective-permute-start.36 = (bf16[2,128,1024]{2,1,0:T(8,128)(2,1)S(1)}, bf16[2,128,1024]{2,1,0:T(8,128)(2,1)S(1)}, u32[]{:S(2)}, u32[]{:S(2)}) collective-permute-start(bf16[2,128,1024]{2,1,0:T(8,128)(2,1)S(1)} %get-tuple-element.50), channel_id=1, source_target_pairs={{0,16},{16,0},{1,17},{17,1},{2,18},{18,2},{3,19},{19,3},{4,20},{20... | collective-permute-start | bytes 1572872 | tf_op jit(solution)/shard_map/ppermute | solution.py:51
  129.4 13.4 %collective-permute-start.30 = (bf16[3,64,1024]{2,1,0:T(8,128)(2,1)S(1)}, bf16[3,64,1024]{2,1,0:T(8,128)(2,1)S(1)}, u32[]{:S(2)}, u32[]{:S(2)}) collective-permute-start(bf16[3,64,1024]{2,1,0:T(8,128)(2,1)S(1)} %pass_on.24.refs_9_.refs_4_), channel_id=1, source_target_pairs={{2,3},{1,0},{6,7},{5,4},{10,11},{9,8},{14,15},{13,12},{18,19},{17,... | collective-permute-start | bytes 1179656 | tf_op jit(solution)/shard_map/ppermute | solution.py:332
  130.9 31.1 %collective-permute-start.35 = (bf16[2,128,1024]{2,1,0:T(8,128)(2,1)S(1)}, bf16[2,128,1024]{2,1,0:T(8,128)(2,1)S(1)}, u32[]{:S(2)}, u32[]{:S(2)}) collective-permute-start(bf16[2,128,1024]{2,1,0:T(8,128)(2,1)S(1)} %add_on.21.refs_1_), channel_id=1, source_target_pairs={{0,4},{4,0},{8,12},{12,8},{1,5},{5,1},{9,13},{13,9},{2,6},{6,2},{1... | collective-permute-start | bytes 1572872 | tf_op jit(solution)/shard_map/ppermute | solution.py:51
  146.4 15.6 %collective-permute-start.34 = (bf16[2,128,1024]{2,1,0:T(8,128)(2,1)S(1)}, bf16[2,128,1024]{2,1,0:T(8,128)(2,1)S(1)}, u32[]{:S(2)}, u32[]{:S(2)}) collective-permute-start(bf16[2,128,1024]{2,1,0:T(8,128)(2,1)S(1)} %get-tuple-element.45), channel_id=1, source_target_pairs={{0,16},{16,0},{1,17},{17,1},{2,18},{18,2},{3,19},{19,3},{4,20},{20... | collective-permute-start | bytes 1572872 | tf_op jit(solution)/shard_map/ppermute | solution.py:51
  146.6 15.6 %collective-permute-start.37 = (bf16[2,128,1024]{2,1,0:T(8,128)(2,1)S(1)}, bf16[2,128,1024]{2,1,0:T(8,128)(2,1)S(1)}, u32[]{:S(2)}, u32[]{:S(2)}) collective-permute-start(bf16[2,128,1024]{2,1,0:T(8,128)(2,1)S(1)} %add_on.22.refs_13_), channel_id=1, source_target_pairs={{0,12},{4,8},{8,4},{12,0},{1,13},{5,9},{9,5},{13,1},{2,14},{6,10},... | collective-permute-start | bytes 1572872 | tf_op jit(solution)/shard_map/ppermute | solution.py:51

commit v4 on v3

--- a/solution.py
+++ b/solution.py
@@ -25,7 +25,7 @@
     def __init__(self):
         self.last = None
 
-    def call(self, name, kernel, operands, in_specs, out_specs, out_shape, limit=16, **rest):
+    def call(self, name, kernel, operands, in_specs, out_specs, out_shape, limit=16, cost=1000, **rest):
         if self.last is not None:
             count, inner = len(operands), kernel
             operands, in_specs = [*operands, self.last], [*in_specs, ANY]
@@ -39,7 +39,7 @@
             out_specs=out_specs,
             out_shape=out_shape,
             compiler_params=pltpu.CompilerParams(vmem_limit_bytes=limit * MIB),
-            cost_estimate=pl.CostEstimate(flops=1000, bytes_accessed=1000, transcendentals=0),
+            cost_estimate=pl.CostEstimate(flops=1000, bytes_accessed=cost, transcendentals=0),
             name=name,
             **rest,
         )(*operands)
@@ -81,6 +81,19 @@
     )
 
 
+def parted(line, value):
+    _, rows, width = value.shape
+    half = rows // 2
+
+    def kernel(a_ref, *outs):
+        for index, out in enumerate(outs):
+            out[...] = a_ref[index // 2, index % 2 * half : (index % 2 + 1) * half]
+
+    return line.call(
+        "parted", kernel, [value], [LOCAL], [LOCAL] * 4, [shaped(half, width)] * 4, limit=4
+    )
+
+
 def pass_on(line, value):
     def kernel(a_ref, o_ref):
         pass
@@ -102,7 +115,8 @@
     units = weights[0].shape[1]
     tile = min(256, units)
 
-    def kernel(core_ref, own_ref, other_ref, gate_ref, up_ref, down_ref, last_ref, first_ref):
+    def kernel(core_ref, own_ref, *refs):
+        other_refs, (gate_ref, up_ref, down_ref, last_ref, first_ref) = refs[:4], refs[4:]
         here = pl.ds(pl.multiple_of(core_ref[0] * width, width), width)
         there = pl.ds(pl.multiple_of((1 - core_ref[0]) * width, width), width)
 
@@ -112,7 +126,8 @@
             for index, (which, weight) in enumerate(((0, gate_ref), (0, up_ref), (1, down_ref))):
                 left = own_ref[which, low : low + rows]
                 part = jnp.dot(left, weight[here, columns], preferred_element_type=F32)
-                left = other_ref[which, low : low + rows]
+                left = jnp.concatenate([ref[...] for ref in other_refs[2 * which : 2 * which + 2]])
+                left = left[low : low + rows]
                 part += jnp.dot(left, weight[there, columns], preferred_element_type=F32)
                 part = part.astype(BF16)
                 for at in range(0, rows // piece, 2):
@@ -123,8 +138,8 @@
     return line.call(
         "forward_products",
         kernel,
-        [core, own, other, *weights],
-        [SCALAR] + [LOCAL] * 5,
+        [core, own, *other, *weights],
+        [SCALAR] + [LOCAL] * 8,
         [LOCAL] * 2,
         [shaped(3, rows // 2, units)] * 2,
     )
@@ -136,6 +151,30 @@
 
     return line.call(
         "add_on", kernel, [held, received], [LOCAL] * 2, LOCAL, shaped(*held.shape), limit=4
+    )
+
+
+def add_quarters(line, held, quarters, apart):
+    _, rows, width = held.shape
+    half = rows // 2
+
+    def kernel(a_ref, *refs):
+        for index, ref in enumerate(refs[:4]):
+            to = slice(index % 2 * half, (index % 2 + 1) * half)
+            total = a_ref[index // 2, to].astype(F32) + ref[...].astype(F32)
+            if apart:
+                refs[4 + index // 2][0, to] = total.astype(BF16)
+            else:
+                refs[4][index // 2, to] = total.astype(BF16)
+
+    return line.call(
+        "add_quarters",
+        kernel,
+        [held, *quarters],
+        [LOCAL] * 5,
+        [LOCAL] * (1 + apart),
+        [shaped(1, rows, width)] * 2 if apart else [shaped(*held.shape)],
+        limit=4,
     )
 
 
@@ -161,7 +200,8 @@
 
     def kernel(core_ref, place_ref, *refs):
         passed_refs = refs[:count]
-        gate_ref, up_ref, down_ref, keep_ref, send_ref, acts_ref = refs[count:]
+        gate_ref, up_ref, down_ref, keep_ref, acts_ref = refs[count : count + 5]
+        send_refs = refs[count + 5 :]
         near = jnp.minimum(place_ref[0], count - 1 - place_ref[0])
         for index, ref in enumerate(passed_refs):
             far = index >= count // 2
@@ -172,24 +212,28 @@
                     to = (2 * at + far) * piece
                     acts_ref[:, to : to + piece] = ref[:, at * piece : (at + 1) * piece]
 
-        def fill(target, side):
+        def fill(targets, side):
             lines = pl.ds(pl.multiple_of(side * width, width), width)
             out = lax.dot_general(down_ref[lines], acts_ref[0], NT, preferred_element_type=F32)
             grad = lax.dot_general(gate_ref[lines], acts_ref[1], NT, preferred_element_type=F32)
             grad += lax.dot_general(up_ref[lines], acts_ref[2], NT, preferred_element_type=F32)
-            target[0] = out.astype(BF16).T
-            target[1] = grad.astype(BF16).T
-
-        fill(send_ref, 1 - core_ref[0])
-        fill(keep_ref, core_ref[0])
+            out, grad = out.astype(BF16).T, grad.astype(BF16).T
+            if len(targets) == 1:
+                targets[0][0], targets[0][1] = out, grad
+            else:
+                targets[0][...], targets[1][...] = out[:half], out[half:]
+                targets[2][...], targets[3][...] = grad[:half], grad[half:]
+
+        fill(send_refs, 1 - core_ref[0])
+        fill([keep_ref], core_ref[0])
 
     return line.call(
         "backward_products",
         kernel,
         [core, place, *passed, *weights],
         [SCALAR] * 2 + [LOCAL] * (count + 3),
-        [LOCAL] * 3,
-        [shaped(2, rows, width)] * 2 + [shaped(3, rows, units)],
+        [LOCAL] * 6,
+        [shaped(2, rows, width), shaped(3, rows, units)] + [shaped(half, width)] * 4,
     )
 
 
@@ -200,11 +244,12 @@
     tile = min(256, width)
     steps = width // tile
     total = rows * count
+    slots = 3
 
     def kernel(core_ref, *refs):
-        own_refs, other_refs = refs[:count], refs[count : 2 * count]
-        act_refs = refs[2 * count : 2 * count + chunks]
-        _, gate_out, up_out, down_out, all_acts, left, held, sems = refs[2 * count + chunks :]
+        own_refs, other_refs = refs[:count], refs[count : 5 * count]
+        act_refs = refs[5 * count : 5 * count + chunks]
+        _, gate_out, up_out, down_out, all_acts, left, held, sems = refs[5 * count + chunks :]
         for ref, (low, high) in zip(act_refs, spans):
             all_acts[:, low:high] = ref[...]
 
@@ -220,7 +265,7 @@
 
         @pl.loop(0, 2 * steps)
         def _(step):
-            slot = lax.rem(step, 2)
+            slot = lax.rem(step, slots)
             columns = pl.ds(pl.multiple_of(lax.rem(step, steps) * tile, tile), tile)
 
             @pl.when(step < steps)
@@ -231,45 +276,46 @@
             @pl.when(step >= steps)
             def _():
                 for index, ref in enumerate(other_refs):
-                    left[:, index * rows : (index + 1) * rows] = ref[:, :, columns]
-
-            @pl.when(step >= 2)
+                    to = index // 4 * rows + index % 2 * (rows // 2)
+                    left[index // 2 % 2, to : to + rows // 2] = ref[:, columns]
+
+            @pl.when(step >= slots)
             def _():
-                for copy in copies(step - 2, slot):
+                for copy in copies(step - slots, slot):
                     copy.wait()
 
+            out_copies = copies(step, slot)
             for index, (which, act) in enumerate(((0, 1), (0, 2), (1, 0))):
                 held[slot, index] = lax.dot_general(
                     left[which], all_acts[act], TN, preferred_element_type=F32
                 )
-            for copy in copies(step, slot):
-                copy.start()
-
-        for step in (2 * steps - 2, 2 * steps - 1):
-            for copy in copies(step, step % 2):
+                out_copies[index].start()
+
+        for step in range(max(0, 2 * steps - slots), 2 * steps):
+            for copy in copies(step, step % slots):
                 copy.wait()
 
     return line.call(
         "weight_grads",
         kernel,
-        [core, *owns, *others, *acts],
-        [SCALAR] + [LOCAL] * (2 * count + chunks),
+        [core, *owns, *[ref for quarters in others for ref in quarters], *acts],
+        [SCALAR] + [LOCAL] * (5 * count + chunks),
         [ANY] * 4,
         [shaped(16, 128)] + [shaped(2 * width, units, dtype=F32)] * 3,
-        limit=24,
+        limit=32,
         scratch_shapes=[
             pltpu.VMEM((3, total, units), BF16),
             pltpu.VMEM((2, total, tile), BF16),
-            pltpu.VMEM((2, 3, tile, units), F32),
-            pltpu.SemaphoreType.DMA((2, 3)),
+            pltpu.VMEM((slots, 3, tile, units), F32),
+            pltpu.SemaphoreType.DMA((slots, 3)),
         ],
     )
 
 
 def final_sum(line, parts, flip, piece):
-    rows = sum(part.shape[1] for part in parts[0])
-    width = parts[0][0].shape[2]
-    flat = [part for block in parts for part in block]
+    rows = sum(part[0].shape[1] for part in parts[0])
+    width = parts[0][0][0].shape[2]
+    flat = [half for block in parts for part in block for half in part]
 
     def kernel(flip_ref, *refs):
         outs = refs[len(flat) :]
@@ -278,17 +324,18 @@
         for block in parts:
             spans = []
             for part in block:
-                for low in range(0, part.shape[1], piece):
-                    spans.append((refs[at], low))
-                at += 1
+                ends = [(refs[at + i * (len(part) - 1)], i * (2 - len(part))) for i in range(2)]
+                at += len(part)
+                spans += [(ends, low) for low in range(0, part[0].shape[1], piece)]
             sources.append(spans)
         for place in range(rows // piece):
             to = pl.ds(pl.multiple_of((place ^ flip_ref[0]) * piece, piece), piece)
             for index, out_ref in enumerate(outs):
                 total = 0.0
                 for spans in sources:
-                    ref, low = spans[place]
-                    total += ref[index, low : low + piece].astype(F32)
+                    ends, low = spans[place]
+                    ref, which = ends[index]
+                    total += ref[which, low : low + piece].astype(F32)
                 out_ref[to] = total.astype(BF16)
 
     return line.call(
@@ -302,16 +349,20 @@
 
 
 WEIGHTS = -1
-FOUR = (2, 1, 2, 0, 1, 3, 2, 3, 1, 2, 3, 1, 2, 0, 3, 1, 2, 0, 3, 1, 2, 0, 3, 1, 2, 0, 3, 1, 2, 0, 3, 1, 2, 0, 3, WEIGHTS, 1, 0, 3)
+FOUR = (
+    0, 1, 2, 1, 2, 0, 3, 1, 0, 3, 2, 1, 0, 3, 2, 1, 0, 3, 2, 1,
+    0, 3, 2, 1, 0, 3, 2, 0, 1, 1, 3, 2, 1, 2, 2, 3, 3, 3, WEIGHTS, 0,
+    1, 2, 3,
+)
 
 
 def plan_of(n_gy, n_gz, pieces):
+    if (n_gy, n_gz) == (4, 4):
+        return [(d, 0, pieces) for d in (0, 1, 2, 3)], FOUR
     chunks = [(d, 0, pieces) for d in range(n_gy)]
-    if (n_gy, n_gz) == (4, 4):
-        return chunks, FOUR
     events = []
     for at, (d, _, _) in enumerate(chunks):
-        for k in range(-1 if d else 0, 2 * n_gz + (1 if d else 0)):
+        for k in range(-1 if d else 0, 2 * n_gz + (2 if d else 1)):
             events.append((at + 2 * k, at))
     return chunks, [at for _, at in sorted(events)] + [WEIGHTS]
 
@@ -324,7 +375,9 @@
     level = lax.axis_index("gz").astype(jnp.int32)
     place = level.reshape(1)
     flip = (level >= n_gz // 2).astype(jnp.int32).reshape(1)
-    swap_core = functools.partial(swap, axis="gx", size=2, mask=1)
+
+    def swap_core(quarters):
+        return [swap(quarter, "gx", 2, 1) for quarter in quarters]
     line = Line()
 
     def hop(value, step):
@@ -332,7 +385,7 @@
         return lax.ppermute(value, "gz", pairs)
 
     mine = ordered_rows(line, tokens, out_grad, flip, pieces)
-    others = [swap_core(mine)] + [None] * (n_gy - 1)
+    others = [swap_core(parted(line, mine))] + [None] * (n_gy - 1)
     owns = {0: mine}
 
     def send_blocks(d):
@@ -349,7 +402,7 @@
         if others[d] is None:
             yield
             owns[d] = pass_on(line, owns[d])
-            others[d] = swap_core(owns[d])
+            others[d] = swap_core(parted(line, owns[d]))
             send_blocks(d)
         yield
         last, first = forward_products(
@@ -366,17 +419,17 @@
         for step in range(n_gz - 1):
             value = hop(value, step)
             yield
-            if step < n_gz - 2:
-                value = pass_on(line, value)
+            value = pass_on(line, value)
             passed.append(value)
-        keep, send, acts[at] = backward_products(line, core, place, passed, piece, weights)
+        yield
+        keep, acts[at], *send = backward_products(line, core, place, passed, piece, weights)
         got = swap_core(send)
         yield
-        part = add_on(line, keep, got)
+        part = add_quarters(line, keep, got, at == len(plan) - 1)
         if d:
-            part = swap(part, "gy", n_gy, d)
+            part = [swap(half, "gy", n_gy, d) for half in part]
             yield
-            part = pass_on(line, part)
+            part = [pass_on(line, half) for half in part]
         parts[d].append(part)
         yield
 

time: 164 us -> 160 us (0.976)
  waiting for transfers between devices: 52.6 us -> 46.5 us
  starting transfers between devices: 57.9 us -> 63.4 us
  Pallas kernels: 42.9 us -> 39.1 us
    ppermute x24, waiting for transfers between devices: 37.5 us -> 31.8 us  [hop(): return lax.ppermute(value, 'gz', pairs)]
    ppermute x14 -> x39, starting transfers between devices: 11.7 us -> 16.6 us  [swap(): return lax.ppermute(value, axis, [(i, i ^ mask) for i in range(size)])]
    pallas_call x41 -> x50, Pallas kernels: 42.9 us -> 39.1 us  [call(): pl.pallas_call(kernel, in_specs=in_specs, out_specs=out_specs, out_shape=...]
    ppermute x14 -> x39, waiting for transfers between devices: 15.1 us -> 14.7 us  [swap(): return lax.ppermute(value, axis, [(i, i ^ mask) for i in range(size)])]
  transfers between devices with their start and end apart: 38 -> 63, of which waited for: 15 -> 23; matrix products, arithmetic and copies ran while one was open for 0% -> 0% of each run, Pallas kernels for 25% -> 21%
where the time goes in v4:
time: 160 us; the launch traced here: 159 us
  starting transfers between devices  63.4 us (40%)
  waiting for transfers between devices  46.5 us (29%)
  Pallas kernels  39.1 us (24%)
  local copies, waits for them, and re-layouts  8.47 us (5%)
    ppermute x24, starting transfers between devices, hop(): return lax.ppermute(value, 'gz', pairs)  46.9 us
    pallas_call x50, Pallas kernels, call(): pl.pallas_call(kernel, in_specs=in_specs, out_specs=out_specs, out_shape=...  39.1 us
    ppermute x24, waiting for transfers between devices, hop(): return lax.ppermute(value, 'gz', pairs)  31.8 us
    ppermute x39, starting transfers between devices, swap(): return lax.ppermute(value, axis, [(i, i ^ mask) for i in range(size)])  16.6 us
    ppermute x39, waiting for transfers between devices, swap(): return lax.ppermute(value, axis, [(i, i ^ mask) for i in range(size)])  14.7 us
    unnamed x16, local copies, waits for them, and re-layouts  8.47 us
  transfers between devices with their start and end apart: 63, of which 23 were waited for; matrix products, arithmetic and copies ran while one was open for 0% of the time, Pallas kernels for 21%

profile of v4, /device:TPU:0, one launch (start us, length us, event | category | flops | bytes accessed | tf_op | source)
XLA Modules:
  0.0 158.9 jit_solution(1625142114772262997)
XLA Ops:
  0.6 0.9 copy-done.6
  1.6 0.9 copy-done.7
  2.5 0.7 ordered_rows.1.refs_0_.refs_1_
  3.3 3.0 %collective-permute-start.6 = (bf16[2,128,1024]{2,1,0:T(8,128)(2,1)S(1)}, bf16[2,128,1024]{2,1,0:T(8,128)(2,1)S(1)}, u32[]{:S(2)}, u32[]{:S(2)}) collective-permute-start(bf16[2,128,1024]{2,1,0:T(8,128)(2,1)S(1)} %ordered_rows.1.refs_0_.refs_1_), channel_id=1, source_target_pairs={{0,4},{4,0},{8,12},{12,8},{1,5},{5,1},{9,13},{13,9},{2,6},{6,2},{1... | collective-permute-start | bytes 1572872 | tf_op jit(solution)/shard_map/ppermute | solution.py:51
  6.3 1.5 collective-permute-start.5
  7.9 0.5 collective-permute-start.1
  8.5 0.8 collective-permute-done.refs_2_.refs_5_
  9.8 0.8 collective-permute-done.3.refs_5_.refs_8_
  10.6 2.2 %copy-done = bf16[2048,1024]{1,0:T(8,128)(2,1)S(1)} copy-done((bf16[2048,1024]{1,0:T(8,128)(2,1)S(1)}, bf16[2048,1024]{1,0:T(8,128)(2,1)}, u32[]{:S(2)}) %copy-start) | copy-done | bytes 4194328
  12.8 2.2 %copy-done.2 = bf16[2048,1024]{1,0:T(8,128)(2,1)S(1)} copy-done((bf16[2048,1024]{1,0:T(8,128)(2,1)S(1)}, bf16[2048,1024]{1,0:T(8,128)(2,1)}, u32[]{:S(2)}) %copy-start.2) | copy-done | bytes 4194328
  15.0 2.2 %copy-done.4 = bf16[2048,1024]{1,0:T(8,128)(2,1)S(1)} copy-done((bf16[2048,1024]{1,0:T(8,128)(2,1)S(1)}, bf16[2048,1024]{1,0:T(8,128)(2,1)}, u32[]{:S(2)}) %copy-start.4) | copy-done | bytes 4194328
  17.2 2.7 %forward_products.4 = (bf16[3,64,1024]{2,1,0:T(8,128)(2,1)S(1)}, bf16[3,64,1024]{2,1,0:T(8,128)(2,1)S(1)}) custom-call(s32[1]{0:T(128)} %bitcast.1.refs_0_, bf16[2,128,1024]{2,1,0:T(8,128)(2,1)S(1)} %ordered_rows.1.refs_0_.refs_1_, bf16[64,1024]{1,0:T(8,128)(2,1)S(1)} %collective-permute-done.refs_2_.refs_5_, ...), custom_call_target="tpu_custom_call" | custom-call | flops 1000 | bytes 1000 | tf_op jit(solution)/shard_map/forward_products/pallas_call | solution.py:36
  20.3 3.6 %collective-permute-start.4 = (bf16[3,64,1024]{2,1,0:T(8,128)(2,1)S(1)}, bf16[3,64,1024]{2,1,0:T(8,128)(2,1)S(1)}, u32[]{:S(2)}, u32[]{:S(2)}) collective-permute-start(bf16[3,64,1024]{2,1,0:T(8,128)(2,1)S(1)} %get-tuple-element.66.refs_0_), channel_id=1, source_target_pairs={{0,1},{3,2},{4,5},{7,6},{8,9},{11,10},{12,13},{15,14},{16,17},{19,... | collective-permute-start | bytes 1179656 | tf_op jit(solution)/shard_map/ppermute | solution.py:385
  25.3 1.0 collective-permute-start.17
  26.4 0.5 collective-permute-start.9
  27.0 2.7 %forward_products.5 = (bf16[3,64,1024]{2,1,0:T(8,128)(2,1)S(1)}, bf16[3,64,1024]{2,1,0:T(8,128)(2,1)S(1)}) custom-call(s32[1]{0:T(128)} %bitcast.1.refs_0_, bf16[2,128,1024]{2,1,0:T(8,128)(2,1)S(1)} %pass_on.19.refs_0_.refs_1_.refs_2_, bf16[64,1024]{1,0:T(8,128)(2,1)S(1)} %collective-permute-done.11.refs_2_.refs_9_, ...), custom_call_target="tpu_custom_call" | custom-call | flops 1000 | bytes 1000 | tf_op jit(solution)/shard_map/forward_products/pallas_call | solution.py:36
  29.7 2.7 %forward_products.6 = (bf16[3,64,1024]{2,1,0:T(8,128)(2,1)S(1)}, bf16[3,64,1024]{2,1,0:T(8,128)(2,1)S(1)}) custom-call(s32[1]{0:T(128)} %bitcast.1.refs_0_, bf16[2,128,1024]{2,1,0:T(8,128)(2,1)S(1)} %pass_on.20.refs_0_.refs_1_.refs_3_, bf16[64,1024]{1,0:T(8,128)(2,1)S(1)} %collective-permute-done.7.refs_2_.refs_13_, ...), custom_call_target="tpu_custom_call" | custom-call | flops 1000 | bytes 1000 | tf_op jit(solution)/shard_map/forward_products/pallas_call | solution.py:36
  32.8 0.7 collective-permute-start.15
  33.5 7.2 %collective-permute-start.16 = (bf16[3,64,1024]{2,1,0:T(8,128)(2,1)S(1)}, bf16[3,64,1024]{2,1,0:T(8,128)(2,1)S(1)}, u32[]{:S(2)}, u32[]{:S(2)}) collective-permute-start(bf16[3,64,1024]{2,1,0:T(8,128)(2,1)S(1)} %get-tuple-element.77.refs_0_), channel_id=1, source_target_pairs={{0,1},{3,2},{4,5},{7,6},{8,9},{11,10},{12,13},{15,14},{16,17},{19,... | collective-permute-start | bytes 1179656 | tf_op jit(solution)/shard_map/ppermute | solution.py:385
  40.7 1.3 collective-permute-start.20
  42.8 7.5 %collective-permute-done.16.refs_1_ = bf16[3,64,1024]{2,1,0:T(8,128)(2,1)S(1)} collective-permute-done((bf16[3,64,1024]{2,1,0:T(8,128)(2,1)S(1)}, bf16[3,64,1024]{2,1,0:T(8,128)(2,1)S(1)}, u32[]{:S(2)}, u32[]{:S(2)}) %collective-permute-start.16) | collective-permute-done | bytes 393248 | tf_op jit(solution)/shard_map/ppermute | solution.py:385
  50.5 0.7 collective-permute-start.19
  51.2 1.3 collective-permute-start.18
  52.5 2.7 %forward_products.7 = (bf16[3,64,1024]{2,1,0:T(8,128)(2,1)S(1)}, bf16[3,64,1024]{2,1,0:T(8,128)(2,1)S(1)}) custom-call(s32[1]{0:T(128)} %bitcast.1.refs_0_, bf16[2,128,1024]{2,1,0:T(8,128)(2,1)S(1)} %pass_on.21.refs_0_.refs_1_.refs_4_, bf16[64,1024]{1,0:T(8,128)(2,1)S(1)} %collective-permute-done.21.refs_2_.refs_17_, ...), custom_call_target="tpu_custom_call" | custom-call | flops 1000 | bytes 1000 | tf_op jit(solution)/shard_map/forward_products/pallas_call | solution.py:36
  55.2 6.1 %collective-permute-start.28 = (bf16[3,64,1024]{2,1,0:T(8,128)(2,1)S(1)}, bf16[3,64,1024]{2,1,0:T(8,128)(2,1)S(1)}, u32[]{:S(2)}, u32[]{:S(2)}) collective-permute-start(bf16[3,64,1024]{2,1,0:T(8,128)(2,1)S(1)} %get-tuple-element.84.refs_0_), channel_id=1, source_target_pairs={{0,1},{3,2},{4,5},{7,6},{8,9},{11,10},{12,13},{15,14},{16,17},{19,... | collective-permute-start | bytes 1179656 | tf_op jit(solution)/shard_map/ppermute | solution.py:385
  61.5 0.7 collective-permute-start.27
  62.3 1.3 collective-permute-start.26
  63.6 2.6 %collective-permute-done.18.refs_1_ = bf16[3,64,1024]{2,1,0:T(8,128)(2,1)S(1)} collective-permute-done((bf16[3,64,1024]{2,1,0:T(8,128)(2,1)S(1)}, bf16[3,64,1024]{2,1,0:T(8,128)(2,1)S(1)}, u32[]{:S(2)}, u32[]{:S(2)}) %collective-permute-start.18) | collective-permute-done | bytes 393248 | tf_op jit(solution)/shard_map/ppermute | solution.py:385
  66.4 4.0 %collective-permute-start.25 = (bf16[3,64,1024]{2,1,0:T(8,128)(2,1)S(1)}, bf16[3,64,1024]{2,1,0:T(8,128)(2,1)S(1)}, u32[]{:S(2)}, u32[]{:S(2)}) collective-permute-start(bf16[3,64,1024]{2,1,0:T(8,128)(2,1)S(1)} %activations.4.refs_2_), channel_id=1, source_target_pairs={{0,1},{3,2},{4,5},{7,6},{8,9},{11,10},{12,13},{15,14},{16,17},{19,... | collective-permute-start | bytes 1179656 | tf_op jit(solution)/shard_map/ppermute | solution.py:385
  70.5 0.7 collective-permute-start.32
  71.3 1.3 collective-permute-start.31
  72.6 4.2 %collective-permute-done.26.refs_1_ = bf16[3,64,1024]{2,1,0:T(8,128)(2,1)S(1)} collective-permute-done((bf16[3,64,1024]{2,1,0:T(8,128)(2,1)S(1)}, bf16[3,64,1024]{2,1,0:T(8,128)(2,1)S(1)}, u32[]{:S(2)}, u32[]{:S(2)}) %collective-permute-start.26) | collective-permute-done | bytes 393248 | tf_op jit(solution)/shard_map/ppermute | solution.py:385
  77.0 3.4 %collective-permute-start.30 = (bf16[3,64,1024]{2,1,0:T(8,128)(2,1)S(1)}, bf16[3,64,1024]{2,1,0:T(8,128)(2,1)S(1)}, u32[]{:S(2)}, u32[]{:S(2)}) collective-permute-start(bf16[3,64,1024]{2,1,0:T(8,128)(2,1)S(1)} %activations.5.refs_1_.refs_2_), channel_id=1, source_target_pairs={{0,1},{3,2},{4,5},{7,6},{8,9},{11,10},{12,13},{15,14},{16,17},{19,... | collective-permute-start | bytes 1179656 | tf_op jit(solution)/shard_map/ppermute | solution.py:385
  80.5 0.7 collective-permute-start.29
  81.3 1.3 collective-permute-start.36
  82.6 3.4 %collective-permute-done.31.refs_1_ = bf16[3,64,1024]{2,1,0:T(8,128)(2,1)S(1)} collective-permute-done((bf16[3,64,1024]{2,1,0:T(8,128)(2,1)S(1)}, bf16[3,64,1024]{2,1,0:T(8,128)(2,1)S(1)}, u32[]{:S(2)}, u32[]{:S(2)}) %collective-permute-start.31) | collective-permute-done | bytes 393248 | tf_op jit(solution)/shard_map/ppermute | solution.py:385
  86.2 2.5 %collective-permute-start.35 = (bf16[3,64,1024]{2,1,0:T(8,128)(2,1)S(1)}, bf16[3,64,1024]{2,1,0:T(8,128)(2,1)S(1)}, u32[]{:S(2)}, u32[]{:S(2)}) collective-permute-start(bf16[3,64,1024]{2,1,0:T(8,128)(2,1)S(1)} %activations.6.refs_1_.refs_2_), channel_id=1, source_target_pairs={{0,1},{3,2},{4,5},{7,6},{8,9},{11,10},{12,13},{15,14},{16,17},{19,... | collective-permute-start | bytes 1179656 | tf_op jit(solution)/shard_map/ppermute | solution.py:385
  88.7 0.7 collective-permute-start.34
  89.5 1.3 collective-permute-start.33
  90.8 4.0 %collective-permute-done.36.refs_1_ = bf16[3,64,1024]{2,1,0:T(8,128)(2,1)S(1)} collective-permute-done((bf16[3,64,1024]{2,1,0:T(8,128)(2,1)S(1)}, bf16[3,64,1024]{2,1,0:T(8,128)(2,1)S(1)}, u32[]{:S(2)}, u32[]{:S(2)}) %collective-permute-start.36) | collective-permute-done | bytes 393248 | tf_op jit(solution)/shard_map/ppermute | solution.py:385
  95.0 2.8 %collective-permute-start.38 = (bf16[3,64,1024]{2,1,0:T(8,128)(2,1)S(1)}, bf16[3,64,1024]{2,1,0:T(8,128)(2,1)S(1)}, u32[]{:S(2)}, u32[]{:S(2)}) collective-permute-start(bf16[3,64,1024]{2,1,0:T(8,128)(2,1)S(1)} %activations.7.refs_1_.refs_2_), channel_id=1, source_target_pairs={{0,1},{3,2},{4,5},{7,6},{8,9},{11,10},{12,13},{15,14},{16,17},{19,... | collective-permute-start | bytes 1179656 | tf_op jit(solution)/shard_map/ppermute | solution.py:385
  97.9 0.7 collective-permute-start.37
  98.6 1.3 collective-permute-start.43
  99.9 3.7 %collective-permute-done.33.refs_0_ = bf16[3,64,1024]{2,1,0:T(8,128)(2,1)S(1)} collective-permute-done((bf16[3,64,1024]{2,1,0:T(8,128)(2,1)S(1)}, bf16[3,64,1024]{2,1,0:T(8,128)(2,1)S(1)}, u32[]{:S(2)}, u32[]{:S(2)}) %collective-permute-start.33) | collective-permute-done | bytes 393248 | tf_op jit(solution)/shard_map/ppermute | solution.py:385
  103.5 0.7 collective-permute-done.38.refs_0_
  104.2 0.7 collective-permute-start.45
  104.9 1.3 collective-permute-start.44
  106.2 3.5 %backward_products.4 = (bf16[2,128,1024]{2,1,0:T(8,128)(2,1)S(1)}, bf16[3,128,1024]{2,1,0:T(8,128)(2,1)S(1)}, bf16[64,1024]{1,0:T(8,128)(2,1)S(1)}, bf16[64,1024...) custom-call(s32[1]{0:T(128)} %bitcast.1.refs_0_, s32[1]{0:T(128)} %bitcast.2.refs_1_, ...), custom_call_target="tpu_custom_call" | custom-call | flops 1000 | bytes 1000 | tf_op jit(solution)/shard_map/backward_products/pallas_call | solution.py:36
  109.8 2.5 %collective-permute-done.43.refs_0_ = bf16[3,64,1024]{2,1,0:T(8,128)(2,1)S(1)} collective-permute-done((bf16[3,64,1024]{2,1,0:T(8,128)(2,1)S(1)}, bf16[3,64,1024]{2,1,0:T(8,128)(2,1)S(1)}, u32[]{:S(2)}, u32[]{:S(2)}) %collective-permute-start.43) | collective-permute-done | bytes 393248 | tf_op jit(solution)/shard_map/ppermute | solution.py:385
  112.3 3.7 %backward_products.5 = (bf16[2,128,1024]{2,1,0:T(8,128)(2,1)S(1)}, bf16[3,128,1024]{2,1,0:T(8,128)(2,1)S(1)}, bf16[64,1024]{1,0:T(8,128)(2,1)S(1)}, bf16[64,1024...) custom-call(s32[1]{0:T(128)} %bitcast.1.refs_0_, s32[1]{0:T(128)} %bitcast.2.refs_1_, ...), custom_call_target="tpu_custom_call" | custom-call | flops 1000 | bytes 1000 | tf_op jit(solution)/shard_map/backward_products/pallas_call | solution.py:36
  116.0 1.3 collective-permute-start.50
  118.0 2.4 %collective-permute-done.44.refs_0_ = bf16[3,64,1024]{2,1,0:T(8,128)(2,1)S(1)} collective-permute-done((bf16[3,64,1024]{2,1,0:T(8,128)(2,1)S(1)}, bf16[3,64,1024]{2,1,0:T(8,128)(2,1)S(1)}, u32[]{:S(2)}, u32[]{:S(2)}) %collective-permute-start.44) | collective-permute-done | bytes 393248 | tf_op jit(solution)/shard_map/ppermute | solution.py:385
  120.4 1.3 collective-permute-done.49.refs_4_
  121.8 3.5 %backward_products.6 = (bf16[2,128,1024]{2,1,0:T(8,128)(2,1)S(1)}, bf16[3,128,1024]{2,1,0:T(8,128)(2,1)S(1)}, bf16[64,1024]{1,0:T(8,128)(2,1)S(1)}, bf16[64,1024...) custom-call(s32[1]{0:T(128)} %bitcast.1.refs_0_, s32[1]{0:T(128)} %bitcast.2.refs_1_, ...), custom_call_target="tpu_custom_call" | custom-call | flops 1000 | bytes 1000 | tf_op jit(solution)/shard_map/backward_products/pallas_call | solution.py:36
  128.1 3.5 %backward_products.7 = (bf16[2,128,1024]{2,1,0:T(8,128)(2,1)S(1)}, bf16[3,128,1024]{2,1,0:T(8,128)(2,1)S(1)}, bf16[64,1024]{1,0:T(8,128)(2,1)S(1)}, bf16[64,1024...) custom-call(s32[1]{0:T(128)} %bitcast.1.refs_0_, s32[1]{0:T(128)} %bitcast.2.refs_1_, ...), custom_call_target="tpu_custom_call" | custom-call | flops 1000 | bytes 1000 | tf_op jit(solution)/shard_map/backward_products/pallas_call | solution.py:36
  131.7 0.6 collective-permute-start.59
  132.5 1.0 collective-permute-start.60
  134.1 0.8 collective-permute-done.57.refs_3_
  135.5 2.0 %collective-permute-start.61 = (bf16[1,128,1024]{2,1,0:T(8,128)(2,1)S(1)}, bf16[1,128,1024]{2,1,0:T(8,128)(2,1)S(1)}, u32[]{:S(2)}, u32[]{:S(2)}) collective-permute-start(bf16[1,128,1024]{2,1,0:T(8,128)(2,1)S(1)} %get-tuple-element.109.refs_25_), channel_id=1, source_target_pairs={{0,12},{4,8},{8,4},{12,0},{1,13},{5,9},{9,5},{13,1},{2,14},{6,10},... | collective-permute-start | bytes 786440 | tf_op jit(solution)/shard_map/ppermute | solution.py:51
  137.5 1.0 collective-permute-start.62
  138.5 10.0 %weight_grads.1 = (bf16[16,128]{1,0:T(8,128)(2,1)S(1)}, f32[2048,1024]{1,0:T(8,128)}, f32[2048,1024]{1,0:T(8,128)}, f32[2048,1024]{1,0:T(8,128)}) custom-call(s32[1]{0:T(128)} %bitcast.1.refs_0_, bf16[2,128,1024]{2,1,0:T(8,128)(2,1)S(1)} %ordered_rows.1.refs_0_.refs_1_, bf16[2,128,1024]{2,1,0:T(8,128)(2,1)S(1)} %pass_on.19.refs_0_.refs_1_.refs_2_, ...), custom_call_target="tpu_custom_call" | custom-call | flops 1000 | bytes 1000 | tf_op jit(solution)/shard_map/weight_grads/pallas_call | solution.py:36
  148.7 4.0 %collective-permute-done.61.refs_0_ = bf16[1,128,1024]{2,1,0:T(8,128)(2,1)S(1)} collective-permute-done((bf16[1,128,1024]{2,1,0:T(8,128)(2,1)S(1)}, bf16[1,128,1024]{2,1,0:T(8,128)(2,1)S(1)}, u32[]{:S(2)}, u32[]{:S(2)}) %collective-permute-start.61) | collective-permute-done | bytes 262176 | tf_op jit(solution)/shard_map/ppermute | solution.py:51
  152.7 5.2 %collective-permute-done.62.refs_0_ = bf16[1,128,1024]{2,1,0:T(8,128)(2,1)S(1)} collective-permute-done((bf16[1,128,1024]{2,1,0:T(8,128)(2,1)S(1)}, bf16[1,128,1024]{2,1,0:T(8,128)(2,1)S(1)}, u32[]{:S(2)}, u32[]{:S(2)}) %collective-permute-start.62) | collective-permute-done | bytes 262176 | tf_op jit(solution)/shard_map/ppermute | solution.py:51
  157.9 1.0 final_sum.1
  (128 shorter events, 10.4 us)
Async XLA Ops:
  3.3 16.6 %collective-permute-start.6 = (bf16[2,128,1024]{2,1,0:T(8,128)(2,1)S(1)}, bf16[2,128,1024]{2,1,0:T(8,128)(2,1)S(1)}, u32[]{:S(2)}, u32[]{:S(2)}) collective-permute-start(bf16[2,128,1024]{2,1,0:T(8,128)(2,1)S(1)} %ordered_rows.1.refs_0_.refs_1_), channel_id=1, source_target_pairs={{0,4},{4,0},{8,12},{12,8},{1,5},{5,1},{9,13},{13,9},{2,6},{6,2},{1... | collective-permute-start | bytes 1572872 | tf_op jit(solution)/shard_map/ppermute | solution.py:51
  6.3 13.7 %collective-permute-start.5 = (bf16[2,128,1024]{2,1,0:T(8,128)(2,1)S(1)}, bf16[2,128,1024]{2,1,0:T(8,128)(2,1)S(1)}, u32[]{:S(2)}, u32[]{:S(2)}) collective-permute-start(bf16[2,128,1024]{2,1,0:T(8,128)(2,1)S(1)} %ordered_rows.1.refs_0_.refs_1_), channel_id=1, source_target_pairs={{0,8},{4,12},{8,0},{12,4},{1,9},{5,13},{9,1},{13,5},{2,10},{6,14},... | collective-permute-start | bytes 1572872 | tf_op jit(solution)/shard_map/ppermute | solution.py:51
  7.8 1.4 collective-permute-start
  7.9 1.5 collective-permute-start.1
  8.4 1.3 collective-permute-start.2
  9.3 1.3 collective-permute-start.3
  17.2 9.8 %copy-start.5 = (bf16[2048,1024]{1,0:T(8,128)(2,1)S(1)}, bf16[2048,1024]{1,0:T(8,128)(2,1)}, u32[]{:S(2)}) copy-start(bf16[2048,1024]{1,0:T(8,128)(2,1)} %refs_8_.15) | copy-start | bytes 12582916
  20.0 4.5 %collective-permute-start.7 = (bf16[64,1024]{1,0:T(8,128)(2,1)S(1)}, bf16[64,1024]{1,0:T(8,128)(2,1)S(1)}, u32[]{:S(2)}, u32[]{:S(2)}) collective-permute-start(bf16[64,1024]{1,0:T(8,128)(2,1)S(1)} %get-tuple-element.68.refs_9_), channel_id=1, source_target_pairs={{0,16},{16,0},{1,17},{17,1},{2,18},{18,2},{3,19},{19,3},{4,20},{20... | collective-permute-start | bytes 393224 | tf_op jit(solution)/shard_map/ppermute | solution.py:51
  20.3 12.5 %collective-permute-start.4 = (bf16[3,64,1024]{2,1,0:T(8,128)(2,1)S(1)}, bf16[3,64,1024]{2,1,0:T(8,128)(2,1)S(1)}, u32[]{:S(2)}, u32[]{:S(2)}) collective-permute-start(bf16[3,64,1024]{2,1,0:T(8,128)(2,1)S(1)} %get-tuple-element.66.refs_0_), channel_id=1, source_target_pairs={{0,1},{3,2},{4,5},{7,6},{8,9},{11,10},{12,13},{15,14},{16,17},{19,... | collective-permute-start | bytes 1179656 | tf_op jit(solution)/shard_map/ppermute | solution.py:385
  23.9 1.4 collective-permute-start.11
  24.0 2.3 %collective-permute-start.12 = (bf16[64,1024]{1,0:T(8,128)(2,1)S(1)}, bf16[64,1024]{1,0:T(8,128)(2,1)S(1)}, u32[]{:S(2)}, u32[]{:S(2)}) collective-permute-start(bf16[64,1024]{1,0:T(8,128)(2,1)S(1)} %get-tuple-element.72), channel_id=1, source_target_pairs={{0,16},{16,0},{1,17},{17,1},{2,18},{18,2},{3,19},{19,3},{4,20},{20... | collective-permute-start | bytes 393224 | tf_op jit(solution)/shard_map/ppermute | solution.py:51
  24.5 1.9 %collective-permute-start.13 = (bf16[64,1024]{1,0:T(8,128)(2,1)S(1)}, bf16[64,1024]{1,0:T(8,128)(2,1)S(1)}, u32[]{:S(2)}, u32[]{:S(2)}) collective-permute-start(bf16[64,1024]{1,0:T(8,128)(2,1)S(1)} %get-tuple-element.73), channel_id=1, source_target_pairs={{0,16},{16,0},{1,17},{17,1},{2,18},{18,2},{3,19},{19,3},{4,20},{20... | collective-permute-start | bytes 393224 | tf_op jit(solution)/shard_map/ppermute | solution.py:51
  24.6 2.3 %collective-permute-start.14 = (bf16[64,1024]{1,0:T(8,128)(2,1)S(1)}, bf16[64,1024]{1,0:T(8,128)(2,1)S(1)}, u32[]{:S(2)}, u32[]{:S(2)}) collective-permute-start(bf16[64,1024]{1,0:T(8,128)(2,1)S(1)} %get-tuple-element.74), channel_id=1, source_target_pairs={{0,16},{16,0},{1,17},{17,1},{2,18},{18,2},{3,19},{19,3},{4,20},{20... | collective-permute-start | bytes 393224 | tf_op jit(solution)/shard_map/ppermute | solution.py:51
  25.3 16.8 %collective-permute-start.17 = (bf16[2,128,1024]{2,1,0:T(8,128)(2,1)S(1)}, bf16[2,128,1024]{2,1,0:T(8,128)(2,1)S(1)}, u32[]{:S(2)}, u32[]{:S(2)}) collective-permute-start(bf16[2,128,1024]{2,1,0:T(8,128)(2,1)S(1)} %pass_on.19.refs_0_.refs_1_.refs_2_), channel_id=1, source_target_pairs={{0,8},{4,12},{8,0},{12,4},{1,9},{5,13},{9,1},{13,5},{2,10},{6,14},... | collective-permute-start | bytes 1572872 | tf_op jit(solution)/shard_map/ppermute | solution.py:51
  26.4 3.3 %collective-permute-start.8 = (bf16[64,1024]{1,0:T(8,128)(2,1)S(1)}, bf16[64,1024]{1,0:T(8,128)(2,1)S(1)}, u32[]{:S(2)}, u32[]{:S(2)}) collective-permute-start(bf16[64,1024]{1,0:T(8,128)(2,1)S(1)} %get-tuple-element.69), channel_id=1, source_target_pairs={{0,16},{16,0},{1,17},{17,1},{2,18},{18,2},{3,19},{19,3},{4,20},{20... | collective-permute-start | bytes 393224 | tf_op jit(solution)/shard_map/ppermute | solution.py:51
  26.4 3.3 %collective-permute-start.9 = (bf16[64,1024]{1,0:T(8,128)(2,1)S(1)}, bf16[64,1024]{1,0:T(8,128)(2,1)S(1)}, u32[]{:S(2)}, u32[]{:S(2)}) collective-permute-start(bf16[64,1024]{1,0:T(8,128)(2,1)S(1)} %get-tuple-element.70), channel_id=1, source_target_pairs={{0,16},{16,0},{1,17},{17,1},{2,18},{18,2},{3,19},{19,3},{4,20},{20... | collective-permute-start | bytes 393224 | tf_op jit(solution)/shard_map/ppermute | solution.py:51
  26.9 2.8 %collective-permute-start.10 = (bf16[64,1024]{1,0:T(8,128)(2,1)S(1)}, bf16[64,1024]{1,0:T(8,128)(2,1)S(1)}, u32[]{:S(2)}, u32[]{:S(2)}) collective-permute-start(bf16[64,1024]{1,0:T(8,128)(2,1)S(1)} %get-tuple-element.71), channel_id=1, source_target_pairs={{0,16},{16,0},{1,17},{17,1},{2,18},{18,2},{3,19},{19,3},{4,20},{20... | collective-permute-start | bytes 393224 | tf_op jit(solution)/shard_map/ppermute | solution.py:51
  32.8 9.9 %collective-permute-start.15 = (bf16[3,64,1024]{2,1,0:T(8,128)(2,1)S(1)}, bf16[3,64,1024]{2,1,0:T(8,128)(2,1)S(1)}, u32[]{:S(2)}, u32[]{:S(2)}) collective-permute-start(bf16[3,64,1024]{2,1,0:T(8,128)(2,1)S(1)} %add_on.8.refs_1_), channel_id=1, source_target_pairs={{1,2},{2,1},{5,6},{6,5},{9,10},{10,9},{13,14},{14,13},{17,18},{18,... | collective-permute-start | bytes 1179656 | tf_op jit(solution)/shard_map/ppermute | solution.py:385
  33.5 16.7 %collective-permute-start.16 = (bf16[3,64,1024]{2,1,0:T(8,128)(2,1)S(1)}, bf16[3,64,1024]{2,1,0:T(8,128)(2,1)S(1)}, u32[]{:S(2)}, u32[]{:S(2)}) collective-permute-start(bf16[3,64,1024]{2,1,0:T(8,128)(2,1)S(1)} %get-tuple-element.77.refs_0_), channel_id=1, source_target_pairs={{0,1},{3,2},{4,5},{7,6},{8,9},{11,10},{12,13},{15,14},{16,17},{19,... | collective-permute-start | bytes 1179656 | tf_op jit(solution)/shard_map/ppermute | solution.py:385
  40.7 20.6 %collective-permute-start.20 = (bf16[3,64,1024]{2,1,0:T(8,128)(2,1)S(1)}, bf16[3,64,1024]{2,1,0:T(8,128)(2,1)S(1)}, u32[]{:S(2)}, u32[]{:S(2)}) collective-permute-start(bf16[3,64,1024]{2,1,0:T(8,128)(2,1)S(1)} %get-tuple-element.79.refs_0_), channel_id=1, source_target_pairs={{0,1},{3,2},{4,5},{7,6},{8,9},{11,10},{12,13},{15,14},{16,17},{19,... | collective-permute-start | bytes 1179656 | tf_op jit(solution)/shard_map/ppermute | solution.py:385
  42.1 8.4 %collective-permute-start.21 = (bf16[64,1024]{1,0:T(8,128)(2,1)S(1)}, bf16[64,1024]{1,0:T(8,128)(2,1)S(1)}, u32[]{:S(2)}, u32[]{:S(2)}) collective-permute-start(bf16[64,1024]{1,0:T(8,128)(2,1)S(1)} %get-tuple-element.78.refs_2_), channel_id=1, source_target_pairs={{0,16},{16,0},{1,17},{17,1},{2,18},{18,2},{3,19},{19,3},{4,20},{20... | collective-permute-start | bytes 393224 | tf_op jit(solution)/shard_map/ppermute | solution.py:51
  42.2 9.0 %collective-permute-start.22 = (bf16[64,1024]{1,0:T(8,128)(2,1)S(1)}, bf16[64,1024]{1,0:T(8,128)(2,1)S(1)}, u32[]{:S(2)}, u32[]{:S(2)}) collective-permute-start(bf16[64,1024]{1,0:T(8,128)(2,1)S(1)} %get-tuple-element.80), channel_id=1, source_target_pairs={{0,16},{16,0},{1,17},{17,1},{2,18},{18,2},{3,19},{19,3},{4,20},{20... | collective-permute-start | bytes 393224 | tf_op jit(solution)/shard_map/ppermute | solution.py:51
  42.7 9.8 %collective-permute-start.23 = (bf16[64,1024]{1,0:T(8,128)(2,1)S(1)}, bf16[64,1024]{1,0:T(8,128)(2,1)S(1)}, u32[]{:S(2)}, u32[]{:S(2)}) collective-permute-start(bf16[64,1024]{1,0:T(8,128)(2,1)S(1)} %get-tuple-element.81), channel_id=1, source_target_pairs={{0,16},{16,0},{1,17},{17,1},{2,18},{18,2},{3,19},{19,3},{4,20},{20... | collective-permute-start | bytes 393224 | tf_op jit(solution)/shard_map/ppermute | solution.py:51
  50.3 2.2 %collective-permute-start.24 = (bf16[64,1024]{1,0:T(8,128)(2,1)S(1)}, bf16[64,1024]{1,0:T(8,128)(2,1)S(1)}, u32[]{:S(2)}, u32[]{:S(2)}) collective-permute-start(bf16[64,1024]{1,0:T(8,128)(2,1)S(1)} %get-tuple-element.82), channel_id=1, source_target_pairs={{0,16},{16,0},{1,17},{17,1},{2,18},{18,2},{3,19},{19,3},{4,20},{20... | collective-permute-start | bytes 393224 | tf_op jit(solution)/shard_map/ppermute | solution.py:51
  50.5 11.7 %collective-permute-start.19 = (bf16[3,64,1024]{2,1,0:T(8,128)(2,1)S(1)}, bf16[3,64,1024]{2,1,0:T(8,128)(2,1)S(1)}, u32[]{:S(2)}, u32[]{:S(2)}) collective-permute-start(bf16[3,64,1024]{2,1,0:T(8,128)(2,1)S(1)} %add_on.9.refs_2_), channel_id=1, source_target_pairs={{1,2},{2,1},{5,6},{6,5},{9,10},{10,9},{13,14},{14,13},{17,18},{18,... | collective-permute-start | bytes 1179656 | tf_op jit(solution)/shard_map/ppermute | solution.py:385
  51.2 14.9 %collective-permute-start.18 = (bf16[3,64,1024]{2,1,0:T(8,128)(2,1)S(1)}, bf16[3,64,1024]{2,1,0:T(8,128)(2,1)S(1)}, u32[]{:S(2)}, u32[]{:S(2)}) collective-permute-start(bf16[3,64,1024]{2,1,0:T(8,128)(2,1)S(1)} %add_on.10.refs_9_), channel_id=1, source_target_pairs={{2,3},{1,0},{6,7},{5,4},{10,11},{9,8},{14,15},{13,12},{18,19},{17,... | collective-permute-start | bytes 1179656 | tf_op jit(solution)/shard_map/ppermute | solution.py:385
  55.2 15.2 %collective-permute-start.28 = (bf16[3,64,1024]{2,1,0:T(8,128)(2,1)S(1)}, bf16[3,64,1024]{2,1,0:T(8,128)(2,1)S(1)}, u32[]{:S(2)}, u32[]{:S(2)}) collective-permute-start(bf16[3,64,1024]{2,1,0:T(8,128)(2,1)S(1)} %get-tuple-element.84.refs_0_), channel_id=1, source_target_pairs={{0,1},{3,2},{4,5},{7,6},{8,9},{11,10},{12,13},{15,14},{16,17},{19,... | collective-permute-start | bytes 1179656 | tf_op jit(solution)/shard_map/ppermute | solution.py:385
  61.5 9.7 %collective-permute-start.27 = (bf16[3,64,1024]{2,1,0:T(8,128)(2,1)S(1)}, bf16[3,64,1024]{2,1,0:T(8,128)(2,1)S(1)}, u32[]{:S(2)}, u32[]{:S(2)}) collective-permute-start(bf16[3,64,1024]{2,1,0:T(8,128)(2,1)S(1)} %add_on.11.refs_2_), channel_id=1, source_target_pairs={{1,2},{2,1},{5,6},{6,5},{9,10},{10,9},{13,14},{14,13},{17,18},{18,... | collective-permute-start | bytes 1179656 | tf_op jit(solution)/shard_map/ppermute | solution.py:385
  62.3 14.5 %collective-permute-start.26 = (bf16[3,64,1024]{2,1,0:T(8,128)(2,1)S(1)}, bf16[3,64,1024]{2,1,0:T(8,128)(2,1)S(1)}, u32[]{:S(2)}, u32[]{:S(2)}) collective-permute-start(bf16[3,64,1024]{2,1,0:T(8,128)(2,1)S(1)} %add_on.12.refs_2_), channel_id=1, source_target_pairs={{2,3},{1,0},{6,7},{5,4},{10,11},{9,8},{14,15},{13,12},{18,19},{17,... | collective-permute-start | bytes 1179656 | tf_op jit(solution)/shard_map/ppermute | solution.py:385
  66.4 14.1 %collective-permute-start.25 = (bf16[3,64,1024]{2,1,0:T(8,128)(2,1)S(1)}, bf16[3,64,1024]{2,1,0:T(8,128)(2,1)S(1)}, u32[]{:S(2)}, u32[]{:S(2)}) collective-permute-start(bf16[3,64,1024]{2,1,0:T(8,128)(2,1)S(1)} %activations.4.refs_2_), channel_id=1, source_target_pairs={{0,1},{3,2},{4,5},{7,6},{8,9},{11,10},{12,13},{15,14},{16,17},{19,... | collective-permute-start | bytes 1179656 | tf_op jit(solution)/shard_map/ppermute | solution.py:385
  70.5 10.7 %collective-permute-start.32 = (bf16[3,64,1024]{2,1,0:T(8,128)(2,1)S(1)}, bf16[3,64,1024]{2,1,0:T(8,128)(2,1)S(1)}, u32[]{:S(2)}, u32[]{:S(2)}) collective-permute-start(bf16[3,64,1024]{2,1,0:T(8,128)(2,1)S(1)} %add_on.13.refs_2_), channel_id=1, source_target_pairs={{1,2},{2,1},{5,6},{6,5},{9,10},{10,9},{13,14},{14,13},{17,18},{18,... | collective-permute-start | bytes 1179656 | tf_op jit(solution)/shard_map/ppermute | solution.py:385
  71.3 14.7 %collective-permute-start.31 = (bf16[3,64,1024]{2,1,0:T(8,128)(2,1)S(1)}, bf16[3,64,1024]{2,1,0:T(8,128)(2,1)S(1)}, u32[]{:S(2)}, u32[]{:S(2)}) collective-permute-start(bf16[3,64,1024]{2,1,0:T(8,128)(2,1)S(1)} %add_on.14.refs_2_), channel_id=1, source_target_pairs={{2,3},{1,0},{6,7},{5,4},{10,11},{9,8},{14,15},{13,12},{18,19},{17,... | collective-permute-start | bytes 1179656 | tf_op jit(solution)/shard_map/ppermute | solution.py:385
  77.0 11.8 %collective-permute-start.30 = (bf16[3,64,1024]{2,1,0:T(8,128)(2,1)S(1)}, bf16[3,64,1024]{2,1,0:T(8,128)(2,1)S(1)}, u32[]{:S(2)}, u32[]{:S(2)}) collective-permute-start(bf16[3,64,1024]{2,1,0:T(8,128)(2,1)S(1)} %activations.5.refs_1_.refs_2_), channel_id=1, source_target_pairs={{0,1},{3,2},{4,5},{7,6},{8,9},{11,10},{12,13},{15,14},{16,17},{19,... | collective-permute-start | bytes 1179656 | tf_op jit(solution)/shard_map/ppermute | solution.py:385
  80.5 9.0 %collective-permute-start.29 = (bf16[3,64,1024]{2,1,0:T(8,128)(2,1)S(1)}, bf16[3,64,1024]{2,1,0:T(8,128)(2,1)S(1)}, u32[]{:S(2)}, u32[]{:S(2)}) collective-permute-start(bf16[3,64,1024]{2,1,0:T(8,128)(2,1)S(1)} %pass_on.22.refs_2_.refs_3_), channel_id=1, source_target_pairs={{1,2},{2,1},{5,6},{6,5},{9,10},{10,9},{13,14},{14,13},{17,18},{18,... | collective-permute-start | bytes 1179656 | tf_op jit(solution)/shard_map/ppermute | solution.py:385
  81.3 13.5 %collective-permute-start.36 = (bf16[3,64,1024]{2,1,0:T(8,128)(2,1)S(1)}, bf16[3,64,1024]{2,1,0:T(8,128)(2,1)S(1)}, u32[]{:S(2)}, u32[]{:S(2)}) collective-permute-start(bf16[3,64,1024]{2,1,0:T(8,128)(2,1)S(1)} %add_on.15.refs_2_), channel_id=1, source_target_pairs={{2,3},{1,0},{6,7},{5,4},{10,11},{9,8},{14,15},{13,12},{18,19},{17,... | collective-permute-start | bytes 1179656 | tf_op jit(solution)/shard_map/ppermute | solution.py:385
  86.2 11.6 %collective-permute-start.35 = (bf16[3,64,1024]{2,1,0:T(8,128)(2,1)S(1)}, bf16[3,64,1024]{2,1,0:T(8,128)(2,1)S(1)}, u32[]{:S(2)}, u32[]{:S(2)}) collective-permute-start(bf16[3,64,1024]{2,1,0:T(8,128)(2,1)S(1)} %activations.6.refs_1_.refs_2_), channel_id=1, source_target_pairs={{0,1},{3,2},{4,5},{7,6},{8,9},{11,10},{12,13},{15,14},{16,17},{19,... | collective-permute-start | bytes 1179656 | tf_op jit(solution)/shard_map/ppermute | solution.py:385
  88.7 9.8 %collective-permute-start.34 = (bf16[3,64,1024]{2,1,0:T(8,128)(2,1)S(1)}, bf16[3,64,1024]{2,1,0:T(8,128)(2,1)S(1)}, u32[]{:S(2)}, u32[]{:S(2)}) collective-permute-start(bf16[3,64,1024]{2,1,0:T(8,128)(2,1)S(1)} %pass_on.23.refs_1_.refs_3_), channel_id=1, source_target_pairs={{1,2},{2,1},{5,6},{6,5},{9,10},{10,9},{13,14},{14,13},{17,18},{18,... | collective-permute-start | bytes 1179656 | tf_op jit(solution)/shard_map/ppermute | solution.py:385
  89.5 14.1 %collective-permute-start.33 = (bf16[3,64,1024]{2,1,0:T(8,128)(2,1)S(1)}, bf16[3,64,1024]{2,1,0:T(8,128)(2,1)S(1)}, u32[]{:S(2)}, u32[]{:S(2)}) collective-permute-start(bf16[3,64,1024]{2,1,0:T(8,128)(2,1)S(1)} %pass_on.24.refs_2_.refs_4_), channel_id=1, source_target_pairs={{2,3},{1,0},{6,7},{5,4},{10,11},{9,8},{14,15},{13,12},{18,19},{17,... | collective-permute-start | bytes 1179656 | tf_op jit(solution)/shard_map/ppermute | solution.py:385
  95.0 9.2 %collective-permute-start.38 = (bf16[3,64,1024]{2,1,0:T(8,128)(2,1)S(1)}, bf16[3,64,1024]{2,1,0:T(8,128)(2,1)S(1)}, u32[]{:S(2)}, u32[]{:S(2)}) collective-permute-start(bf16[3,64,1024]{2,1,0:T(8,128)(2,1)S(1)} %activations.7.refs_1_.refs_2_), channel_id=1, source_target_pairs={{0,1},{3,2},{4,5},{7,6},{8,9},{11,10},{12,13},{15,14},{16,17},{19,... | collective-permute-start | bytes 1179656 | tf_op jit(solution)/shard_map/ppermute | solution.py:385
  97.9 7.1 %collective-permute-start.37 = (bf16[3,64,1024]{2,1,0:T(8,128)(2,1)S(1)}, bf16[3,64,1024]{2,1,0:T(8,128)(2,1)S(1)}, u32[]{:S(2)}, u32[]{:S(2)}) collective-permute-start(bf16[3,64,1024]{2,1,0:T(8,128)(2,1)S(1)} %pass_on.25.refs_1_.refs_3_), channel_id=1, source_target_pairs={{1,2},{2,1},{5,6},{6,5},{9,10},{10,9},{13,14},{14,13},{17,18},{18,... | collective-permute-start | bytes 1179656 | tf_op jit(solution)/shard_map/ppermute | solution.py:385
  98.6 13.7 %collective-permute-start.43 = (bf16[3,64,1024]{2,1,0:T(8,128)(2,1)S(1)}, bf16[3,64,1024]{2,1,0:T(8,128)(2,1)S(1)}, u32[]{:S(2)}, u32[]{:S(2)}) collective-permute-start(bf16[3,64,1024]{2,1,0:T(8,128)(2,1)S(1)} %pass_on.26.refs_1_.refs_4_), channel_id=1, source_target_pairs={{2,3},{1,0},{6,7},{5,4},{10,11},{9,8},{14,15},{13,12},{18,19},{17,... | collective-permute-start | bytes 1179656 | tf_op jit(solution)/shard_map/ppermute | solution.py:385
  104.2 11.8 %collective-permute-start.45 = (bf16[3,64,1024]{2,1,0:T(8,128)(2,1)S(1)}, bf16[3,64,1024]{2,1,0:T(8,128)(2,1)S(1)}, u32[]{:S(2)}, u32[]{:S(2)}) collective-permute-start(bf16[3,64,1024]{2,1,0:T(8,128)(2,1)S(1)} %pass_on.28.refs_1_.refs_3_), channel_id=1, source_target_pairs={{1,2},{2,1},{5,6},{6,5},{9,10},{10,9},{13,14},{14,13},{17,18},{18,... | collective-permute-start | bytes 1179656 | tf_op jit(solution)/shard_map/ppermute | solution.py:385
  104.9 15.4 %collective-permute-start.44 = (bf16[3,64,1024]{2,1,0:T(8,128)(2,1)S(1)}, bf16[3,64,1024]{2,1,0:T(8,128)(2,1)S(1)}, u32[]{:S(2)}, u32[]{:S(2)}) collective-permute-start(bf16[3,64,1024]{2,1,0:T(8,128)(2,1)S(1)} %pass_on.29.refs_9_.refs_4_), channel_id=1, source_target_pairs={{2,3},{1,0},{6,7},{5,4},{10,11},{9,8},{14,15},{13,12},{18,19},{17,... | collective-permute-start | bytes 1179656 | tf_op jit(solution)/shard_map/ppermute | solution.py:385
  116.0 12.1 %collective-permute-start.50 = (bf16[3,64,1024]{2,1,0:T(8,128)(2,1)S(1)}, bf16[3,64,1024]{2,1,0:T(8,128)(2,1)S(1)}, u32[]{:S(2)}, u32[]{:S(2)}) collective-permute-start(bf16[3,64,1024]{2,1,0:T(8,128)(2,1)S(1)} %pass_on.31.refs_1_.refs_4_), channel_id=1, source_target_pairs={{2,3},{1,0},{6,7},{5,4},{10,11},{9,8},{14,15},{13,12},{18,19},{17,... | collective-permute-start | bytes 1179656 | tf_op jit(solution)/shard_map/ppermute | solution.py:385
  117.3 3.0 %collective-permute-start.46 = (bf16[64,1024]{1,0:T(8,128)(2,1)S(1)}, bf16[64,1024]{1,0:T(8,128)(2,1)S(1)}, u32[]{:S(2)}, u32[]{:S(2)}) collective-permute-start(bf16[64,1024]{1,0:T(8,128)(2,1)S(1)} %get-tuple-element.93), channel_id=1, source_target_pairs={{0,16},{16,0},{1,17},{17,1},{2,18},{18,2},{3,19},{19,3},{4,20},{20... | collective-permute-start | bytes 393224 | tf_op jit(solution)/shard_map/ppermute | solution.py:51
  117.4 2.9 %collective-permute-start.47 = (bf16[64,1024]{1,0:T(8,128)(2,1)S(1)}, bf16[64,1024]{1,0:T(8,128)(2,1)S(1)}, u32[]{:S(2)}, u32[]{:S(2)}) collective-permute-start(bf16[64,1024]{1,0:T(8,128)(2,1)S(1)} %get-tuple-element.94), channel_id=1, source_target_pairs={{0,16},{16,0},{1,17},{17,1},{2,18},{18,2},{3,19},{19,3},{4,20},{20... | collective-permute-start | bytes 393224 | tf_op jit(solution)/shard_map/ppermute | solution.py:51
  117.9 2.5 %collective-permute-start.48 = (bf16[64,1024]{1,0:T(8,128)(2,1)S(1)}, bf16[64,1024]{1,0:T(8,128)(2,1)S(1)}, u32[]{:S(2)}, u32[]{:S(2)}) collective-permute-start(bf16[64,1024]{1,0:T(8,128)(2,1)S(1)} %get-tuple-element.95), channel_id=1, source_target_pairs={{0,16},{16,0},{1,17},{17,1},{2,18},{18,2},{3,19},{19,3},{4,20},{20... | collective-permute-start | bytes 393224 | tf_op jit(solution)/shard_map/ppermute | solution.py:51
  120.4 1.3 collective-permute-start.49
  125.4 1.4 collective-permute-start.51
  125.6 1.4 collective-permute-start.52
  126.0 1.3 collective-permute-start.53
  126.1 1.4 collective-permute-start.54
  131.6 2.0 %collective-permute-start.55 = (bf16[64,1024]{1,0:T(8,128)(2,1)S(1)}, bf16[64,1024]{1,0:T(8,128)(2,1)S(1)}, u32[]{:S(2)}, u32[]{:S(2)}) collective-permute-start(bf16[64,1024]{1,0:T(8,128)(2,1)S(1)} %get-tuple-element.105), channel_id=1, source_target_pairs={{0,16},{16,0},{1,17},{17,1},{2,18},{18,2},{3,19},{19,3},{4,20},{20... | collective-permute-start | bytes 393224 | tf_op jit(solution)/shard_map/ppermute | solution.py:51
  131.7 16.9 %collective-permute-start.59 = (bf16[2,128,1024]{2,1,0:T(8,128)(2,1)S(1)}, bf16[2,128,1024]{2,1,0:T(8,128)(2,1)S(1)}, u32[]{:S(2)}, u32[]{:S(2)}) collective-permute-start(bf16[2,128,1024]{2,1,0:T(8,128)(2,1)S(1)} %add_quarters.4.refs_9_), channel_id=1, source_target_pairs={{0,4},{4,0},{8,12},{12,8},{1,5},{5,1},{9,13},{13,9},{2,6},{6,2},{1... | collective-permute-start | bytes 1572872 | tf_op jit(solution)/shard_map/ppermute | solution.py:51
  132.3 1.7 %collective-permute-start.56 = (bf16[64,1024]{1,0:T(8,128)(2,1)S(1)}, bf16[64,1024]{1,0:T(8,128)(2,1)S(1)}, u32[]{:S(2)}, u32[]{:S(2)}) collective-permute-start(bf16[64,1024]{1,0:T(8,128)(2,1)S(1)} %get-tuple-element.106), channel_id=1, source_target_pairs={{0,16},{16,0},{1,17},{17,1},{2,18},{18,2},{3,19},{19,3},{4,20},{20... | collective-permute-start | bytes 393224 | tf_op jit(solution)/shard_map/ppermute | solution.py:51
  132.5 16.2 %collective-permute-start.60 = (bf16[2,128,1024]{2,1,0:T(8,128)(2,1)S(1)}, bf16[2,128,1024]{2,1,0:T(8,128)(2,1)S(1)}, u32[]{:S(2)}, u32[]{:S(2)}) collective-permute-start(bf16[2,128,1024]{2,1,0:T(8,128)(2,1)S(1)} %add_quarters.5.refs_1_), channel_id=1, source_target_pairs={{0,8},{4,12},{8,0},{12,4},{1,9},{5,13},{9,1},{13,5},{2,10},{6,14},... | collective-permute-start | bytes 1572872 | tf_op jit(solution)/shard_map/ppermute | solution.py:51
  133.5 1.3 collective-permute-start.57
  133.6 1.5 collective-permute-start.58
  134.0 1.5 collective-permute-start.39
  134.9 2.6 %collective-permute-start.40 = (bf16[64,1024]{1,0:T(8,128)(2,1)S(1)}, bf16[64,1024]{1,0:T(8,128)(2,1)S(1)}, u32[]{:S(2)}, u32[]{:S(2)}) collective-permute-start(bf16[64,1024]{1,0:T(8,128)(2,1)S(1)} %get-tuple-element.87), channel_id=1, source_target_pairs={{0,16},{16,0},{1,17},{17,1},{2,18},{18,2},{3,19},{19,3},{4,20},{20... | collective-permute-start | bytes 393224 | tf_op jit(solution)/shard_map/ppermute | solution.py:51
  135.0 3.5 %collective-permute-start.41 = (bf16[64,1024]{1,0:T(8,128)(2,1)S(1)}, bf16[64,1024]{1,0:T(8,128)(2,1)S(1)}, u32[]{:S(2)}, u32[]{:S(2)}) collective-permute-start(bf16[64,1024]{1,0:T(8,128)(2,1)S(1)} %get-tuple-element.88), channel_id=1, source_target_pairs={{0,16},{16,0},{1,17},{17,1},{2,18},{18,2},{3,19},{19,3},{4,20},{20... | collective-permute-start | bytes 393224 | tf_op jit(solution)/shard_map/ppermute | solution.py:51
  135.5 17.2 %collective-permute-start.61 = (bf16[1,128,1024]{2,1,0:T(8,128)(2,1)S(1)}, bf16[1,128,1024]{2,1,0:T(8,128)(2,1)S(1)}, u32[]{:S(2)}, u32[]{:S(2)}) collective-permute-start(bf16[1,128,1024]{2,1,0:T(8,128)(2,1)S(1)} %get-tuple-element.109.refs_25_), channel_id=1, source_target_pairs={{0,12},{4,8},{8,4},{12,0},{1,13},{5,9},{9,5},{13,1},{2,14},{6,10},... | collective-permute-start | bytes 786440 | tf_op jit(solution)/shard_map/ppermute | solution.py:51
  137.5 20.4 %collective-permute-start.62 = (bf16[1,128,1024]{2,1,0:T(8,128)(2,1)S(1)}, bf16[1,128,1024]{2,1,0:T(8,128)(2,1)S(1)}, u32[]{:S(2)}, u32[]{:S(2)}) collective-permute-start(bf16[1,128,1024]{2,1,0:T(8,128)(2,1)S(1)} %get-tuple-element.111), channel_id=1, source_target_pairs={{0,12},{4,8},{8,4},{12,0},{1,13},{5,9},{9,5},{13,1},{2,14},{6,10},... | collective-permute-start | bytes 786440 | tf_op jit(solution)/shard_map/ppermute | solution.py:51
  138.5 10.0 %collective-permute-start.42 = (bf16[64,1024]{1,0:T(8,128)(2,1)S(1)}, bf16[64,1024]{1,0:T(8,128)(2,1)S(1)}, u32[]{:S(2)}, u32[]{:S(2)}) collective-permute-start(bf16[64,1024]{1,0:T(8,128)(2,1)S(1)} %get-tuple-element.89), channel_id=1, source_target_pairs={{0,16},{16,0},{1,17},{17,1},{2,18},{18,2},{3,19},{19,3},{4,20},{20... | collective-permute-start | bytes 393224 | tf_op jit(solution)/shard_map/ppermute | solution.py:51
  (7 other events, 28.0 us)

commit v5 on v4

--- a/solution.py
+++ b/solution.py
@@ -351,8 +351,8 @@
 WEIGHTS = -1
 FOUR = (
     0, 1, 2, 1, 2, 0, 3, 1, 0, 3, 2, 1, 0, 3, 2, 1, 0, 3, 2, 1,
-    0, 3, 2, 1, 0, 3, 2, 0, 1, 1, 3, 2, 1, 2, 2, 3, 3, 3, WEIGHTS, 0,
-    1, 2, 3,
+    0, 3, 2, 1, 0, 3, 2, 0, 1, 3, 1, 1, 2, 2, 3, 2, 3, 1, 3, 0,
+    WEIGHTS, 2, 3,
 )
 
 

time: 160 us -> 162 us (1.012)
  starting transfers between devices: 63.4 us -> 67.3 us
    ppermute x24, waiting for transfers between devices: 31.8 us -> 25.7 us  [hop(): return lax.ppermute(value, 'gz', pairs)]
    ppermute x39, waiting for transfers between devices: 14.7 us -> 19.7 us  [swap(): return lax.ppermute(value, axis, [(i, i ^ mask) for i in range(size)])]
    ppermute x24, starting transfers between devices: 46.9 us -> 51 us  [hop(): return lax.ppermute(value, 'gz', pairs)]
  transfers between devices with their start and end apart: 63 -> 63, of which waited for: 23 -> 25; matrix products, arithmetic and copies ran while one was open for 0% -> 0% of each run, Pallas kernels for 21% -> 23%
where the time goes in v5:
time: 162 us
  starting transfers between devices  67.3 us (42%)
  waiting for transfers between devices  45.4 us (28%)
  Pallas kernels  39.2 us (24%)
  local copies, waits for them, and re-layouts  8.47 us (5%)
    ppermute x24, starting transfers between devices, hop(): return lax.ppermute(value, 'gz', pairs)  51 us
    pallas_call x50, Pallas kernels, call(): pl.pallas_call(kernel, in_specs=in_specs, out_specs=out_specs, out_shape=...  39.2 us
    ppermute x24, waiting for transfers between devices, hop(): return lax.ppermute(value, 'gz', pairs)  25.7 us
    ppermute x39, waiting for transfers between devices, swap(): return lax.ppermute(value, axis, [(i, i ^ mask) for i in range(size)])  19.7 us
    ppermute x39, starting transfers between devices, swap(): return lax.ppermute(value, axis, [(i, i ^ mask) for i in range(size)])  16.2 us
    unnamed x16, local copies, waits for them, and re-layouts  8.47 us
  transfers between devices with their start and end apart: 63, of which 25 were waited for; matrix products, arithmetic and copies ran while one was open for 0% of the time, Pallas kernels for 23%

profile of v5, /device:TPU:0, one launch (start us, length us, event | category | flops | bytes accessed | tf_op | source)
XLA Modules:
  0.0 161.6 jit_solution(9302000142380131554)
XLA Ops:
  0.6 0.9 copy-done.6
  1.6 0.9 copy-done.7
  2.5 0.7 ordered_rows.1.refs_0_.refs_1_
  3.3 3.0 %collective-permute-start.6 = (bf16[2,128,1024]{2,1,0:T(8,128)(2,1)S(1)}, bf16[2,128,1024]{2,1,0:T(8,128)(2,1)S(1)}, u32[]{:S(2)}, u32[]{:S(2)}) collective-permute-start(bf16[2,128,1024]{2,1,0:T(8,128)(2,1)S(1)} %ordered_rows.1.refs_0_.refs_1_), channel_id=1, source_target_pairs={{0,4},{4,0},{8,12},{12,8},{1,5},{5,1},{9,13},{13,9},{2,6},{6,2},{1... | collective-permute-start | bytes 1572872 | tf_op jit(solution)/shard_map/ppermute | solution.py:51
  6.3 1.5 collective-permute-start.5
  8.5 0.8 collective-permute-done.1.refs_3_.refs_6_
  9.8 0.8 collective-permute-done.refs_2_.refs_5_
  10.6 2.2 %copy-done = bf16[2048,1024]{1,0:T(8,128)(2,1)S(1)} copy-done((bf16[2048,1024]{1,0:T(8,128)(2,1)S(1)}, bf16[2048,1024]{1,0:T(8,128)(2,1)}, u32[]{:S(2)}) %copy-start) | copy-done | bytes 4194328
  12.8 2.2 %copy-done.2 = bf16[2048,1024]{1,0:T(8,128)(2,1)S(1)} copy-done((bf16[2048,1024]{1,0:T(8,128)(2,1)S(1)}, bf16[2048,1024]{1,0:T(8,128)(2,1)}, u32[]{:S(2)}) %copy-start.2) | copy-done | bytes 4194328
  15.0 2.2 %copy-done.4 = bf16[2048,1024]{1,0:T(8,128)(2,1)S(1)} copy-done((bf16[2048,1024]{1,0:T(8,128)(2,1)S(1)}, bf16[2048,1024]{1,0:T(8,128)(2,1)}, u32[]{:S(2)}) %copy-start.4) | copy-done | bytes 4194328
  17.2 2.7 %forward_products.4 = (bf16[3,64,1024]{2,1,0:T(8,128)(2,1)S(1)}, bf16[3,64,1024]{2,1,0:T(8,128)(2,1)S(1)}) custom-call(s32[1]{0:T(128)} %bitcast.1.refs_0_, bf16[2,128,1024]{2,1,0:T(8,128)(2,1)S(1)} %ordered_rows.1.refs_0_.refs_1_, bf16[64,1024]{1,0:T(8,128)(2,1)S(1)} %collective-permute-done.refs_2_.refs_5_, ...), custom_call_target="tpu_custom_call" | custom-call | flops 1000 | bytes 1000 | tf_op jit(solution)/shard_map/forward_products/pallas_call | solution.py:36
  20.2 3.6 %collective-permute-start.4 = (bf16[3,64,1024]{2,1,0:T(8,128)(2,1)S(1)}, bf16[3,64,1024]{2,1,0:T(8,128)(2,1)S(1)}, u32[]{:S(2)}, u32[]{:S(2)}) collective-permute-start(bf16[3,64,1024]{2,1,0:T(8,128)(2,1)S(1)} %get-tuple-element.66.refs_0_), channel_id=1, source_target_pairs={{0,1},{3,2},{4,5},{7,6},{8,9},{11,10},{12,13},{15,14},{16,17},{19,... | collective-permute-start | bytes 1179656 | tf_op jit(solution)/shard_map/ppermute | solution.py:385
  26.4 2.7 %forward_products.5 = (bf16[3,64,1024]{2,1,0:T(8,128)(2,1)S(1)}, bf16[3,64,1024]{2,1,0:T(8,128)(2,1)S(1)}) custom-call(s32[1]{0:T(128)} %bitcast.1.refs_0_, bf16[2,128,1024]{2,1,0:T(8,128)(2,1)S(1)} %pass_on.19.refs_0_.refs_1_.refs_2_, bf16[64,1024]{1,0:T(8,128)(2,1)S(1)} %collective-permute-done.11.refs_2_.refs_9_, ...), custom_call_target="tpu_custom_call" | custom-call | flops 1000 | bytes 1000 | tf_op jit(solution)/shard_map/forward_products/pallas_call | solution.py:36
  29.1 1.3 collective-permute-start.16
  30.4 2.7 %forward_products.6 = (bf16[3,64,1024]{2,1,0:T(8,128)(2,1)S(1)}, bf16[3,64,1024]{2,1,0:T(8,128)(2,1)S(1)}) custom-call(s32[1]{0:T(128)} %bitcast.1.refs_0_, bf16[2,128,1024]{2,1,0:T(8,128)(2,1)S(1)} %pass_on.20.refs_0_.refs_1_.refs_3_, bf16[64,1024]{1,0:T(8,128)(2,1)S(1)} %collective-permute-done.7.refs_2_.refs_13_, ...), custom_call_target="tpu_custom_call" | custom-call | flops 1000 | bytes 1000 | tf_op jit(solution)/shard_map/forward_products/pallas_call | solution.py:36
  33.3 0.7 collective-permute-start.15
  34.0 5.2 %collective-permute-done.17.refs_0_ = bf16[2,128,1024]{2,1,0:T(8,128)(2,1)S(1)} collective-permute-done((bf16[2,128,1024]{2,1,0:T(8,128)(2,1)S(1)}, bf16[2,128,1024]{2,1,0:T(8,128)(2,1)S(1)}, u32[]{:S(2)}, u32[]{:S(2)}) %collective-permute-start.17) | collective-permute-done | bytes 524320 | tf_op jit(solution)/shard_map/ppermute | solution.py:51
  39.9 1.2 collective-permute-done.16.refs_1_
  41.2 8.4 %collective-permute-start.20 = (bf16[3,64,1024]{2,1,0:T(8,128)(2,1)S(1)}, bf16[3,64,1024]{2,1,0:T(8,128)(2,1)S(1)}, u32[]{:S(2)}, u32[]{:S(2)}) collective-permute-start(bf16[3,64,1024]{2,1,0:T(8,128)(2,1)S(1)} %get-tuple-element.79.refs_0_), channel_id=1, source_target_pairs={{0,1},{3,2},{4,5},{7,6},{8,9},{11,10},{12,13},{15,14},{16,17},{19,... | collective-permute-start | bytes 1179656 | tf_op jit(solution)/shard_map/ppermute | solution.py:385
  49.8 0.7 collective-permute-start.19
  50.5 1.3 collective-permute-start.18
  51.8 2.7 %forward_products.7 = (bf16[3,64,1024]{2,1,0:T(8,128)(2,1)S(1)}, bf16[3,64,1024]{2,1,0:T(8,128)(2,1)S(1)}) custom-call(s32[1]{0:T(128)} %bitcast.1.refs_0_, bf16[2,128,1024]{2,1,0:T(8,128)(2,1)S(1)} %pass_on.21.refs_0_.refs_1_.refs_4_, bf16[64,1024]{1,0:T(8,128)(2,1)S(1)} %collective-permute-done.21.refs_2_.refs_17_, ...), custom_call_target="tpu_custom_call" | custom-call | flops 1000 | bytes 1000 | tf_op jit(solution)/shard_map/forward_products/pallas_call | solution.py:36
  54.5 4.6 %collective-permute-start.28 = (bf16[3,64,1024]{2,1,0:T(8,128)(2,1)S(1)}, bf16[3,64,1024]{2,1,0:T(8,128)(2,1)S(1)}, u32[]{:S(2)}, u32[]{:S(2)}) collective-permute-start(bf16[3,64,1024]{2,1,0:T(8,128)(2,1)S(1)} %get-tuple-element.84.refs_0_), channel_id=1, source_target_pairs={{0,1},{3,2},{4,5},{7,6},{8,9},{11,10},{12,13},{15,14},{16,17},{19,... | collective-permute-start | bytes 1179656 | tf_op jit(solution)/shard_map/ppermute | solution.py:385
  59.2 0.7 collective-permute-start.27
  60.0 1.3 collective-permute-start.26
  61.5 4.6 %collective-permute-start.25 = (bf16[3,64,1024]{2,1,0:T(8,128)(2,1)S(1)}, bf16[3,64,1024]{2,1,0:T(8,128)(2,1)S(1)}, u32[]{:S(2)}, u32[]{:S(2)}) collective-permute-start(bf16[3,64,1024]{2,1,0:T(8,128)(2,1)S(1)} %activations.4.refs_2_), channel_id=1, source_target_pairs={{0,1},{3,2},{4,5},{7,6},{8,9},{11,10},{12,13},{15,14},{16,17},{19,... | collective-permute-start | bytes 1179656 | tf_op jit(solution)/shard_map/ppermute | solution.py:385
  66.1 0.8 collective-permute-done.28.refs_1_
  67.1 0.7 collective-permute-start.32
  67.9 1.3 collective-permute-start.31
  69.2 1.4 collective-permute-done.26.refs_1_
  70.7 5.9 %collective-permute-start.30 = (bf16[3,64,1024]{2,1,0:T(8,128)(2,1)S(1)}, bf16[3,64,1024]{2,1,0:T(8,128)(2,1)S(1)}, u32[]{:S(2)}, u32[]{:S(2)}) collective-permute-start(bf16[3,64,1024]{2,1,0:T(8,128)(2,1)S(1)} %activations.5.refs_1_.refs_2_), channel_id=1, source_target_pairs={{0,1},{3,2},{4,5},{7,6},{8,9},{11,10},{12,13},{15,14},{16,17},{19,... | collective-permute-start | bytes 1179656 | tf_op jit(solution)/shard_map/ppermute | solution.py:385
  76.6 0.7 collective-permute-start.29
  77.5 1.3 collective-permute-start.36
  78.8 2.1 %collective-permute-done.31.refs_1_ = bf16[3,64,1024]{2,1,0:T(8,128)(2,1)S(1)} collective-permute-done((bf16[3,64,1024]{2,1,0:T(8,128)(2,1)S(1)}, bf16[3,64,1024]{2,1,0:T(8,128)(2,1)S(1)}, u32[]{:S(2)}, u32[]{:S(2)}) %collective-permute-start.31) | collective-permute-done | bytes 393248 | tf_op jit(solution)/shard_map/ppermute | solution.py:385
  81.1 4.1 %collective-permute-start.35 = (bf16[3,64,1024]{2,1,0:T(8,128)(2,1)S(1)}, bf16[3,64,1024]{2,1,0:T(8,128)(2,1)S(1)}, u32[]{:S(2)}, u32[]{:S(2)}) collective-permute-start(bf16[3,64,1024]{2,1,0:T(8,128)(2,1)S(1)} %activations.6.refs_1_.refs_2_), channel_id=1, source_target_pairs={{0,1},{3,2},{4,5},{7,6},{8,9},{11,10},{12,13},{15,14},{16,17},{19,... | collective-permute-start | bytes 1179656 | tf_op jit(solution)/shard_map/ppermute | solution.py:385
  85.3 0.7 collective-permute-start.34
  86.0 1.3 collective-permute-start.33
  87.3 3.4 %collective-permute-done.36.refs_1_ = bf16[3,64,1024]{2,1,0:T(8,128)(2,1)S(1)} collective-permute-done((bf16[3,64,1024]{2,1,0:T(8,128)(2,1)S(1)}, bf16[3,64,1024]{2,1,0:T(8,128)(2,1)S(1)}, u32[]{:S(2)}, u32[]{:S(2)}) %collective-permute-start.36) | collective-permute-done | bytes 393248 | tf_op jit(solution)/shard_map/ppermute | solution.py:385
  90.9 2.7 %collective-permute-start.38 = (bf16[3,64,1024]{2,1,0:T(8,128)(2,1)S(1)}, bf16[3,64,1024]{2,1,0:T(8,128)(2,1)S(1)}, u32[]{:S(2)}, u32[]{:S(2)}) collective-permute-start(bf16[3,64,1024]{2,1,0:T(8,128)(2,1)S(1)} %activations.7.refs_1_.refs_2_), channel_id=1, source_target_pairs={{0,1},{3,2},{4,5},{7,6},{8,9},{11,10},{12,13},{15,14},{16,17},{19,... | collective-permute-start | bytes 1179656 | tf_op jit(solution)/shard_map/ppermute | solution.py:385
  93.6 0.7 collective-permute-start.37
  94.3 1.3 collective-permute-start.44
  95.6 3.7 %collective-permute-done.33.refs_0_ = bf16[3,64,1024]{2,1,0:T(8,128)(2,1)S(1)} collective-permute-done((bf16[3,64,1024]{2,1,0:T(8,128)(2,1)S(1)}, bf16[3,64,1024]{2,1,0:T(8,128)(2,1)S(1)}, u32[]{:S(2)}, u32[]{:S(2)}) %collective-permute-start.33) | collective-permute-done | bytes 393248 | tf_op jit(solution)/shard_map/ppermute | solution.py:385
  99.3 0.7 collective-permute-start.43
  100.0 3.5 %backward_products.4 = (bf16[2,128,1024]{2,1,0:T(8,128)(2,1)S(1)}, bf16[3,128,1024]{2,1,0:T(8,128)(2,1)S(1)}, bf16[64,1024]{1,0:T(8,128)(2,1)S(1)}, bf16[64,1024...) custom-call(s32[1]{0:T(128)} %bitcast.1.refs_0_, s32[1]{0:T(128)} %bitcast.2.refs_1_, ...), custom_call_target="tpu_custom_call" | custom-call | flops 1000 | bytes 1000 | tf_op jit(solution)/shard_map/backward_products/pallas_call | solution.py:36
  103.6 3.1 %collective-permute-done.44.refs_0_ = bf16[3,64,1024]{2,1,0:T(8,128)(2,1)S(1)} collective-permute-done((bf16[3,64,1024]{2,1,0:T(8,128)(2,1)S(1)}, bf16[3,64,1024]{2,1,0:T(8,128)(2,1)S(1)}, u32[]{:S(2)}, u32[]{:S(2)}) %collective-permute-start.44) | collective-permute-done | bytes 393248 | tf_op jit(solution)/shard_map/ppermute | solution.py:385
  106.7 1.3 collective-permute-start.46
  108.0 3.7 %backward_products.5 = (bf16[2,128,1024]{2,1,0:T(8,128)(2,1)S(1)}, bf16[3,128,1024]{2,1,0:T(8,128)(2,1)S(1)}, bf16[64,1024]{1,0:T(8,128)(2,1)S(1)}, bf16[64,1024...) custom-call(s32[1]{0:T(128)} %bitcast.1.refs_0_, s32[1]{0:T(128)} %bitcast.2.refs_1_, ...), custom_call_target="tpu_custom_call" | custom-call | flops 1000 | bytes 1000 | tf_op jit(solution)/shard_map/backward_products/pallas_call | solution.py:36
  111.8 1.3 collective-permute-start.45
  113.1 0.6 collective-permute-start.48
  115.3 0.6 collective-permute-start.59
  115.9 5.1 %collective-permute-done.46.refs_0_ = bf16[3,64,1024]{2,1,0:T(8,128)(2,1)S(1)} collective-permute-done((bf16[3,64,1024]{2,1,0:T(8,128)(2,1)S(1)}, bf16[3,64,1024]{2,1,0:T(8,128)(2,1)S(1)}, u32[]{:S(2)}, u32[]{:S(2)}) %collective-permute-start.46) | collective-permute-done | bytes 393248 | tf_op jit(solution)/shard_map/ppermute | solution.py:385
  120.9 3.5 %backward_products.6 = (bf16[2,128,1024]{2,1,0:T(8,128)(2,1)S(1)}, bf16[3,128,1024]{2,1,0:T(8,128)(2,1)S(1)}, bf16[64,1024]{1,0:T(8,128)(2,1)S(1)}, bf16[64,1024...) custom-call(s32[1]{0:T(128)} %bitcast.1.refs_0_, s32[1]{0:T(128)} %bitcast.2.refs_1_, ...), custom_call_target="tpu_custom_call" | custom-call | flops 1000 | bytes 1000 | tf_op jit(solution)/shard_map/backward_products/pallas_call | solution.py:36
  125.1 4.8 %collective-permute-done.45.refs_0_ = bf16[3,64,1024]{2,1,0:T(8,128)(2,1)S(1)} collective-permute-done((bf16[3,64,1024]{2,1,0:T(8,128)(2,1)S(1)}, bf16[3,64,1024]{2,1,0:T(8,128)(2,1)S(1)}, u32[]{:S(2)}, u32[]{:S(2)}) %collective-permute-start.45) | collective-permute-done | bytes 393248 | tf_op jit(solution)/shard_map/ppermute | solution.py:385
  130.0 1.3 collective-permute-done.54.refs_4_
  131.4 3.5 %backward_products.7 = (bf16[2,128,1024]{2,1,0:T(8,128)(2,1)S(1)}, bf16[3,128,1024]{2,1,0:T(8,128)(2,1)S(1)}, bf16[64,1024]{1,0:T(8,128)(2,1)S(1)}, bf16[64,1024...) custom-call(s32[1]{0:T(128)} %bitcast.1.refs_0_, s32[1]{0:T(128)} %bitcast.2.refs_1_, ...), custom_call_target="tpu_custom_call" | custom-call | flops 1000 | bytes 1000 | tf_op jit(solution)/shard_map/backward_products/pallas_call | solution.py:36
  135.2 0.5 collective-permute-start.60
  136.5 0.5 collective-permute-done.56.refs_2_
  137.8 1.4 collective-permute-start.61
  139.2 1.6 collective-permute-start.62
  140.8 0.5 collective-permute-start.42
  141.3 0.8 collective-permute-done.41.refs_3_
  142.5 10.0 %weight_grads.1 = (bf16[16,128]{1,0:T(8,128)(2,1)S(1)}, f32[2048,1024]{1,0:T(8,128)}, f32[2048,1024]{1,0:T(8,128)}, f32[2048,1024]{1,0:T(8,128)}) custom-call(s32[1]{0:T(128)} %bitcast.1.refs_0_, bf16[2,128,1024]{2,1,0:T(8,128)(2,1)S(1)} %ordered_rows.1.refs_0_.refs_1_, bf16[2,128,1024]{2,1,0:T(8,128)(2,1)S(1)} %pass_on.19.refs_0_.refs_1_.refs_2_, ...), custom_call_target="tpu_custom_call" | custom-call | flops 1000 | bytes 1000 | tf_op jit(solution)/shard_map/weight_grads/pallas_call | solution.py:36
  152.5 8.1 %collective-permute-done.60.refs_0_ = bf16[2,128,1024]{2,1,0:T(8,128)(2,1)S(1)} collective-permute-done((bf16[2,128,1024]{2,1,0:T(8,128)(2,1)S(1)}, bf16[2,128,1024]{2,1,0:T(8,128)(2,1)S(1)}, u32[]{:S(2)}, u32[]{:S(2)}) %collective-permute-start.60) | collective-permute-done | bytes 524320 | tf_op jit(solution)/shard_map/ppermute | solution.py:51
  160.6 1.0 final_sum.1
  (128 shorter events, 11.1 us)
Async XLA Ops:
  3.3 16.6 %collective-permute-start.6 = (bf16[2,128,1024]{2,1,0:T(8,128)(2,1)S(1)}, bf16[2,128,1024]{2,1,0:T(8,128)(2,1)S(1)}, u32[]{:S(2)}, u32[]{:S(2)}) collective-permute-start(bf16[2,128,1024]{2,1,0:T(8,128)(2,1)S(1)} %ordered_rows.1.refs_0_.refs_1_), channel_id=1, source_target_pairs={{0,4},{4,0},{8,12},{12,8},{1,5},{5,1},{9,13},{13,9},{2,6},{6,2},{1... | collective-permute-start | bytes 1572872 | tf_op jit(solution)/shard_map/ppermute | solution.py:51
  6.3 18.1 %collective-permute-start.5 = (bf16[2,128,1024]{2,1,0:T(8,128)(2,1)S(1)}, bf16[2,128,1024]{2,1,0:T(8,128)(2,1)S(1)}, u32[]{:S(2)}, u32[]{:S(2)}) collective-permute-start(bf16[2,128,1024]{2,1,0:T(8,128)(2,1)S(1)} %ordered_rows.1.refs_0_.refs_1_), channel_id=1, source_target_pairs={{0,8},{4,12},{8,0},{12,4},{1,9},{5,13},{9,1},{13,5},{2,10},{6,14},... | collective-permute-start | bytes 1572872 | tf_op jit(solution)/shard_map/ppermute | solution.py:51
  7.8 1.4 collective-permute-start.1
  7.9 1.5 collective-permute-start.2
  8.4 1.3 collective-permute-start.3
  9.3 1.3 collective-permute-start
  17.2 9.2 %copy-start.5 = (bf16[2048,1024]{1,0:T(8,128)(2,1)S(1)}, bf16[2048,1024]{1,0:T(8,128)(2,1)}, u32[]{:S(2)}) copy-start(bf16[2048,1024]{1,0:T(8,128)(2,1)} %refs_8_.15) | copy-start | bytes 12582916
  20.0 4.6 %collective-permute-start.12 = (bf16[64,1024]{1,0:T(8,128)(2,1)S(1)}, bf16[64,1024]{1,0:T(8,128)(2,1)S(1)}, u32[]{:S(2)}, u32[]{:S(2)}) collective-permute-start(bf16[64,1024]{1,0:T(8,128)(2,1)S(1)} %get-tuple-element.72), channel_id=1, source_target_pairs={{0,16},{16,0},{1,17},{17,1},{2,18},{18,2},{3,19},{19,3},{4,20},{20... | collective-permute-start | bytes 393224 | tf_op jit(solution)/shard_map/ppermute | solution.py:51
  20.2 13.0 %collective-permute-start.4 = (bf16[3,64,1024]{2,1,0:T(8,128)(2,1)S(1)}, bf16[3,64,1024]{2,1,0:T(8,128)(2,1)S(1)}, u32[]{:S(2)}, u32[]{:S(2)}) collective-permute-start(bf16[3,64,1024]{2,1,0:T(8,128)(2,1)S(1)} %get-tuple-element.66.refs_0_), channel_id=1, source_target_pairs={{0,1},{3,2},{4,5},{7,6},{8,9},{11,10},{12,13},{15,14},{16,17},{19,... | collective-permute-start | bytes 1179656 | tf_op jit(solution)/shard_map/ppermute | solution.py:385
  23.8 1.4 collective-permute-start.13
  24.0 1.8 %collective-permute-start.14 = (bf16[64,1024]{1,0:T(8,128)(2,1)S(1)}, bf16[64,1024]{1,0:T(8,128)(2,1)S(1)}, u32[]{:S(2)}, u32[]{:S(2)}) collective-permute-start(bf16[64,1024]{1,0:T(8,128)(2,1)S(1)} %get-tuple-element.74), channel_id=1, source_target_pairs={{0,16},{16,0},{1,17},{17,1},{2,18},{18,2},{3,19},{19,3},{4,20},{20... | collective-permute-start | bytes 393224 | tf_op jit(solution)/shard_map/ppermute | solution.py:51
  24.4 1.3 collective-permute-start.11
  24.5 1.7 %collective-permute-start.8 = (bf16[64,1024]{1,0:T(8,128)(2,1)S(1)}, bf16[64,1024]{1,0:T(8,128)(2,1)S(1)}, u32[]{:S(2)}, u32[]{:S(2)}) collective-permute-start(bf16[64,1024]{1,0:T(8,128)(2,1)S(1)} %get-tuple-element.69), channel_id=1, source_target_pairs={{0,16},{16,0},{1,17},{17,1},{2,18},{18,2},{3,19},{19,3},{4,20},{20... | collective-permute-start | bytes 393224 | tf_op jit(solution)/shard_map/ppermute | solution.py:51
  25.2 14.0 %collective-permute-start.17 = (bf16[2,128,1024]{2,1,0:T(8,128)(2,1)S(1)}, bf16[2,128,1024]{2,1,0:T(8,128)(2,1)S(1)}, u32[]{:S(2)}, u32[]{:S(2)}) collective-permute-start(bf16[2,128,1024]{2,1,0:T(8,128)(2,1)S(1)} %pass_on.19.refs_0_.refs_1_.refs_2_), channel_id=1, source_target_pairs={{0,8},{4,12},{8,0},{12,4},{1,9},{5,13},{9,1},{13,5},{2,10},{6,14},... | collective-permute-start | bytes 1572872 | tf_op jit(solution)/shard_map/ppermute | solution.py:51
  25.8 3.3 %collective-permute-start.9 = (bf16[64,1024]{1,0:T(8,128)(2,1)S(1)}, bf16[64,1024]{1,0:T(8,128)(2,1)S(1)}, u32[]{:S(2)}, u32[]{:S(2)}) collective-permute-start(bf16[64,1024]{1,0:T(8,128)(2,1)S(1)} %get-tuple-element.70), channel_id=1, source_target_pairs={{0,16},{16,0},{1,17},{17,1},{2,18},{18,2},{3,19},{19,3},{4,20},{20... | collective-permute-start | bytes 393224 | tf_op jit(solution)/shard_map/ppermute | solution.py:51
  25.8 4.7 %collective-permute-start.10 = (bf16[64,1024]{1,0:T(8,128)(2,1)S(1)}, bf16[64,1024]{1,0:T(8,128)(2,1)S(1)}, u32[]{:S(2)}, u32[]{:S(2)}) collective-permute-start(bf16[64,1024]{1,0:T(8,128)(2,1)S(1)} %get-tuple-element.71), channel_id=1, source_target_pairs={{0,16},{16,0},{1,17},{17,1},{2,18},{18,2},{3,19},{19,3},{4,20},{20... | collective-permute-start | bytes 393224 | tf_op jit(solution)/shard_map/ppermute | solution.py:51
  26.3 4.2 %collective-permute-start.7 = (bf16[64,1024]{1,0:T(8,128)(2,1)S(1)}, bf16[64,1024]{1,0:T(8,128)(2,1)S(1)}, u32[]{:S(2)}, u32[]{:S(2)}) collective-permute-start(bf16[64,1024]{1,0:T(8,128)(2,1)S(1)} %get-tuple-element.68.refs_9_), channel_id=1, source_target_pairs={{0,16},{16,0},{1,17},{17,1},{2,18},{18,2},{3,19},{19,3},{4,20},{20... | collective-permute-start | bytes 393224 | tf_op jit(solution)/shard_map/ppermute | solution.py:51
  29.1 12.0 %collective-permute-start.16 = (bf16[3,64,1024]{2,1,0:T(8,128)(2,1)S(1)}, bf16[3,64,1024]{2,1,0:T(8,128)(2,1)S(1)}, u32[]{:S(2)}, u32[]{:S(2)}) collective-permute-start(bf16[3,64,1024]{2,1,0:T(8,128)(2,1)S(1)} %get-tuple-element.77.refs_0_), channel_id=1, source_target_pairs={{0,1},{3,2},{4,5},{7,6},{8,9},{11,10},{12,13},{15,14},{16,17},{19,... | collective-permute-start | bytes 1179656 | tf_op jit(solution)/shard_map/ppermute | solution.py:385
  33.3 7.9 %collective-permute-start.15 = (bf16[3,64,1024]{2,1,0:T(8,128)(2,1)S(1)}, bf16[3,64,1024]{2,1,0:T(8,128)(2,1)S(1)}, u32[]{:S(2)}, u32[]{:S(2)}) collective-permute-start(bf16[3,64,1024]{2,1,0:T(8,128)(2,1)S(1)} %add_on.8.refs_1_), channel_id=1, source_target_pairs={{1,2},{2,1},{5,6},{6,5},{9,10},{10,9},{13,14},{14,13},{17,18},{18,... | collective-permute-start | bytes 1179656 | tf_op jit(solution)/shard_map/ppermute | solution.py:385
  39.3 10.5 %collective-permute-start.22 = (bf16[64,1024]{1,0:T(8,128)(2,1)S(1)}, bf16[64,1024]{1,0:T(8,128)(2,1)S(1)}, u32[]{:S(2)}, u32[]{:S(2)}) collective-permute-start(bf16[64,1024]{1,0:T(8,128)(2,1)S(1)} %get-tuple-element.80), channel_id=1, source_target_pairs={{0,16},{16,0},{1,17},{17,1},{2,18},{18,2},{3,19},{19,3},{4,20},{20... | collective-permute-start | bytes 393224 | tf_op jit(solution)/shard_map/ppermute | solution.py:51
  39.3 11.1 %collective-permute-start.23 = (bf16[64,1024]{1,0:T(8,128)(2,1)S(1)}, bf16[64,1024]{1,0:T(8,128)(2,1)S(1)}, u32[]{:S(2)}, u32[]{:S(2)}) collective-permute-start(bf16[64,1024]{1,0:T(8,128)(2,1)S(1)} %get-tuple-element.81), channel_id=1, source_target_pairs={{0,16},{16,0},{1,17},{17,1},{2,18},{18,2},{3,19},{19,3},{4,20},{20... | collective-permute-start | bytes 393224 | tf_op jit(solution)/shard_map/ppermute | solution.py:51
  39.8 11.9 %collective-permute-start.24 = (bf16[64,1024]{1,0:T(8,128)(2,1)S(1)}, bf16[64,1024]{1,0:T(8,128)(2,1)S(1)}, u32[]{:S(2)}, u32[]{:S(2)}) collective-permute-start(bf16[64,1024]{1,0:T(8,128)(2,1)S(1)} %get-tuple-element.82), channel_id=1, source_target_pairs={{0,16},{16,0},{1,17},{17,1},{2,18},{18,2},{3,19},{19,3},{4,20},{20... | collective-permute-start | bytes 393224 | tf_op jit(solution)/shard_map/ppermute | solution.py:51
  41.1 10.7 %collective-permute-start.21 = (bf16[64,1024]{1,0:T(8,128)(2,1)S(1)}, bf16[64,1024]{1,0:T(8,128)(2,1)S(1)}, u32[]{:S(2)}, u32[]{:S(2)}) collective-permute-start(bf16[64,1024]{1,0:T(8,128)(2,1)S(1)} %get-tuple-element.78.refs_2_), channel_id=1, source_target_pairs={{0,16},{16,0},{1,17},{17,1},{2,18},{18,2},{3,19},{19,3},{4,20},{20... | collective-permute-start | bytes 393224 | tf_op jit(solution)/shard_map/ppermute | solution.py:51
  41.2 17.9 %collective-permute-start.20 = (bf16[3,64,1024]{2,1,0:T(8,128)(2,1)S(1)}, bf16[3,64,1024]{2,1,0:T(8,128)(2,1)S(1)}, u32[]{:S(2)}, u32[]{:S(2)}) collective-permute-start(bf16[3,64,1024]{2,1,0:T(8,128)(2,1)S(1)} %get-tuple-element.79.refs_0_), channel_id=1, source_target_pairs={{0,1},{3,2},{4,5},{7,6},{8,9},{11,10},{12,13},{15,14},{16,17},{19,... | collective-permute-start | bytes 1179656 | tf_op jit(solution)/shard_map/ppermute | solution.py:385
  49.8 10.1 %collective-permute-start.19 = (bf16[3,64,1024]{2,1,0:T(8,128)(2,1)S(1)}, bf16[3,64,1024]{2,1,0:T(8,128)(2,1)S(1)}, u32[]{:S(2)}, u32[]{:S(2)}) collective-permute-start(bf16[3,64,1024]{2,1,0:T(8,128)(2,1)S(1)} %add_on.9.refs_2_), channel_id=1, source_target_pairs={{1,2},{2,1},{5,6},{6,5},{9,10},{10,9},{13,14},{14,13},{17,18},{18,... | collective-permute-start | bytes 1179656 | tf_op jit(solution)/shard_map/ppermute | solution.py:385
  50.5 10.9 %collective-permute-start.18 = (bf16[3,64,1024]{2,1,0:T(8,128)(2,1)S(1)}, bf16[3,64,1024]{2,1,0:T(8,128)(2,1)S(1)}, u32[]{:S(2)}, u32[]{:S(2)}) collective-permute-start(bf16[3,64,1024]{2,1,0:T(8,128)(2,1)S(1)} %add_on.10.refs_9_), channel_id=1, source_target_pairs={{2,3},{1,0},{6,7},{5,4},{10,11},{9,8},{14,15},{13,12},{18,19},{17,... | collective-permute-start | bytes 1179656 | tf_op jit(solution)/shard_map/ppermute | solution.py:385
  54.5 12.5 %collective-permute-start.28 = (bf16[3,64,1024]{2,1,0:T(8,128)(2,1)S(1)}, bf16[3,64,1024]{2,1,0:T(8,128)(2,1)S(1)}, u32[]{:S(2)}, u32[]{:S(2)}) collective-permute-start(bf16[3,64,1024]{2,1,0:T(8,128)(2,1)S(1)} %get-tuple-element.84.refs_0_), channel_id=1, source_target_pairs={{0,1},{3,2},{4,5},{7,6},{8,9},{11,10},{12,13},{15,14},{16,17},{19,... | collective-permute-start | bytes 1179656 | tf_op jit(solution)/shard_map/ppermute | solution.py:385
  59.2 8.5 %collective-permute-start.27 = (bf16[3,64,1024]{2,1,0:T(8,128)(2,1)S(1)}, bf16[3,64,1024]{2,1,0:T(8,128)(2,1)S(1)}, u32[]{:S(2)}, u32[]{:S(2)}) collective-permute-start(bf16[3,64,1024]{2,1,0:T(8,128)(2,1)S(1)} %add_on.11.refs_2_), channel_id=1, source_target_pairs={{1,2},{2,1},{5,6},{6,5},{9,10},{10,9},{13,14},{14,13},{17,18},{18,... | collective-permute-start | bytes 1179656 | tf_op jit(solution)/shard_map/ppermute | solution.py:385
  60.0 10.5 %collective-permute-start.26 = (bf16[3,64,1024]{2,1,0:T(8,128)(2,1)S(1)}, bf16[3,64,1024]{2,1,0:T(8,128)(2,1)S(1)}, u32[]{:S(2)}, u32[]{:S(2)}) collective-permute-start(bf16[3,64,1024]{2,1,0:T(8,128)(2,1)S(1)} %add_on.12.refs_2_), channel_id=1, source_target_pairs={{2,3},{1,0},{6,7},{5,4},{10,11},{9,8},{14,15},{13,12},{18,19},{17,... | collective-permute-start | bytes 1179656 | tf_op jit(solution)/shard_map/ppermute | solution.py:385
  61.5 15.1 %collective-permute-start.25 = (bf16[3,64,1024]{2,1,0:T(8,128)(2,1)S(1)}, bf16[3,64,1024]{2,1,0:T(8,128)(2,1)S(1)}, u32[]{:S(2)}, u32[]{:S(2)}) collective-permute-start(bf16[3,64,1024]{2,1,0:T(8,128)(2,1)S(1)} %activations.4.refs_2_), channel_id=1, source_target_pairs={{0,1},{3,2},{4,5},{7,6},{8,9},{11,10},{12,13},{15,14},{16,17},{19,... | collective-permute-start | bytes 1179656 | tf_op jit(solution)/shard_map/ppermute | solution.py:385
  67.1 10.3 %collective-permute-start.32 = (bf16[3,64,1024]{2,1,0:T(8,128)(2,1)S(1)}, bf16[3,64,1024]{2,1,0:T(8,128)(2,1)S(1)}, u32[]{:S(2)}, u32[]{:S(2)}) collective-permute-start(bf16[3,64,1024]{2,1,0:T(8,128)(2,1)S(1)} %add_on.13.refs_2_), channel_id=1, source_target_pairs={{1,2},{2,1},{5,6},{6,5},{9,10},{10,9},{13,14},{14,13},{17,18},{18,... | collective-permute-start | bytes 1179656 | tf_op jit(solution)/shard_map/ppermute | solution.py:385
  67.9 13.0 %collective-permute-start.31 = (bf16[3,64,1024]{2,1,0:T(8,128)(2,1)S(1)}, bf16[3,64,1024]{2,1,0:T(8,128)(2,1)S(1)}, u32[]{:S(2)}, u32[]{:S(2)}) collective-permute-start(bf16[3,64,1024]{2,1,0:T(8,128)(2,1)S(1)} %add_on.14.refs_2_), channel_id=1, source_target_pairs={{2,3},{1,0},{6,7},{5,4},{10,11},{9,8},{14,15},{13,12},{18,19},{17,... | collective-permute-start | bytes 1179656 | tf_op jit(solution)/shard_map/ppermute | solution.py:385
  70.7 14.5 %collective-permute-start.30 = (bf16[3,64,1024]{2,1,0:T(8,128)(2,1)S(1)}, bf16[3,64,1024]{2,1,0:T(8,128)(2,1)S(1)}, u32[]{:S(2)}, u32[]{:S(2)}) collective-permute-start(bf16[3,64,1024]{2,1,0:T(8,128)(2,1)S(1)} %activations.5.refs_1_.refs_2_), channel_id=1, source_target_pairs={{0,1},{3,2},{4,5},{7,6},{8,9},{11,10},{12,13},{15,14},{16,17},{19,... | collective-permute-start | bytes 1179656 | tf_op jit(solution)/shard_map/ppermute | solution.py:385
  76.6 9.3 %collective-permute-start.29 = (bf16[3,64,1024]{2,1,0:T(8,128)(2,1)S(1)}, bf16[3,64,1024]{2,1,0:T(8,128)(2,1)S(1)}, u32[]{:S(2)}, u32[]{:S(2)}) collective-permute-start(bf16[3,64,1024]{2,1,0:T(8,128)(2,1)S(1)} %pass_on.22.refs_2_.refs_3_), channel_id=1, source_target_pairs={{1,2},{2,1},{5,6},{6,5},{9,10},{10,9},{13,14},{14,13},{17,18},{18,... | collective-permute-start | bytes 1179656 | tf_op jit(solution)/shard_map/ppermute | solution.py:385
  77.5 13.2 %collective-permute-start.36 = (bf16[3,64,1024]{2,1,0:T(8,128)(2,1)S(1)}, bf16[3,64,1024]{2,1,0:T(8,128)(2,1)S(1)}, u32[]{:S(2)}, u32[]{:S(2)}) collective-permute-start(bf16[3,64,1024]{2,1,0:T(8,128)(2,1)S(1)} %add_on.15.refs_2_), channel_id=1, source_target_pairs={{2,3},{1,0},{6,7},{5,4},{10,11},{9,8},{14,15},{13,12},{18,19},{17,... | collective-permute-start | bytes 1179656 | tf_op jit(solution)/shard_map/ppermute | solution.py:385
  81.1 12.5 %collective-permute-start.35 = (bf16[3,64,1024]{2,1,0:T(8,128)(2,1)S(1)}, bf16[3,64,1024]{2,1,0:T(8,128)(2,1)S(1)}, u32[]{:S(2)}, u32[]{:S(2)}) collective-permute-start(bf16[3,64,1024]{2,1,0:T(8,128)(2,1)S(1)} %activations.6.refs_1_.refs_2_), channel_id=1, source_target_pairs={{0,1},{3,2},{4,5},{7,6},{8,9},{11,10},{12,13},{15,14},{16,17},{19,... | collective-permute-start | bytes 1179656 | tf_op jit(solution)/shard_map/ppermute | solution.py:385
  85.3 9.0 %collective-permute-start.34 = (bf16[3,64,1024]{2,1,0:T(8,128)(2,1)S(1)}, bf16[3,64,1024]{2,1,0:T(8,128)(2,1)S(1)}, u32[]{:S(2)}, u32[]{:S(2)}) collective-permute-start(bf16[3,64,1024]{2,1,0:T(8,128)(2,1)S(1)} %pass_on.23.refs_1_.refs_3_), channel_id=1, source_target_pairs={{1,2},{2,1},{5,6},{6,5},{9,10},{10,9},{13,14},{14,13},{17,18},{18,... | collective-permute-start | bytes 1179656 | tf_op jit(solution)/shard_map/ppermute | solution.py:385
  86.0 13.3 %collective-permute-start.33 = (bf16[3,64,1024]{2,1,0:T(8,128)(2,1)S(1)}, bf16[3,64,1024]{2,1,0:T(8,128)(2,1)S(1)}, u32[]{:S(2)}, u32[]{:S(2)}) collective-permute-start(bf16[3,64,1024]{2,1,0:T(8,128)(2,1)S(1)} %pass_on.24.refs_2_.refs_4_), channel_id=1, source_target_pairs={{2,3},{1,0},{6,7},{5,4},{10,11},{9,8},{14,15},{13,12},{18,19},{17,... | collective-permute-start | bytes 1179656 | tf_op jit(solution)/shard_map/ppermute | solution.py:385
  90.9 8.4 %collective-permute-start.38 = (bf16[3,64,1024]{2,1,0:T(8,128)(2,1)S(1)}, bf16[3,64,1024]{2,1,0:T(8,128)(2,1)S(1)}, u32[]{:S(2)}, u32[]{:S(2)}) collective-permute-start(bf16[3,64,1024]{2,1,0:T(8,128)(2,1)S(1)} %activations.7.refs_1_.refs_2_), channel_id=1, source_target_pairs={{0,1},{3,2},{4,5},{7,6},{8,9},{11,10},{12,13},{15,14},{16,17},{19,... | collective-permute-start | bytes 1179656 | tf_op jit(solution)/shard_map/ppermute | solution.py:385
  93.6 6.4 %collective-permute-start.37 = (bf16[3,64,1024]{2,1,0:T(8,128)(2,1)S(1)}, bf16[3,64,1024]{2,1,0:T(8,128)(2,1)S(1)}, u32[]{:S(2)}, u32[]{:S(2)}) collective-permute-start(bf16[3,64,1024]{2,1,0:T(8,128)(2,1)S(1)} %pass_on.25.refs_1_.refs_3_), channel_id=1, source_target_pairs={{1,2},{2,1},{5,6},{6,5},{9,10},{10,9},{13,14},{14,13},{17,18},{18,... | collective-permute-start | bytes 1179656 | tf_op jit(solution)/shard_map/ppermute | solution.py:385
  94.3 12.3 %collective-permute-start.44 = (bf16[3,64,1024]{2,1,0:T(8,128)(2,1)S(1)}, bf16[3,64,1024]{2,1,0:T(8,128)(2,1)S(1)}, u32[]{:S(2)}, u32[]{:S(2)}) collective-permute-start(bf16[3,64,1024]{2,1,0:T(8,128)(2,1)S(1)} %pass_on.26.refs_1_.refs_4_), channel_id=1, source_target_pairs={{2,3},{1,0},{6,7},{5,4},{10,11},{9,8},{14,15},{13,12},{18,19},{17,... | collective-permute-start | bytes 1179656 | tf_op jit(solution)/shard_map/ppermute | solution.py:385
  99.3 7.4 %collective-permute-start.43 = (bf16[3,64,1024]{2,1,0:T(8,128)(2,1)S(1)}, bf16[3,64,1024]{2,1,0:T(8,128)(2,1)S(1)}, u32[]{:S(2)}, u32[]{:S(2)}) collective-permute-start(bf16[3,64,1024]{2,1,0:T(8,128)(2,1)S(1)} %pass_on.28.refs_1_.refs_3_), channel_id=1, source_target_pairs={{1,2},{2,1},{5,6},{6,5},{9,10},{10,9},{13,14},{14,13},{17,18},{18,... | collective-permute-start | bytes 1179656 | tf_op jit(solution)/shard_map/ppermute | solution.py:385
  106.7 14.3 %collective-permute-start.46 = (bf16[3,64,1024]{2,1,0:T(8,128)(2,1)S(1)}, bf16[3,64,1024]{2,1,0:T(8,128)(2,1)S(1)}, u32[]{:S(2)}, u32[]{:S(2)}) collective-permute-start(bf16[3,64,1024]{2,1,0:T(8,128)(2,1)S(1)} %pass_on.29.refs_9_.refs_4_), channel_id=1, source_target_pairs={{2,3},{1,0},{6,7},{5,4},{10,11},{9,8},{14,15},{13,12},{18,19},{17,... | collective-permute-start | bytes 1179656 | tf_op jit(solution)/shard_map/ppermute | solution.py:385
  111.7 2.0 %collective-permute-start.47 = (bf16[64,1024]{1,0:T(8,128)(2,1)S(1)}, bf16[64,1024]{1,0:T(8,128)(2,1)S(1)}, u32[]{:S(2)}, u32[]{:S(2)}) collective-permute-start(bf16[64,1024]{1,0:T(8,128)(2,1)S(1)} %get-tuple-element.91), channel_id=1, source_target_pairs={{0,16},{16,0},{1,17},{17,1},{2,18},{18,2},{3,19},{19,3},{4,20},{20... | collective-permute-start | bytes 393224 | tf_op jit(solution)/shard_map/ppermute | solution.py:51
  111.8 18.2 %collective-permute-start.45 = (bf16[3,64,1024]{2,1,0:T(8,128)(2,1)S(1)}, bf16[3,64,1024]{2,1,0:T(8,128)(2,1)S(1)}, u32[]{:S(2)}, u32[]{:S(2)}) collective-permute-start(bf16[3,64,1024]{2,1,0:T(8,128)(2,1)S(1)} %pass_on.31.refs_9_.refs_4_), channel_id=1, source_target_pairs={{2,3},{1,0},{6,7},{5,4},{10,11},{9,8},{14,15},{13,12},{18,19},{17,... | collective-permute-start | bytes 1179656 | tf_op jit(solution)/shard_map/ppermute | solution.py:385
  113.1 1.5 collective-permute-start.48
  113.6 1.3 collective-permute-start.49
  113.7 1.5 collective-permute-start.50
  115.3 21.9 %collective-permute-start.59 = (bf16[2,128,1024]{2,1,0:T(8,128)(2,1)S(1)}, bf16[2,128,1024]{2,1,0:T(8,128)(2,1)S(1)}, u32[]{:S(2)}, u32[]{:S(2)}) collective-permute-start(bf16[2,128,1024]{2,1,0:T(8,128)(2,1)S(1)} %add_quarters.4.refs_1_), channel_id=1, source_target_pairs={{0,4},{4,0},{8,12},{12,8},{1,5},{5,1},{9,13},{13,9},{2,6},{6,2},{1... | collective-permute-start | bytes 1572872 | tf_op jit(solution)/shard_map/ppermute | solution.py:51
  124.5 5.5 %collective-permute-start.51 = (bf16[64,1024]{1,0:T(8,128)(2,1)S(1)}, bf16[64,1024]{1,0:T(8,128)(2,1)S(1)}, u32[]{:S(2)}, u32[]{:S(2)}) collective-permute-start(bf16[64,1024]{1,0:T(8,128)(2,1)S(1)} %get-tuple-element.96), channel_id=1, source_target_pairs={{0,16},{16,0},{1,17},{17,1},{2,18},{18,2},{3,19},{19,3},{4,20},{20... | collective-permute-start | bytes 393224 | tf_op jit(solution)/shard_map/ppermute | solution.py:51
  124.5 5.4 %collective-permute-start.52 = (bf16[64,1024]{1,0:T(8,128)(2,1)S(1)}, bf16[64,1024]{1,0:T(8,128)(2,1)S(1)}, u32[]{:S(2)}, u32[]{:S(2)}) collective-permute-start(bf16[64,1024]{1,0:T(8,128)(2,1)S(1)} %get-tuple-element.97), channel_id=1, source_target_pairs={{0,16},{16,0},{1,17},{17,1},{2,18},{18,2},{3,19},{19,3},{4,20},{20... | collective-permute-start | bytes 393224 | tf_op jit(solution)/shard_map/ppermute | solution.py:51
  125.0 4.9 %collective-permute-start.53 = (bf16[64,1024]{1,0:T(8,128)(2,1)S(1)}, bf16[64,1024]{1,0:T(8,128)(2,1)S(1)}, u32[]{:S(2)}, u32[]{:S(2)}) collective-permute-start(bf16[64,1024]{1,0:T(8,128)(2,1)S(1)} %get-tuple-element.98), channel_id=1, source_target_pairs={{0,16},{16,0},{1,17},{17,1},{2,18},{18,2},{3,19},{19,3},{4,20},{20... | collective-permute-start | bytes 393224 | tf_op jit(solution)/shard_map/ppermute | solution.py:51
  129.9 1.3 collective-permute-start.54
  134.9 1.4 collective-permute-start.55
  135.2 25.4 %collective-permute-start.60 = (bf16[2,128,1024]{2,1,0:T(8,128)(2,1)S(1)}, bf16[2,128,1024]{2,1,0:T(8,128)(2,1)S(1)}, u32[]{:S(2)}, u32[]{:S(2)}) collective-permute-start(bf16[2,128,1024]{2,1,0:T(8,128)(2,1)S(1)} %add_quarters.5.refs_9_), channel_id=1, source_target_pairs={{0,8},{4,12},{8,0},{12,4},{1,9},{5,13},{9,1},{13,5},{2,10},{6,14},... | collective-permute-start | bytes 1572872 | tf_op jit(solution)/shard_map/ppermute | solution.py:51
  135.7 1.3 collective-permute-start.56
  135.8 1.8 %collective-permute-start.57 = (bf16[64,1024]{1,0:T(8,128)(2,1)S(1)}, bf16[64,1024]{1,0:T(8,128)(2,1)S(1)}, u32[]{:S(2)}, u32[]{:S(2)}) collective-permute-start(bf16[64,1024]{1,0:T(8,128)(2,1)S(1)} %get-tuple-element.103), channel_id=1, source_target_pairs={{0,16},{16,0},{1,17},{17,1},{2,18},{18,2},{3,19},{19,3},{4,20},{20... | collective-permute-start | bytes 393224 | tf_op jit(solution)/shard_map/ppermute | solution.py:51
  136.4 1.3 collective-permute-start.58
  137.0 3.8 %collective-permute-start.39 = (bf16[64,1024]{1,0:T(8,128)(2,1)S(1)}, bf16[64,1024]{1,0:T(8,128)(2,1)S(1)}, u32[]{:S(2)}, u32[]{:S(2)}) collective-permute-start(bf16[64,1024]{1,0:T(8,128)(2,1)S(1)} %get-tuple-element.86), channel_id=1, source_target_pairs={{0,16},{16,0},{1,17},{17,1},{2,18},{18,2},{3,19},{19,3},{4,20},{20... | collective-permute-start | bytes 393224 | tf_op jit(solution)/shard_map/ppermute | solution.py:51
  137.2 3.6 %collective-permute-start.40 = (bf16[64,1024]{1,0:T(8,128)(2,1)S(1)}, bf16[64,1024]{1,0:T(8,128)(2,1)S(1)}, u32[]{:S(2)}, u32[]{:S(2)}) collective-permute-start(bf16[64,1024]{1,0:T(8,128)(2,1)S(1)} %get-tuple-element.87), channel_id=1, source_target_pairs={{0,16},{16,0},{1,17},{17,1},{2,18},{18,2},{3,19},{19,3},{4,20},{20... | collective-permute-start | bytes 393224 | tf_op jit(solution)/shard_map/ppermute | solution.py:51
  137.8 22.8 %collective-permute-start.61 = (bf16[1,128,1024]{2,1,0:T(8,128)(2,1)S(1)}, bf16[1,128,1024]{2,1,0:T(8,128)(2,1)S(1)}, u32[]{:S(2)}, u32[]{:S(2)}) collective-permute-start(bf16[1,128,1024]{2,1,0:T(8,128)(2,1)S(1)} %get-tuple-element.105.refs_5_), channel_id=1, source_target_pairs={{0,12},{4,8},{8,4},{12,0},{1,13},{5,9},{9,5},{13,1},{2,14},{6,10},... | collective-permute-start | bytes 786440 | tf_op jit(solution)/shard_map/ppermute | solution.py:51
  139.2 21.4 %collective-permute-start.62 = (bf16[1,128,1024]{2,1,0:T(8,128)(2,1)S(1)}, bf16[1,128,1024]{2,1,0:T(8,128)(2,1)S(1)}, u32[]{:S(2)}, u32[]{:S(2)}) collective-permute-start(bf16[1,128,1024]{2,1,0:T(8,128)(2,1)S(1)} %get-tuple-element.111), channel_id=1, source_target_pairs={{0,12},{4,8},{8,4},{12,0},{1,13},{5,9},{9,5},{13,1},{2,14},{6,10},... | collective-permute-start | bytes 786440 | tf_op jit(solution)/shard_map/ppermute | solution.py:51
  140.8 1.3 collective-permute-start.41
  140.8 1.5 collective-permute-start.42
  (7 other events, 26.9 us)

commit v6 on v5

--- a/solution.py
+++ b/solution.py
@@ -351,8 +351,8 @@
 WEIGHTS = -1
 FOUR = (
     0, 1, 2, 1, 2, 0, 3, 1, 0, 3, 2, 1, 0, 3, 2, 1, 0, 3, 2, 1,
-    0, 3, 2, 1, 0, 3, 2, 0, 1, 3, 1, 1, 2, 2, 3, 2, 3, 1, 3, 0,
-    WEIGHTS, 2, 3,
+    0, 3, 2, 1, 0, 3, 2, 0, 1, 1, 3, 2, 1, 2, 2, 3, 3, 1, 3, 2,
+    WEIGHTS, 0, 3,
 )
 
 

time: 162 us -> 157 us (0.969)
  waiting for transfers between devices: 45.4 us -> 39.3 us
    ppermute x39, waiting for transfers between devices: 19.7 us -> 6.38 us  [swap(): return lax.ppermute(value, axis, [(i, i ^ mask) for i in range(size)])]
    ppermute x24, waiting for transfers between devices: 25.7 us -> 32.9 us  [hop(): return lax.ppermute(value, 'gz', pairs)]
  transfers between devices with their start and end apart: 63 -> 63, of which waited for: 25 -> 23; matrix products, arithmetic and copies ran while one was open for 0% -> 0% of each run, Pallas kernels for 23% -> 22%
where the time goes in v6:
time: 157 us; the launch traced here: 156 us
  starting transfers between devices  68.1 us (43%)
  waiting for transfers between devices  39.3 us (25%)
  Pallas kernels  39.1 us (25%)
  local copies, waits for them, and re-layouts  8.47 us (5%)
    ppermute x24, starting transfers between devices, hop(): return lax.ppermute(value, 'gz', pairs)  51.1 us
    pallas_call x50, Pallas kernels, call(): pl.pallas_call(kernel, in_specs=in_specs, out_specs=out_specs, out_shape=...  39.1 us
    ppermute x24, waiting for transfers between devices, hop(): return lax.ppermute(value, 'gz', pairs)  32.9 us
    ppermute x39, starting transfers between devices, swap(): return lax.ppermute(value, axis, [(i, i ^ mask) for i in range(size)])  17 us
    unnamed x16, local copies, waits for them, and re-layouts  8.47 us
    ppermute x39, waiting for transfers between devices, swap(): return lax.ppermute(value, axis, [(i, i ^ mask) for i in range(size)])  6.38 us
  transfers between devices with their start and end apart: 63, of which 23 were waited for; matrix products, arithmetic and copies ran while one was open for 0% of the time, Pallas kernels for 22%

profile of v6, /device:TPU:0, one launch (start us, length us, event | category | flops | bytes accessed | tf_op | source)
XLA Modules:
  0.0 156.2 jit_solution(10479814875093792713)
XLA Ops:
  0.6 0.9 copy-done.6
  1.6 0.9 copy-done.7
  2.5 0.7 ordered_rows.1.refs_0_.refs_1_
  3.3 3.0 %collective-permute-start.6 = (bf16[2,128,1024]{2,1,0:T(8,128)(2,1)S(1)}, bf16[2,128,1024]{2,1,0:T(8,128)(2,1)S(1)}, u32[]{:S(2)}, u32[]{:S(2)}) collective-permute-start(bf16[2,128,1024]{2,1,0:T(8,128)(2,1)S(1)} %ordered_rows.1.refs_0_.refs_1_), channel_id=1, source_target_pairs={{0,4},{4,0},{8,12},{12,8},{1,5},{5,1},{9,13},{13,9},{2,6},{6,2},{1... | collective-permute-start | bytes 1572872 | tf_op jit(solution)/shard_map/ppermute | solution.py:51
  6.3 1.5 collective-permute-start.5
  8.5 0.8 collective-permute-done.1.refs_3_.refs_6_
  9.8 0.8 collective-permute-done.refs_2_.refs_5_
  10.6 2.2 %copy-done = bf16[2048,1024]{1,0:T(8,128)(2,1)S(1)} copy-done((bf16[2048,1024]{1,0:T(8,128)(2,1)S(1)}, bf16[2048,1024]{1,0:T(8,128)(2,1)}, u32[]{:S(2)}) %copy-start) | copy-done | bytes 4194328
  12.8 2.2 %copy-done.2 = bf16[2048,1024]{1,0:T(8,128)(2,1)S(1)} copy-done((bf16[2048,1024]{1,0:T(8,128)(2,1)S(1)}, bf16[2048,1024]{1,0:T(8,128)(2,1)}, u32[]{:S(2)}) %copy-start.2) | copy-done | bytes 4194328
  15.0 2.2 %copy-done.4 = bf16[2048,1024]{1,0:T(8,128)(2,1)S(1)} copy-done((bf16[2048,1024]{1,0:T(8,128)(2,1)S(1)}, bf16[2048,1024]{1,0:T(8,128)(2,1)}, u32[]{:S(2)}) %copy-start.4) | copy-done | bytes 4194328
  17.2 2.7 %forward_products.4 = (bf16[3,64,1024]{2,1,0:T(8,128)(2,1)S(1)}, bf16[3,64,1024]{2,1,0:T(8,128)(2,1)S(1)}) custom-call(s32[1]{0:T(128)} %bitcast.1.refs_0_, bf16[2,128,1024]{2,1,0:T(8,128)(2,1)S(1)} %ordered_rows.1.refs_0_.refs_1_, bf16[64,1024]{1,0:T(8,128)(2,1)S(1)} %collective-permute-done.refs_2_.refs_5_, ...), custom_call_target="tpu_custom_call" | custom-call | flops 1000 | bytes 1000 | tf_op jit(solution)/shard_map/forward_products/pallas_call | solution.py:36
  20.2 3.6 %collective-permute-start.4 = (bf16[3,64,1024]{2,1,0:T(8,128)(2,1)S(1)}, bf16[3,64,1024]{2,1,0:T(8,128)(2,1)S(1)}, u32[]{:S(2)}, u32[]{:S(2)}) collective-permute-start(bf16[3,64,1024]{2,1,0:T(8,128)(2,1)S(1)} %get-tuple-element.66.refs_0_), channel_id=1, source_target_pairs={{0,1},{3,2},{4,5},{7,6},{8,9},{11,10},{12,13},{15,14},{16,17},{19,... | collective-permute-start | bytes 1179656 | tf_op jit(solution)/shard_map/ppermute | solution.py:385
  25.8 0.5 collective-permute-start.10
  26.4 2.7 %forward_products.5 = (bf16[3,64,1024]{2,1,0:T(8,128)(2,1)S(1)}, bf16[3,64,1024]{2,1,0:T(8,128)(2,1)S(1)}) custom-call(s32[1]{0:T(128)} %bitcast.1.refs_0_, bf16[2,128,1024]{2,1,0:T(8,128)(2,1)S(1)} %pass_on.19.refs_0_.refs_1_.refs_2_, bf16[64,1024]{1,0:T(8,128)(2,1)S(1)} %collective-permute-done.11.refs_2_.refs_9_, ...), custom_call_target="tpu_custom_call" | custom-call | flops 1000 | bytes 1000 | tf_op jit(solution)/shard_map/forward_products/pallas_call | solution.py:36
  29.1 1.3 collective-permute-start.16
  30.4 2.7 %forward_products.6 = (bf16[3,64,1024]{2,1,0:T(8,128)(2,1)S(1)}, bf16[3,64,1024]{2,1,0:T(8,128)(2,1)S(1)}) custom-call(s32[1]{0:T(128)} %bitcast.1.refs_0_, bf16[2,128,1024]{2,1,0:T(8,128)(2,1)S(1)} %pass_on.20.refs_0_.refs_1_.refs_3_, bf16[64,1024]{1,0:T(8,128)(2,1)S(1)} %collective-permute-done.7.refs_2_.refs_13_, ...), custom_call_target="tpu_custom_call" | custom-call | flops 1000 | bytes 1000 | tf_op jit(solution)/shard_map/forward_products/pallas_call | solution.py:36
  33.3 0.7 collective-permute-start.15
  34.0 7.2 %collective-permute-start.20 = (bf16[3,64,1024]{2,1,0:T(8,128)(2,1)S(1)}, bf16[3,64,1024]{2,1,0:T(8,128)(2,1)S(1)}, u32[]{:S(2)}, u32[]{:S(2)}) collective-permute-start(bf16[3,64,1024]{2,1,0:T(8,128)(2,1)S(1)} %get-tuple-element.79.refs_0_), channel_id=1, source_target_pairs={{0,1},{3,2},{4,5},{7,6},{8,9},{11,10},{12,13},{15,14},{16,17},{19,... | collective-permute-start | bytes 1179656 | tf_op jit(solution)/shard_map/ppermute | solution.py:385
  42.7 0.7 collective-permute-start.19
  43.5 1.3 collective-permute-start.18
  44.8 2.7 %forward_products.7 = (bf16[3,64,1024]{2,1,0:T(8,128)(2,1)S(1)}, bf16[3,64,1024]{2,1,0:T(8,128)(2,1)S(1)}) custom-call(s32[1]{0:T(128)} %bitcast.1.refs_0_, bf16[2,128,1024]{2,1,0:T(8,128)(2,1)S(1)} %pass_on.21.refs_0_.refs_1_.refs_4_, bf16[64,1024]{1,0:T(8,128)(2,1)S(1)} %collective-permute-done.21.refs_2_.refs_17_, ...), custom_call_target="tpu_custom_call" | custom-call | flops 1000 | bytes 1000 | tf_op jit(solution)/shard_map/forward_products/pallas_call | solution.py:36
  47.5 9.9 %collective-permute-start.28 = (bf16[3,64,1024]{2,1,0:T(8,128)(2,1)S(1)}, bf16[3,64,1024]{2,1,0:T(8,128)(2,1)S(1)}, u32[]{:S(2)}, u32[]{:S(2)}) collective-permute-start(bf16[3,64,1024]{2,1,0:T(8,128)(2,1)S(1)} %get-tuple-element.84.refs_0_), channel_id=1, source_target_pairs={{0,1},{3,2},{4,5},{7,6},{8,9},{11,10},{12,13},{15,14},{16,17},{19,... | collective-permute-start | bytes 1179656 | tf_op jit(solution)/shard_map/ppermute | solution.py:385
  57.6 0.7 collective-permute-start.27
  58.4 1.3 collective-permute-start.26
  59.7 2.6 %collective-permute-done.18.refs_1_ = bf16[3,64,1024]{2,1,0:T(8,128)(2,1)S(1)} collective-permute-done((bf16[3,64,1024]{2,1,0:T(8,128)(2,1)S(1)}, bf16[3,64,1024]{2,1,0:T(8,128)(2,1)S(1)}, u32[]{:S(2)}, u32[]{:S(2)}) %collective-permute-start.18) | collective-permute-done | bytes 393248 | tf_op jit(solution)/shard_map/ppermute | solution.py:385
  62.4 2.4 %collective-permute-start.25 = (bf16[3,64,1024]{2,1,0:T(8,128)(2,1)S(1)}, bf16[3,64,1024]{2,1,0:T(8,128)(2,1)S(1)}, u32[]{:S(2)}, u32[]{:S(2)}) collective-permute-start(bf16[3,64,1024]{2,1,0:T(8,128)(2,1)S(1)} %activations.4.refs_2_), channel_id=1, source_target_pairs={{0,1},{3,2},{4,5},{7,6},{8,9},{11,10},{12,13},{15,14},{16,17},{19,... | collective-permute-start | bytes 1179656 | tf_op jit(solution)/shard_map/ppermute | solution.py:385
  64.9 2.0 %collective-permute-done.28.refs_1_ = bf16[3,64,1024]{2,1,0:T(8,128)(2,1)S(1)} collective-permute-done((bf16[3,64,1024]{2,1,0:T(8,128)(2,1)S(1)}, bf16[3,64,1024]{2,1,0:T(8,128)(2,1)S(1)}, u32[]{:S(2)}, u32[]{:S(2)}) %collective-permute-start.28) | collective-permute-done | bytes 393248 | tf_op jit(solution)/shard_map/ppermute | solution.py:385
  67.0 0.7 collective-permute-start.32
  67.8 1.3 collective-permute-start.31
  69.1 2.6 %collective-permute-done.26.refs_1_ = bf16[3,64,1024]{2,1,0:T(8,128)(2,1)S(1)} collective-permute-done((bf16[3,64,1024]{2,1,0:T(8,128)(2,1)S(1)}, bf16[3,64,1024]{2,1,0:T(8,128)(2,1)S(1)}, u32[]{:S(2)}, u32[]{:S(2)}) %collective-permute-start.26) | collective-permute-done | bytes 393248 | tf_op jit(solution)/shard_map/ppermute | solution.py:385
  71.9 3.2 %collective-permute-start.30 = (bf16[3,64,1024]{2,1,0:T(8,128)(2,1)S(1)}, bf16[3,64,1024]{2,1,0:T(8,128)(2,1)S(1)}, u32[]{:S(2)}, u32[]{:S(2)}) collective-permute-start(bf16[3,64,1024]{2,1,0:T(8,128)(2,1)S(1)} %activations.5.refs_1_.refs_2_), channel_id=1, source_target_pairs={{0,1},{3,2},{4,5},{7,6},{8,9},{11,10},{12,13},{15,14},{16,17},{19,... | collective-permute-start | bytes 1179656 | tf_op jit(solution)/shard_map/ppermute | solution.py:385
  75.2 0.7 collective-permute-start.29
  76.0 1.3 collective-permute-start.36
  77.3 3.6 %collective-permute-done.31.refs_1_ = bf16[3,64,1024]{2,1,0:T(8,128)(2,1)S(1)} collective-permute-done((bf16[3,64,1024]{2,1,0:T(8,128)(2,1)S(1)}, bf16[3,64,1024]{2,1,0:T(8,128)(2,1)S(1)}, u32[]{:S(2)}, u32[]{:S(2)}) %collective-permute-start.31) | collective-permute-done | bytes 393248 | tf_op jit(solution)/shard_map/ppermute | solution.py:385
  81.1 3.5 %collective-permute-start.35 = (bf16[3,64,1024]{2,1,0:T(8,128)(2,1)S(1)}, bf16[3,64,1024]{2,1,0:T(8,128)(2,1)S(1)}, u32[]{:S(2)}, u32[]{:S(2)}) collective-permute-start(bf16[3,64,1024]{2,1,0:T(8,128)(2,1)S(1)} %activations.6.refs_1_.refs_2_), channel_id=1, source_target_pairs={{0,1},{3,2},{4,5},{7,6},{8,9},{11,10},{12,13},{15,14},{16,17},{19,... | collective-permute-start | bytes 1179656 | tf_op jit(solution)/shard_map/ppermute | solution.py:385
  84.7 0.7 collective-permute-start.34
  85.4 1.3 collective-permute-start.33
  86.7 2.8 %collective-permute-done.36.refs_1_ = bf16[3,64,1024]{2,1,0:T(8,128)(2,1)S(1)} collective-permute-done((bf16[3,64,1024]{2,1,0:T(8,128)(2,1)S(1)}, bf16[3,64,1024]{2,1,0:T(8,128)(2,1)S(1)}, u32[]{:S(2)}, u32[]{:S(2)}) %collective-permute-start.36) | collective-permute-done | bytes 393248 | tf_op jit(solution)/shard_map/ppermute | solution.py:385
  89.7 4.1 %collective-permute-start.38 = (bf16[3,64,1024]{2,1,0:T(8,128)(2,1)S(1)}, bf16[3,64,1024]{2,1,0:T(8,128)(2,1)S(1)}, u32[]{:S(2)}, u32[]{:S(2)}) collective-permute-start(bf16[3,64,1024]{2,1,0:T(8,128)(2,1)S(1)} %activations.7.refs_1_.refs_2_), channel_id=1, source_target_pairs={{0,1},{3,2},{4,5},{7,6},{8,9},{11,10},{12,13},{15,14},{16,17},{19,... | collective-permute-start | bytes 1179656 | tf_op jit(solution)/shard_map/ppermute | solution.py:385
  93.8 0.7 collective-permute-start.37
  94.5 1.3 collective-permute-start.43
  95.8 2.1 %collective-permute-done.33.refs_0_ = bf16[3,64,1024]{2,1,0:T(8,128)(2,1)S(1)} collective-permute-done((bf16[3,64,1024]{2,1,0:T(8,128)(2,1)S(1)}, bf16[3,64,1024]{2,1,0:T(8,128)(2,1)S(1)}, u32[]{:S(2)}, u32[]{:S(2)}) %collective-permute-start.33) | collective-permute-done | bytes 393248 | tf_op jit(solution)/shard_map/ppermute | solution.py:385
  98.0 1.9 %collective-permute-done.38.refs_0_ = bf16[3,64,1024]{2,1,0:T(8,128)(2,1)S(1)} collective-permute-done((bf16[3,64,1024]{2,1,0:T(8,128)(2,1)S(1)}, bf16[3,64,1024]{2,1,0:T(8,128)(2,1)S(1)}, u32[]{:S(2)}, u32[]{:S(2)}) %collective-permute-start.38) | collective-permute-done | bytes 393248 | tf_op jit(solution)/shard_map/ppermute | solution.py:385
  99.9 0.7 collective-permute-start.45
  100.6 1.3 collective-permute-start.44
  101.9 3.5 %backward_products.4 = (bf16[2,128,1024]{2,1,0:T(8,128)(2,1)S(1)}, bf16[3,128,1024]{2,1,0:T(8,128)(2,1)S(1)}, bf16[64,1024]{1,0:T(8,128)(2,1)S(1)}, bf16[64,1024...) custom-call(s32[1]{0:T(128)} %bitcast.1.refs_0_, s32[1]{0:T(128)} %bitcast.2.refs_1_, ...), custom_call_target="tpu_custom_call" | custom-call | flops 1000 | bytes 1000 | tf_op jit(solution)/shard_map/backward_products/pallas_call | solution.py:36
  105.4 1.9 %collective-permute-done.43.refs_0_ = bf16[3,64,1024]{2,1,0:T(8,128)(2,1)S(1)} collective-permute-done((bf16[3,64,1024]{2,1,0:T(8,128)(2,1)S(1)}, bf16[3,64,1024]{2,1,0:T(8,128)(2,1)S(1)}, u32[]{:S(2)}, u32[]{:S(2)}) %collective-permute-start.43) | collective-permute-done | bytes 393248 | tf_op jit(solution)/shard_map/ppermute | solution.py:385
  107.3 3.7 %backward_products.5 = (bf16[2,128,1024]{2,1,0:T(8,128)(2,1)S(1)}, bf16[3,128,1024]{2,1,0:T(8,128)(2,1)S(1)}, bf16[64,1024]{1,0:T(8,128)(2,1)S(1)}, bf16[64,1024...) custom-call(s32[1]{0:T(128)} %bitcast.1.refs_0_, s32[1]{0:T(128)} %bitcast.2.refs_1_, ...), custom_call_target="tpu_custom_call" | custom-call | flops 1000 | bytes 1000 | tf_op jit(solution)/shard_map/backward_products/pallas_call | solution.py:36
  112.1 3.3 %collective-permute-done.44.refs_0_ = bf16[3,64,1024]{2,1,0:T(8,128)(2,1)S(1)} collective-permute-done((bf16[3,64,1024]{2,1,0:T(8,128)(2,1)S(1)}, bf16[3,64,1024]{2,1,0:T(8,128)(2,1)S(1)}, u32[]{:S(2)}, u32[]{:S(2)}) %collective-permute-start.44) | collective-permute-done | bytes 393248 | tf_op jit(solution)/shard_map/ppermute | solution.py:385
  115.5 3.5 %backward_products.6 = (bf16[2,128,1024]{2,1,0:T(8,128)(2,1)S(1)}, bf16[3,128,1024]{2,1,0:T(8,128)(2,1)S(1)}, bf16[64,1024]{1,0:T(8,128)(2,1)S(1)}, bf16[64,1024...) custom-call(s32[1]{0:T(128)} %bitcast.1.refs_0_, s32[1]{0:T(128)} %bitcast.2.refs_1_, ...), custom_call_target="tpu_custom_call" | custom-call | flops 1000 | bytes 1000 | tf_op jit(solution)/shard_map/backward_products/pallas_call | solution.py:36
  119.1 1.3 collective-permute-start.50
  120.4 0.6 collective-permute-start.60
  121.8 0.6 collective-permute-done.52.refs_2_
  123.0 0.9 collective-permute-start.55
  123.9 9.9 %collective-permute-done.50.refs_0_ = bf16[3,64,1024]{2,1,0:T(8,128)(2,1)S(1)} collective-permute-done((bf16[3,64,1024]{2,1,0:T(8,128)(2,1)S(1)}, bf16[3,64,1024]{2,1,0:T(8,128)(2,1)S(1)}, u32[]{:S(2)}, u32[]{:S(2)}) %collective-permute-start.50) | collective-permute-done | bytes 393248 | tf_op jit(solution)/shard_map/ppermute | solution.py:385
  133.9 3.5 %backward_products.7 = (bf16[2,128,1024]{2,1,0:T(8,128)(2,1)S(1)}, bf16[3,128,1024]{2,1,0:T(8,128)(2,1)S(1)}, bf16[64,1024]{1,0:T(8,128)(2,1)S(1)}, bf16[64,1024...) custom-call(s32[1]{0:T(128)} %bitcast.1.refs_0_, s32[1]{0:T(128)} %bitcast.2.refs_1_, ...), custom_call_target="tpu_custom_call" | custom-call | flops 1000 | bytes 1000 | tf_op jit(solution)/shard_map/backward_products/pallas_call | solution.py:36
  138.1 0.8 collective-permute-done.56.refs_1_
  139.3 0.8 collective-permute-done.59.refs_4_
  140.3 0.9 collective-permute-start.61
  141.2 2.1 %collective-permute-start.62 = (bf16[1,128,1024]{2,1,0:T(8,128)(2,1)S(1)}, bf16[1,128,1024]{2,1,0:T(8,128)(2,1)S(1)}, u32[]{:S(2)}, u32[]{:S(2)}) collective-permute-start(bf16[1,128,1024]{2,1,0:T(8,128)(2,1)S(1)} %get-tuple-element.111), channel_id=1, source_target_pairs={{0,12},{4,8},{8,4},{12,0},{1,13},{5,9},{9,5},{13,1},{2,14},{6,10},... | collective-permute-start | bytes 786440 | tf_op jit(solution)/shard_map/ppermute | solution.py:51
  143.3 0.5 collective-permute-start.41
  143.9 10.0 %weight_grads.1 = (bf16[16,128]{1,0:T(8,128)(2,1)S(1)}, f32[2048,1024]{1,0:T(8,128)}, f32[2048,1024]{1,0:T(8,128)}, f32[2048,1024]{1,0:T(8,128)}) custom-call(s32[1]{0:T(128)} %bitcast.1.refs_0_, bf16[2,128,1024]{2,1,0:T(8,128)(2,1)S(1)} %ordered_rows.1.refs_0_.refs_1_, bf16[2,128,1024]{2,1,0:T(8,128)(2,1)S(1)} %pass_on.19.refs_0_.refs_1_.refs_2_, ...), custom_call_target="tpu_custom_call" | custom-call | flops 1000 | bytes 1000 | tf_op jit(solution)/shard_map/weight_grads/pallas_call | solution.py:36
  154.0 1.2 collective-permute-done.62.refs_0_
  155.2 1.0 final_sum.1
  (128 shorter events, 10.9 us)
Async XLA Ops:
  3.3 16.6 %collective-permute-start.6 = (bf16[2,128,1024]{2,1,0:T(8,128)(2,1)S(1)}, bf16[2,128,1024]{2,1,0:T(8,128)(2,1)S(1)}, u32[]{:S(2)}, u32[]{:S(2)}) collective-permute-start(bf16[2,128,1024]{2,1,0:T(8,128)(2,1)S(1)} %ordered_rows.1.refs_0_.refs_1_), channel_id=1, source_target_pairs={{0,4},{4,0},{8,12},{12,8},{1,5},{5,1},{9,13},{13,9},{2,6},{6,2},{1... | collective-permute-start | bytes 1572872 | tf_op jit(solution)/shard_map/ppermute | solution.py:51
  6.3 18.1 %collective-permute-start.5 = (bf16[2,128,1024]{2,1,0:T(8,128)(2,1)S(1)}, bf16[2,128,1024]{2,1,0:T(8,128)(2,1)S(1)}, u32[]{:S(2)}, u32[]{:S(2)}) collective-permute-start(bf16[2,128,1024]{2,1,0:T(8,128)(2,1)S(1)} %ordered_rows.1.refs_0_.refs_1_), channel_id=1, source_target_pairs={{0,8},{4,12},{8,0},{12,4},{1,9},{5,13},{9,1},{13,5},{2,10},{6,14},... | collective-permute-start | bytes 1572872 | tf_op jit(solution)/shard_map/ppermute | solution.py:51
  7.8 1.4 collective-permute-start.1
  7.9 1.5 collective-permute-start.2
  8.4 1.3 collective-permute-start.3
  9.3 1.3 collective-permute-start
  17.2 9.2 %copy-start.5 = (bf16[2048,1024]{1,0:T(8,128)(2,1)S(1)}, bf16[2048,1024]{1,0:T(8,128)(2,1)}, u32[]{:S(2)}) copy-start(bf16[2048,1024]{1,0:T(8,128)(2,1)} %refs_8_.15) | copy-start | bytes 12582916
  20.0 4.6 %collective-permute-start.12 = (bf16[64,1024]{1,0:T(8,128)(2,1)S(1)}, bf16[64,1024]{1,0:T(8,128)(2,1)S(1)}, u32[]{:S(2)}, u32[]{:S(2)}) collective-permute-start(bf16[64,1024]{1,0:T(8,128)(2,1)S(1)} %get-tuple-element.72), channel_id=1, source_target_pairs={{0,16},{16,0},{1,17},{17,1},{2,18},{18,2},{3,19},{19,3},{4,20},{20... | collective-permute-start | bytes 393224 | tf_op jit(solution)/shard_map/ppermute | solution.py:51
  20.2 13.0 %collective-permute-start.4 = (bf16[3,64,1024]{2,1,0:T(8,128)(2,1)S(1)}, bf16[3,64,1024]{2,1,0:T(8,128)(2,1)S(1)}, u32[]{:S(2)}, u32[]{:S(2)}) collective-permute-start(bf16[3,64,1024]{2,1,0:T(8,128)(2,1)S(1)} %get-tuple-element.66.refs_0_), channel_id=1, source_target_pairs={{0,1},{3,2},{4,5},{7,6},{8,9},{11,10},{12,13},{15,14},{16,17},{19,... | collective-permute-start | bytes 1179656 | tf_op jit(solution)/shard_map/ppermute | solution.py:385
  23.8 1.4 collective-permute-start.13
  24.0 1.8 %collective-permute-start.14 = (bf16[64,1024]{1,0:T(8,128)(2,1)S(1)}, bf16[64,1024]{1,0:T(8,128)(2,1)S(1)}, u32[]{:S(2)}, u32[]{:S(2)}) collective-permute-start(bf16[64,1024]{1,0:T(8,128)(2,1)S(1)} %get-tuple-element.74), channel_id=1, source_target_pairs={{0,16},{16,0},{1,17},{17,1},{2,18},{18,2},{3,19},{19,3},{4,20},{20... | collective-permute-start | bytes 393224 | tf_op jit(solution)/shard_map/ppermute | solution.py:51
  24.4 1.3 collective-permute-start.11
  24.5 1.7 %collective-permute-start.8 = (bf16[64,1024]{1,0:T(8,128)(2,1)S(1)}, bf16[64,1024]{1,0:T(8,128)(2,1)S(1)}, u32[]{:S(2)}, u32[]{:S(2)}) collective-permute-start(bf16[64,1024]{1,0:T(8,128)(2,1)S(1)} %get-tuple-element.69), channel_id=1, source_target_pairs={{0,16},{16,0},{1,17},{17,1},{2,18},{18,2},{3,19},{19,3},{4,20},{20... | collective-permute-start | bytes 393224 | tf_op jit(solution)/shard_map/ppermute | solution.py:51
  25.2 16.0 %collective-permute-start.17 = (bf16[2,128,1024]{2,1,0:T(8,128)(2,1)S(1)}, bf16[2,128,1024]{2,1,0:T(8,128)(2,1)S(1)}, u32[]{:S(2)}, u32[]{:S(2)}) collective-permute-start(bf16[2,128,1024]{2,1,0:T(8,128)(2,1)S(1)} %pass_on.19.refs_0_.refs_1_.refs_2_), channel_id=1, source_target_pairs={{0,8},{4,12},{8,0},{12,4},{1,9},{5,13},{9,1},{13,5},{2,10},{6,14},... | collective-permute-start | bytes 1572872 | tf_op jit(solution)/shard_map/ppermute | solution.py:51
  25.8 3.3 %collective-permute-start.9 = (bf16[64,1024]{1,0:T(8,128)(2,1)S(1)}, bf16[64,1024]{1,0:T(8,128)(2,1)S(1)}, u32[]{:S(2)}, u32[]{:S(2)}) collective-permute-start(bf16[64,1024]{1,0:T(8,128)(2,1)S(1)} %get-tuple-element.70), channel_id=1, source_target_pairs={{0,16},{16,0},{1,17},{17,1},{2,18},{18,2},{3,19},{19,3},{4,20},{20... | collective-permute-start | bytes 393224 | tf_op jit(solution)/shard_map/ppermute | solution.py:51
  25.8 4.7 %collective-permute-start.10 = (bf16[64,1024]{1,0:T(8,128)(2,1)S(1)}, bf16[64,1024]{1,0:T(8,128)(2,1)S(1)}, u32[]{:S(2)}, u32[]{:S(2)}) collective-permute-start(bf16[64,1024]{1,0:T(8,128)(2,1)S(1)} %get-tuple-element.71), channel_id=1, source_target_pairs={{0,16},{16,0},{1,17},{17,1},{2,18},{18,2},{3,19},{19,3},{4,20},{20... | collective-permute-start | bytes 393224 | tf_op jit(solution)/shard_map/ppermute | solution.py:51
  26.3 4.2 %collective-permute-start.7 = (bf16[64,1024]{1,0:T(8,128)(2,1)S(1)}, bf16[64,1024]{1,0:T(8,128)(2,1)S(1)}, u32[]{:S(2)}, u32[]{:S(2)}) collective-permute-start(bf16[64,1024]{1,0:T(8,128)(2,1)S(1)} %get-tuple-element.68.refs_9_), channel_id=1, source_target_pairs={{0,16},{16,0},{1,17},{17,1},{2,18},{18,2},{3,19},{19,3},{4,20},{20... | collective-permute-start | bytes 393224 | tf_op jit(solution)/shard_map/ppermute | solution.py:51
  29.1 12.8 %collective-permute-start.16 = (bf16[3,64,1024]{2,1,0:T(8,128)(2,1)S(1)}, bf16[3,64,1024]{2,1,0:T(8,128)(2,1)S(1)}, u32[]{:S(2)}, u32[]{:S(2)}) collective-permute-start(bf16[3,64,1024]{2,1,0:T(8,128)(2,1)S(1)} %get-tuple-element.77.refs_0_), channel_id=1, source_target_pairs={{0,1},{3,2},{4,5},{7,6},{8,9},{11,10},{12,13},{15,14},{16,17},{19,... | collective-permute-start | bytes 1179656 | tf_op jit(solution)/shard_map/ppermute | solution.py:385
  33.3 8.6 %collective-permute-start.15 = (bf16[3,64,1024]{2,1,0:T(8,128)(2,1)S(1)}, bf16[3,64,1024]{2,1,0:T(8,128)(2,1)S(1)}, u32[]{:S(2)}, u32[]{:S(2)}) collective-permute-start(bf16[3,64,1024]{2,1,0:T(8,128)(2,1)S(1)} %add_on.8.refs_1_), channel_id=1, source_target_pairs={{1,2},{2,1},{5,6},{6,5},{9,10},{10,9},{13,14},{14,13},{17,18},{18,... | collective-permute-start | bytes 1179656 | tf_op jit(solution)/shard_map/ppermute | solution.py:385
  34.0 23.4 %collective-permute-start.20 = (bf16[3,64,1024]{2,1,0:T(8,128)(2,1)S(1)}, bf16[3,64,1024]{2,1,0:T(8,128)(2,1)S(1)}, u32[]{:S(2)}, u32[]{:S(2)}) collective-permute-start(bf16[3,64,1024]{2,1,0:T(8,128)(2,1)S(1)} %get-tuple-element.79.refs_0_), channel_id=1, source_target_pairs={{0,1},{3,2},{4,5},{7,6},{8,9},{11,10},{12,13},{15,14},{16,17},{19,... | collective-permute-start | bytes 1179656 | tf_op jit(solution)/shard_map/ppermute | solution.py:385
  41.3 1.4 collective-permute-start.22
  41.4 2.1 %collective-permute-start.23 = (bf16[64,1024]{1,0:T(8,128)(2,1)S(1)}, bf16[64,1024]{1,0:T(8,128)(2,1)S(1)}, u32[]{:S(2)}, u32[]{:S(2)}) collective-permute-start(bf16[64,1024]{1,0:T(8,128)(2,1)S(1)} %get-tuple-element.81), channel_id=1, source_target_pairs={{0,16},{16,0},{1,17},{17,1},{2,18},{18,2},{3,19},{19,3},{4,20},{20... | collective-permute-start | bytes 393224 | tf_op jit(solution)/shard_map/ppermute | solution.py:51
  41.9 2.9 %collective-permute-start.24 = (bf16[64,1024]{1,0:T(8,128)(2,1)S(1)}, bf16[64,1024]{1,0:T(8,128)(2,1)S(1)}, u32[]{:S(2)}, u32[]{:S(2)}) collective-permute-start(bf16[64,1024]{1,0:T(8,128)(2,1)S(1)} %get-tuple-element.82), channel_id=1, source_target_pairs={{0,16},{16,0},{1,17},{17,1},{2,18},{18,2},{3,19},{19,3},{4,20},{20... | collective-permute-start | bytes 393224 | tf_op jit(solution)/shard_map/ppermute | solution.py:51
  42.0 2.9 %collective-permute-start.21 = (bf16[64,1024]{1,0:T(8,128)(2,1)S(1)}, bf16[64,1024]{1,0:T(8,128)(2,1)S(1)}, u32[]{:S(2)}, u32[]{:S(2)}) collective-permute-start(bf16[64,1024]{1,0:T(8,128)(2,1)S(1)} %get-tuple-element.78.refs_2_), channel_id=1, source_target_pairs={{0,16},{16,0},{1,17},{17,1},{2,18},{18,2},{3,19},{19,3},{4,20},{20... | collective-permute-start | bytes 393224 | tf_op jit(solution)/shard_map/ppermute | solution.py:51
  42.7 15.5 %collective-permute-start.19 = (bf16[3,64,1024]{2,1,0:T(8,128)(2,1)S(1)}, bf16[3,64,1024]{2,1,0:T(8,128)(2,1)S(1)}, u32[]{:S(2)}, u32[]{:S(2)}) collective-permute-start(bf16[3,64,1024]{2,1,0:T(8,128)(2,1)S(1)} %add_on.9.refs_2_), channel_id=1, source_target_pairs={{1,2},{2,1},{5,6},{6,5},{9,10},{10,9},{13,14},{14,13},{17,18},{18,... | collective-permute-start | bytes 1179656 | tf_op jit(solution)/shard_map/ppermute | solution.py:385
  43.5 18.7 %collective-permute-start.18 = (bf16[3,64,1024]{2,1,0:T(8,128)(2,1)S(1)}, bf16[3,64,1024]{2,1,0:T(8,128)(2,1)S(1)}, u32[]{:S(2)}, u32[]{:S(2)}) collective-permute-start(bf16[3,64,1024]{2,1,0:T(8,128)(2,1)S(1)} %add_on.10.refs_9_), channel_id=1, source_target_pairs={{2,3},{1,0},{6,7},{5,4},{10,11},{9,8},{14,15},{13,12},{18,19},{17,... | collective-permute-start | bytes 1179656 | tf_op jit(solution)/shard_map/ppermute | solution.py:385
  47.5 19.4 %collective-permute-start.28 = (bf16[3,64,1024]{2,1,0:T(8,128)(2,1)S(1)}, bf16[3,64,1024]{2,1,0:T(8,128)(2,1)S(1)}, u32[]{:S(2)}, u32[]{:S(2)}) collective-permute-start(bf16[3,64,1024]{2,1,0:T(8,128)(2,1)S(1)} %get-tuple-element.84.refs_0_), channel_id=1, source_target_pairs={{0,1},{3,2},{4,5},{7,6},{8,9},{11,10},{12,13},{15,14},{16,17},{19,... | collective-permute-start | bytes 1179656 | tf_op jit(solution)/shard_map/ppermute | solution.py:385
  57.6 10.1 %collective-permute-start.27 = (bf16[3,64,1024]{2,1,0:T(8,128)(2,1)S(1)}, bf16[3,64,1024]{2,1,0:T(8,128)(2,1)S(1)}, u32[]{:S(2)}, u32[]{:S(2)}) collective-permute-start(bf16[3,64,1024]{2,1,0:T(8,128)(2,1)S(1)} %add_on.11.refs_2_), channel_id=1, source_target_pairs={{1,2},{2,1},{5,6},{6,5},{9,10},{10,9},{13,14},{14,13},{17,18},{18,... | collective-permute-start | bytes 1179656 | tf_op jit(solution)/shard_map/ppermute | solution.py:385
  58.4 13.3 %collective-permute-start.26 = (bf16[3,64,1024]{2,1,0:T(8,128)(2,1)S(1)}, bf16[3,64,1024]{2,1,0:T(8,128)(2,1)S(1)}, u32[]{:S(2)}, u32[]{:S(2)}) collective-permute-start(bf16[3,64,1024]{2,1,0:T(8,128)(2,1)S(1)} %add_on.12.refs_2_), channel_id=1, source_target_pairs={{2,3},{1,0},{6,7},{5,4},{10,11},{9,8},{14,15},{13,12},{18,19},{17,... | collective-permute-start | bytes 1179656 | tf_op jit(solution)/shard_map/ppermute | solution.py:385
  62.4 12.8 %collective-permute-start.25 = (bf16[3,64,1024]{2,1,0:T(8,128)(2,1)S(1)}, bf16[3,64,1024]{2,1,0:T(8,128)(2,1)S(1)}, u32[]{:S(2)}, u32[]{:S(2)}) collective-permute-start(bf16[3,64,1024]{2,1,0:T(8,128)(2,1)S(1)} %activations.4.refs_2_), channel_id=1, source_target_pairs={{0,1},{3,2},{4,5},{7,6},{8,9},{11,10},{12,13},{15,14},{16,17},{19,... | collective-permute-start | bytes 1179656 | tf_op jit(solution)/shard_map/ppermute | solution.py:385
  67.0 8.9 %collective-permute-start.32 = (bf16[3,64,1024]{2,1,0:T(8,128)(2,1)S(1)}, bf16[3,64,1024]{2,1,0:T(8,128)(2,1)S(1)}, u32[]{:S(2)}, u32[]{:S(2)}) collective-permute-start(bf16[3,64,1024]{2,1,0:T(8,128)(2,1)S(1)} %add_on.13.refs_2_), channel_id=1, source_target_pairs={{1,2},{2,1},{5,6},{6,5},{9,10},{10,9},{13,14},{14,13},{17,18},{18,... | collective-permute-start | bytes 1179656 | tf_op jit(solution)/shard_map/ppermute | solution.py:385
  67.8 13.1 %collective-permute-start.31 = (bf16[3,64,1024]{2,1,0:T(8,128)(2,1)S(1)}, bf16[3,64,1024]{2,1,0:T(8,128)(2,1)S(1)}, u32[]{:S(2)}, u32[]{:S(2)}) collective-permute-start(bf16[3,64,1024]{2,1,0:T(8,128)(2,1)S(1)} %add_on.14.refs_2_), channel_id=1, source_target_pairs={{2,3},{1,0},{6,7},{5,4},{10,11},{9,8},{14,15},{13,12},{18,19},{17,... | collective-permute-start | bytes 1179656 | tf_op jit(solution)/shard_map/ppermute | solution.py:385
  71.9 12.8 %collective-permute-start.30 = (bf16[3,64,1024]{2,1,0:T(8,128)(2,1)S(1)}, bf16[3,64,1024]{2,1,0:T(8,128)(2,1)S(1)}, u32[]{:S(2)}, u32[]{:S(2)}) collective-permute-start(bf16[3,64,1024]{2,1,0:T(8,128)(2,1)S(1)} %activations.5.refs_1_.refs_2_), channel_id=1, source_target_pairs={{0,1},{3,2},{4,5},{7,6},{8,9},{11,10},{12,13},{15,14},{16,17},{19,... | collective-permute-start | bytes 1179656 | tf_op jit(solution)/shard_map/ppermute | solution.py:385
  75.2 10.2 %collective-permute-start.29 = (bf16[3,64,1024]{2,1,0:T(8,128)(2,1)S(1)}, bf16[3,64,1024]{2,1,0:T(8,128)(2,1)S(1)}, u32[]{:S(2)}, u32[]{:S(2)}) collective-permute-start(bf16[3,64,1024]{2,1,0:T(8,128)(2,1)S(1)} %pass_on.22.refs_2_.refs_3_), channel_id=1, source_target_pairs={{1,2},{2,1},{5,6},{6,5},{9,10},{10,9},{13,14},{14,13},{17,18},{18,... | collective-permute-start | bytes 1179656 | tf_op jit(solution)/shard_map/ppermute | solution.py:385
  76.0 13.5 %collective-permute-start.36 = (bf16[3,64,1024]{2,1,0:T(8,128)(2,1)S(1)}, bf16[3,64,1024]{2,1,0:T(8,128)(2,1)S(1)}, u32[]{:S(2)}, u32[]{:S(2)}) collective-permute-start(bf16[3,64,1024]{2,1,0:T(8,128)(2,1)S(1)} %add_on.15.refs_2_), channel_id=1, source_target_pairs={{2,3},{1,0},{6,7},{5,4},{10,11},{9,8},{14,15},{13,12},{18,19},{17,... | collective-permute-start | bytes 1179656 | tf_op jit(solution)/shard_map/ppermute | solution.py:385
  81.1 12.7 %collective-permute-start.35 = (bf16[3,64,1024]{2,1,0:T(8,128)(2,1)S(1)}, bf16[3,64,1024]{2,1,0:T(8,128)(2,1)S(1)}, u32[]{:S(2)}, u32[]{:S(2)}) collective-permute-start(bf16[3,64,1024]{2,1,0:T(8,128)(2,1)S(1)} %activations.6.refs_1_.refs_2_), channel_id=1, source_target_pairs={{0,1},{3,2},{4,5},{7,6},{8,9},{11,10},{12,13},{15,14},{16,17},{19,... | collective-permute-start | bytes 1179656 | tf_op jit(solution)/shard_map/ppermute | solution.py:385
  84.7 9.9 %collective-permute-start.34 = (bf16[3,64,1024]{2,1,0:T(8,128)(2,1)S(1)}, bf16[3,64,1024]{2,1,0:T(8,128)(2,1)S(1)}, u32[]{:S(2)}, u32[]{:S(2)}) collective-permute-start(bf16[3,64,1024]{2,1,0:T(8,128)(2,1)S(1)} %pass_on.23.refs_1_.refs_3_), channel_id=1, source_target_pairs={{1,2},{2,1},{5,6},{6,5},{9,10},{10,9},{13,14},{14,13},{17,18},{18,... | collective-permute-start | bytes 1179656 | tf_op jit(solution)/shard_map/ppermute | solution.py:385
  85.4 12.6 %collective-permute-start.33 = (bf16[3,64,1024]{2,1,0:T(8,128)(2,1)S(1)}, bf16[3,64,1024]{2,1,0:T(8,128)(2,1)S(1)}, u32[]{:S(2)}, u32[]{:S(2)}) collective-permute-start(bf16[3,64,1024]{2,1,0:T(8,128)(2,1)S(1)} %pass_on.24.refs_2_.refs_4_), channel_id=1, source_target_pairs={{2,3},{1,0},{6,7},{5,4},{10,11},{9,8},{14,15},{13,12},{18,19},{17,... | collective-permute-start | bytes 1179656 | tf_op jit(solution)/shard_map/ppermute | solution.py:385
  89.7 10.2 %collective-permute-start.38 = (bf16[3,64,1024]{2,1,0:T(8,128)(2,1)S(1)}, bf16[3,64,1024]{2,1,0:T(8,128)(2,1)S(1)}, u32[]{:S(2)}, u32[]{:S(2)}) collective-permute-start(bf16[3,64,1024]{2,1,0:T(8,128)(2,1)S(1)} %activations.7.refs_1_.refs_2_), channel_id=1, source_target_pairs={{0,1},{3,2},{4,5},{7,6},{8,9},{11,10},{12,13},{15,14},{16,17},{19,... | collective-permute-start | bytes 1179656 | tf_op jit(solution)/shard_map/ppermute | solution.py:385
  93.8 6.7 %collective-permute-start.37 = (bf16[3,64,1024]{2,1,0:T(8,128)(2,1)S(1)}, bf16[3,64,1024]{2,1,0:T(8,128)(2,1)S(1)}, u32[]{:S(2)}, u32[]{:S(2)}) collective-permute-start(bf16[3,64,1024]{2,1,0:T(8,128)(2,1)S(1)} %pass_on.25.refs_1_.refs_3_), channel_id=1, source_target_pairs={{1,2},{2,1},{5,6},{6,5},{9,10},{10,9},{13,14},{14,13},{17,18},{18,... | collective-permute-start | bytes 1179656 | tf_op jit(solution)/shard_map/ppermute | solution.py:385
  94.5 12.7 %collective-permute-start.43 = (bf16[3,64,1024]{2,1,0:T(8,128)(2,1)S(1)}, bf16[3,64,1024]{2,1,0:T(8,128)(2,1)S(1)}, u32[]{:S(2)}, u32[]{:S(2)}) collective-permute-start(bf16[3,64,1024]{2,1,0:T(8,128)(2,1)S(1)} %pass_on.26.refs_1_.refs_4_), channel_id=1, source_target_pairs={{2,3},{1,0},{6,7},{5,4},{10,11},{9,8},{14,15},{13,12},{18,19},{17,... | collective-permute-start | bytes 1179656 | tf_op jit(solution)/shard_map/ppermute | solution.py:385
  99.9 11.8 %collective-permute-start.45 = (bf16[3,64,1024]{2,1,0:T(8,128)(2,1)S(1)}, bf16[3,64,1024]{2,1,0:T(8,128)(2,1)S(1)}, u32[]{:S(2)}, u32[]{:S(2)}) collective-permute-start(bf16[3,64,1024]{2,1,0:T(8,128)(2,1)S(1)} %pass_on.28.refs_1_.refs_3_), channel_id=1, source_target_pairs={{1,2},{2,1},{5,6},{6,5},{9,10},{10,9},{13,14},{14,13},{17,18},{18,... | collective-permute-start | bytes 1179656 | tf_op jit(solution)/shard_map/ppermute | solution.py:385
  100.6 14.8 %collective-permute-start.44 = (bf16[3,64,1024]{2,1,0:T(8,128)(2,1)S(1)}, bf16[3,64,1024]{2,1,0:T(8,128)(2,1)S(1)}, u32[]{:S(2)}, u32[]{:S(2)}) collective-permute-start(bf16[3,64,1024]{2,1,0:T(8,128)(2,1)S(1)} %pass_on.29.refs_9_.refs_4_), channel_id=1, source_target_pairs={{2,3},{1,0},{6,7},{5,4},{10,11},{9,8},{14,15},{13,12},{18,19},{17,... | collective-permute-start | bytes 1179656 | tf_op jit(solution)/shard_map/ppermute | solution.py:385
  111.0 4.4 %collective-permute-start.46 = (bf16[64,1024]{1,0:T(8,128)(2,1)S(1)}, bf16[64,1024]{1,0:T(8,128)(2,1)S(1)}, u32[]{:S(2)}, u32[]{:S(2)}) collective-permute-start(bf16[64,1024]{1,0:T(8,128)(2,1)S(1)} %get-tuple-element.93), channel_id=1, source_target_pairs={{0,16},{16,0},{1,17},{17,1},{2,18},{18,2},{3,19},{19,3},{4,20},{20... | collective-permute-start | bytes 393224 | tf_op jit(solution)/shard_map/ppermute | solution.py:51
  111.1 4.3 %collective-permute-start.47 = (bf16[64,1024]{1,0:T(8,128)(2,1)S(1)}, bf16[64,1024]{1,0:T(8,128)(2,1)S(1)}, u32[]{:S(2)}, u32[]{:S(2)}) collective-permute-start(bf16[64,1024]{1,0:T(8,128)(2,1)S(1)} %get-tuple-element.94), channel_id=1, source_target_pairs={{0,16},{16,0},{1,17},{17,1},{2,18},{18,2},{3,19},{19,3},{4,20},{20... | collective-permute-start | bytes 393224 | tf_op jit(solution)/shard_map/ppermute | solution.py:51
  111.6 3.8 %collective-permute-start.48 = (bf16[64,1024]{1,0:T(8,128)(2,1)S(1)}, bf16[64,1024]{1,0:T(8,128)(2,1)S(1)}, u32[]{:S(2)}, u32[]{:S(2)}) collective-permute-start(bf16[64,1024]{1,0:T(8,128)(2,1)S(1)} %get-tuple-element.95), channel_id=1, source_target_pairs={{0,16},{16,0},{1,17},{17,1},{2,18},{18,2},{3,19},{19,3},{4,20},{20... | collective-permute-start | bytes 393224 | tf_op jit(solution)/shard_map/ppermute | solution.py:51
  111.6 3.7 %collective-permute-start.49 = (bf16[64,1024]{1,0:T(8,128)(2,1)S(1)}, bf16[64,1024]{1,0:T(8,128)(2,1)S(1)}, u32[]{:S(2)}, u32[]{:S(2)}) collective-permute-start(bf16[64,1024]{1,0:T(8,128)(2,1)S(1)} %get-tuple-element.96), channel_id=1, source_target_pairs={{0,16},{16,0},{1,17},{17,1},{2,18},{18,2},{3,19},{19,3},{4,20},{20... | collective-permute-start | bytes 393224 | tf_op jit(solution)/shard_map/ppermute | solution.py:51
  119.1 2.5 %collective-permute-start.51 = (bf16[64,1024]{1,0:T(8,128)(2,1)S(1)}, bf16[64,1024]{1,0:T(8,128)(2,1)S(1)}, u32[]{:S(2)}, u32[]{:S(2)}) collective-permute-start(bf16[64,1024]{1,0:T(8,128)(2,1)S(1)} %get-tuple-element.99), channel_id=1, source_target_pairs={{0,16},{16,0},{1,17},{17,1},{2,18},{18,2},{3,19},{19,3},{4,20},{20... | collective-permute-start | bytes 393224 | tf_op jit(solution)/shard_map/ppermute | solution.py:51
  119.1 14.7 %collective-permute-start.50 = (bf16[3,64,1024]{2,1,0:T(8,128)(2,1)S(1)}, bf16[3,64,1024]{2,1,0:T(8,128)(2,1)S(1)}, u32[]{:S(2)}, u32[]{:S(2)}) collective-permute-start(bf16[3,64,1024]{2,1,0:T(8,128)(2,1)S(1)} %pass_on.31.refs_1_.refs_4_), channel_id=1, source_target_pairs={{2,3},{1,0},{6,7},{5,4},{10,11},{9,8},{14,15},{13,12},{18,19},{17,... | collective-permute-start | bytes 1179656 | tf_op jit(solution)/shard_map/ppermute | solution.py:385
  120.4 18.5 %collective-permute-start.60 = (bf16[2,128,1024]{2,1,0:T(8,128)(2,1)S(1)}, bf16[2,128,1024]{2,1,0:T(8,128)(2,1)S(1)}, u32[]{:S(2)}, u32[]{:S(2)}) collective-permute-start(bf16[2,128,1024]{2,1,0:T(8,128)(2,1)S(1)} %add_quarters.4.refs_9_), channel_id=1, source_target_pairs={{0,4},{4,0},{8,12},{12,8},{1,5},{5,1},{9,13},{13,9},{2,6},{6,2},{1... | collective-permute-start | bytes 1572872 | tf_op jit(solution)/shard_map/ppermute | solution.py:51
  121.0 1.3 collective-permute-start.52
  121.2 1.3 collective-permute-start.53
  121.5 1.3 collective-permute-start.54
  123.0 20.8 %collective-permute-start.55 = (bf16[2,128,1024]{2,1,0:T(8,128)(2,1)S(1)}, bf16[2,128,1024]{2,1,0:T(8,128)(2,1)S(1)}, u32[]{:S(2)}, u32[]{:S(2)}) collective-permute-start(bf16[2,128,1024]{2,1,0:T(8,128)(2,1)S(1)} %add_quarters.5.refs_1_), channel_id=1, source_target_pairs={{0,8},{4,12},{8,0},{12,4},{1,9},{5,13},{9,1},{13,5},{2,10},{6,14},... | collective-permute-start | bytes 1572872 | tf_op jit(solution)/shard_map/ppermute | solution.py:51
  137.4 1.4 collective-permute-start.56
  137.5 1.9 %collective-permute-start.57 = (bf16[64,1024]{1,0:T(8,128)(2,1)S(1)}, bf16[64,1024]{1,0:T(8,128)(2,1)S(1)}, u32[]{:S(2)}, u32[]{:S(2)}) collective-permute-start(bf16[64,1024]{1,0:T(8,128)(2,1)S(1)} %get-tuple-element.106), channel_id=1, source_target_pairs={{0,16},{16,0},{1,17},{17,1},{2,18},{18,2},{3,19},{19,3},{4,20},{20... | collective-permute-start | bytes 393224 | tf_op jit(solution)/shard_map/ppermute | solution.py:51
  138.0 1.4 collective-permute-start.58
  138.8 1.3 collective-permute-start.59
  139.0 4.3 %collective-permute-start.39 = (bf16[64,1024]{1,0:T(8,128)(2,1)S(1)}, bf16[64,1024]{1,0:T(8,128)(2,1)S(1)}, u32[]{:S(2)}, u32[]{:S(2)}) collective-permute-start(bf16[64,1024]{1,0:T(8,128)(2,1)S(1)} %get-tuple-element.86), channel_id=1, source_target_pairs={{0,16},{16,0},{1,17},{17,1},{2,18},{18,2},{3,19},{19,3},{4,20},{20... | collective-permute-start | bytes 393224 | tf_op jit(solution)/shard_map/ppermute | solution.py:51
  140.3 13.7 %collective-permute-start.61 = (bf16[1,128,1024]{2,1,0:T(8,128)(2,1)S(1)}, bf16[1,128,1024]{2,1,0:T(8,128)(2,1)S(1)}, u32[]{:S(2)}, u32[]{:S(2)}) collective-permute-start(bf16[1,128,1024]{2,1,0:T(8,128)(2,1)S(1)} %get-tuple-element.109.refs_1_), channel_id=1, source_target_pairs={{0,12},{4,8},{8,4},{12,0},{1,13},{5,9},{9,5},{13,1},{2,14},{6,10},... | collective-permute-start | bytes 786440 | tf_op jit(solution)/shard_map/ppermute | solution.py:51
  141.2 14.1 %collective-permute-start.62 = (bf16[1,128,1024]{2,1,0:T(8,128)(2,1)S(1)}, bf16[1,128,1024]{2,1,0:T(8,128)(2,1)S(1)}, u32[]{:S(2)}, u32[]{:S(2)}) collective-permute-start(bf16[1,128,1024]{2,1,0:T(8,128)(2,1)S(1)} %get-tuple-element.111), channel_id=1, source_target_pairs={{0,12},{4,8},{8,4},{12,0},{1,13},{5,9},{9,5},{13,1},{2,14},{6,10},... | collective-permute-start | bytes 786440 | tf_op jit(solution)/shard_map/ppermute | solution.py:51
  143.3 10.6 %collective-permute-start.40 = (bf16[64,1024]{1,0:T(8,128)(2,1)S(1)}, bf16[64,1024]{1,0:T(8,128)(2,1)S(1)}, u32[]{:S(2)}, u32[]{:S(2)}) collective-permute-start(bf16[64,1024]{1,0:T(8,128)(2,1)S(1)} %get-tuple-element.87), channel_id=1, source_target_pairs={{0,16},{16,0},{1,17},{17,1},{2,18},{18,2},{3,19},{19,3},{4,20},{20... | collective-permute-start | bytes 393224 | tf_op jit(solution)/shard_map/ppermute | solution.py:51
  143.3 10.6 %collective-permute-start.41 = (bf16[64,1024]{1,0:T(8,128)(2,1)S(1)}, bf16[64,1024]{1,0:T(8,128)(2,1)S(1)}, u32[]{:S(2)}, u32[]{:S(2)}) collective-permute-start(bf16[64,1024]{1,0:T(8,128)(2,1)S(1)} %get-tuple-element.88), channel_id=1, source_target_pairs={{0,16},{16,0},{1,17},{17,1},{2,18},{18,2},{3,19},{19,3},{4,20},{20... | collective-permute-start | bytes 393224 | tf_op jit(solution)/shard_map/ppermute | solution.py:51
  143.8 10.1 %collective-permute-start.42 = (bf16[64,1024]{1,0:T(8,128)(2,1)S(1)}, bf16[64,1024]{1,0:T(8,128)(2,1)S(1)}, u32[]{:S(2)}, u32[]{:S(2)}) collective-permute-start(bf16[64,1024]{1,0:T(8,128)(2,1)S(1)} %get-tuple-element.89), channel_id=1, source_target_pairs={{0,16},{16,0},{1,17},{17,1},{2,18},{18,2},{3,19},{19,3},{4,20},{20... | collective-permute-start | bytes 393224 | tf_op jit(solution)/shard_map/ppermute | solution.py:51
  (7 other events, 26.9 us)
